TPU v7x, 32 devices: a whole 2x2x4 slice. The times are simulated.
32 devices in a mesh: section: 4 (over y, x), dp: 8 (over z, core).
Axes of the slice: x: 2, y: 2, z: 4, core: 2. Of those that a mesh axis runs over, the one named last changes fastest.
Arguments:
- patches: bfloat16 [2, 2048, 192], P(None, 'dp'), may hold values from -6 to 6
- lead_times: float32 [2, 8], P(None, 'dp'), may hold values from 0.1 to 1
- short_lengths: int32 [8, 4], P('dp'), may hold values from 1 to 64, 224 in all within a row
- cotangent: bfloat16 [2, 2048, 1024], P(None, 'dp'), may hold values from -6 to 6
- bank: bfloat16 [4, 4096, 1024], P('section', 'dp'), may hold values from -0.25 to 0.25
- patch_w: bfloat16 [48, 4, 1024], replicated, may hold values from -3 to 3
- patch_b: bfloat16 [48, 1024], replicated, may hold values from -3 to 3
- var_emb: bfloat16 [48, 1024], replicated, may hold values from -3 to 3
- agg_query: bfloat16 [1024], replicated, may hold values from -6 to 6
- agg_bias: bfloat16 [3, 1024], replicated, may hold values from -2 to 2
- lead_embed: bfloat16 [2, 1024], replicated, may hold values from -3 to 3
- norm_gain: bfloat16 [2, 1024], replicated, may hold values from 0.5 to 1.5
- norm_bias: bfloat16 [2, 1024], replicated, may hold values from -1.5 to 1.5
- attn_bias: bfloat16 [3, 1024], replicated, may hold values from -2 to 2
- fc1_bias: bfloat16 [4096], replicated, may hold values from -2 to 2
- fc2_bias: bfloat16 [1024], replicated, may hold values from -2 to 2
Outputs:
- output: bfloat16 [2, 2048, 1024], P(None, 'dp', 'section')
- grad_patches: float32 [2, 2048, 192], P(None, 'dp', 'section')
- grad_bank: float32 [4, 4096, 1024], P('section', 'dp')
- grad_patch_w: float32 [48, 4, 1024], replicated
- grad_patch_b: float32 [48, 1024], replicated
- grad_var_emb: float32 [48, 1024], replicated
- grad_agg_query: float32 [1024], replicated
- grad_agg_bias: float32 [3, 1024], replicated
- grad_lead_embed: float32 [2, 1024], replicated
- grad_norm_gain: float32 [2, 1024], replicated
- grad_norm_bias: float32 [2, 1024], replicated
- grad_attn_bias: float32 [3, 1024], replicated
- grad_fc1_bias: float32 [4096], replicated
- grad_fc2_bias: float32 [1024], replicated
Inputs may be any that keep to these rules, and one draw needn't show every extreme that they name: `short_lengths`: the 4 lengths of one index of dp sum to 224; the largest is 64 in every row.
All inputs are finite; a program needn't handle non-finite values.
Results may differ from a plain program's by a relative error of at most 0.03.
Values may be sent and summed in bfloat16 or wider, within the bound.
A program may use at most 448 MiB of HBM per device.

v0:
```python
import math

import jax
import jax.numpy as jnp
from jax import lax
from jax.sharding import PartitionSpec as P

D = 1024
HEADS = 16
HEAD = 64
FF = 4096
VARS = 48
PIX = 4


wide_type = jnp.float32
narrow_type = jnp.bfloat16
highest = lax.Precision.HIGHEST


def shortened(array):

    def short(part):
        return part.astype(jnp.bfloat16) if part.dtype == jnp.float32 else part

    return jax.tree.map(short, array)


def from_behind(array, axis, by):
    length = lax.axis_size(axis)
    pairs = [(i, i + by) for i in range(length) if 0 <= i + by < length]
    return lax.ppermute(array, axis, pairs)


def product(factor_left, factor_right):
    return jnp.dot(factor_left, factor_right, preferred_element_type=wide_type)


def product_left(factor_left, factor_right):
    return lax.dot_general(
        factor_left, factor_right, (((0,), (0,)), ((), ())), preferred_element_type=wide_type
    )


def product_right(factor_left, factor_right):
    return lax.dot_general(
        factor_left, factor_right, (((1,), (1,)), ((), ())), preferred_element_type=wide_type
    )


def norm_layer(stream, gain_row, shift_row):
    centre = stream - jnp.mean(stream, axis=-1, keepdims=True)
    spread = jnp.mean(centre * centre, axis=-1, keepdims=True)
    return centre * lax.rsqrt(spread + 1e-05) * gain_row + shift_row


def gelu_exact(values_in):
    return jax.nn.gelu(values_in, approximate=False)


def position_table(places):
    half_width = D // 2
    frequency = jnp.exp(-math.log(10000.0) * 2.0 * jnp.arange(half_width, dtype=wide_type) / D)
    angles = places.astype(wide_type)[:, None] * frequency[None, :]
    return jnp.concatenate([jnp.sin(angles), jnp.cos(angles)], axis=1)


def layout(lengths_row, row_count):
    segment_ends = jnp.cumsum(lengths_row)
    starts = segment_ends - lengths_row
    places = jnp.arange(row_count, dtype=jnp.int32)
    segment = jnp.sum((places[:, None] >= segment_ends[None, :]).astype(jnp.int32), axis=1)
    member = segment[:, None] == jnp.arange(lengths_row.shape[0], dtype=jnp.int32)[None, :]
    offset = jnp.sum(jnp.where(member, starts[None, :], 0), axis=1)
    offset = jnp.where(segment == lengths_row.shape[0], segment_ends[-1], offset)
    return (segment, places - offset)


def embed_setup(weights, params):
    patch_w, patch_b, var_emb, agg_query, agg_bias = params[:5]
    query_row = product(agg_query[None, :], weights[0])[0] + agg_bias[0].astype(wide_type)
    query_low = query_row.astype(narrow_type)
    key_query = jnp.einsum(
        "dhe,he->dh",
        weights[1].reshape(D, HEADS, HEAD),
        query_low.reshape(HEADS, HEAD),
        preferred_element_type=wide_type,
    )
    key_low = key_query.astype(narrow_type)
    constant = (patch_b.astype(wide_type) + var_emb.astype(wide_type)).astype(narrow_type)
    filters = jnp.einsum("vpd,dh->vph", patch_w, key_low, preferred_element_type=wide_type)
    offsets = product(constant, key_low)
    embed_table = jnp.concatenate([patch_w.reshape(VARS * PIX, D), constant], axis=0)
    return (query_low, key_low, constant, filters, offsets, embed_table)


def embed_rows(pixel_rows, places, lead_time, setup, weights, params):
    query_low, key_low, constant, filters, offsets, embed_table = setup
    agg_bias, lead_embed = (params[4], params[5])
    row_count = pixel_rows.shape[0]
    pixels = pixel_rows.reshape(row_count, VARS, PIX).astype(wide_type)
    scores = (
        jnp.einsum("tvp,vph->tvh", pixels, filters, precision=highest) + offsets[None]
    ) / math.sqrt(HEAD)
    attend = jax.nn.softmax(scores, axis=1)
    attend_low = attend.astype(narrow_type)
    weighted = (attend_low.astype(wide_type)[:, :, :, None] * pixels[:, :, None, :]).astype(
        narrow_type
    )
    operand = jnp.concatenate(
        [
            jnp.transpose(weighted, (0, 2, 1, 3)).reshape(row_count * HEADS, VARS * PIX),
            jnp.transpose(attend_low, (0, 2, 1)).reshape(row_count * HEADS, VARS),
        ],
        axis=1,
    )
    pooled = product(operand, embed_table).astype(narrow_type).reshape(row_count, HEADS, D)
    heads_out = jnp.einsum(
        "thd,dhe->the", pooled, weights[2].reshape(D, HEADS, HEAD), preferred_element_type=wide_type
    ).reshape(row_count, D)
    heads_low = (heads_out + agg_bias[1].astype(wide_type)).astype(narrow_type)
    merged = product(heads_low, weights[3]) + agg_bias[2].astype(wide_type)
    stream = (
        merged
        + position_table(places)
        + lead_time * lead_embed[0].astype(wide_type)
        + lead_embed[1].astype(wide_type)
    )
    return (stream.astype(narrow_type), (pixels, attend, attend_low, operand, pooled, heads_low))


def embed_back(grad_rows, lead_time, setup, saved_state, weights):
    query_low, key_low, constant, filters, offsets, embed_table = setup
    pixels, attend, attend_low, operand, pooled, heads_low = saved_state
    row_count = grad_rows.shape[0]
    grad_wide = grad_rows.astype(wide_type)
    grad_w_out = product_left(heads_low, grad_rows)
    grad_bias_out = jnp.sum(grad_wide, axis=0)
    grad_heads = product_right(grad_rows, weights[3]).astype(narrow_type)
    grad_bias_value = jnp.sum(grad_heads.astype(wide_type), axis=0)
    grad_heads_split = grad_heads.reshape(row_count, HEADS, HEAD)
    grad_w_value = jnp.einsum(
        "thd,the->dhe", pooled, grad_heads_split, preferred_element_type=wide_type
    ).reshape(D, D)
    grad_pooled = jnp.einsum(
        "the,dhe->thd",
        grad_heads_split,
        weights[2].reshape(D, HEADS, HEAD),
        preferred_element_type=wide_type,
    )
    grad_pooled = grad_pooled.astype(narrow_type).reshape(row_count * HEADS, D)
    grad_operand = product_right(grad_pooled, embed_table)
    grad_table = product_left(operand, grad_pooled)
    grad_weighted = grad_operand[:, : VARS * PIX].reshape(row_count, HEADS, VARS, PIX)
    grad_mixing = jnp.transpose(
        grad_operand[:, VARS * PIX :].reshape(row_count, HEADS, VARS), (0, 2, 1)
    )
    grad_attend = (
        jnp.einsum("thvp,tvp->tvh", grad_weighted, pixels, precision=highest) + grad_mixing
    )
    grad_scores = (
        attend
        * (grad_attend - jnp.sum(attend * grad_attend, axis=1, keepdims=True))
        / math.sqrt(HEAD)
    )
    grad_pixels = jnp.einsum(
        "thvp,tvh->tvp", grad_weighted, attend_low.astype(wide_type), precision=highest
    )
    grad_pixels = grad_pixels + jnp.einsum("tvh,vph->tvp", grad_scores, filters, precision=highest)
    grad_filters = jnp.einsum("tvp,tvh->vph", pixels, grad_scores, precision=highest)
    grad_offsets = jnp.sum(grad_scores, axis=0)
    grad_lead = jnp.stack([lead_time * grad_bias_out, grad_bias_out])
    sums = (
        grad_w_out,
        grad_bias_out,
        grad_bias_value,
        grad_w_value,
        grad_table,
        grad_filters,
        grad_offsets,
        grad_lead,
    )
    return (grad_pixels.reshape(row_count, VARS * PIX), sums)


def embed_finish(totals, setup, weights, params):
    (
        grad_w_out,
        grad_bias_out,
        grad_bias_value,
        grad_w_value,
        grad_table,
        grad_filters,
        grad_offsets,
        grad_lead,
    ) = totals
    query_low, key_low, constant, filters, offsets, embed_table = setup
    patch_w, agg_query = (params[0], params[3])
    key_wide = key_low.astype(wide_type)
    grad_patch_w = grad_table[: VARS * PIX].reshape(VARS, PIX, D) + jnp.einsum(
        "vph,dh->vpd", grad_filters, key_wide, precision=highest
    )
    grad_constant = grad_table[VARS * PIX :] + jnp.dot(grad_offsets, key_wide.T, precision=highest)
    grad_key = jnp.einsum("vpd,vph->dh", patch_w.astype(wide_type), grad_filters, precision=highest)
    grad_key = grad_key + jnp.dot(constant.astype(wide_type).T, grad_offsets, precision=highest)
    grad_key_low = grad_key.astype(narrow_type)
    query_heads = query_low.reshape(HEADS, HEAD).astype(wide_type)
    grad_w_key = (grad_key_low.astype(wide_type)[:, :, None] * query_heads[None, :, :]).reshape(
        D, D
    )
    grad_query = jnp.einsum(
        "dhe,dh->he",
        weights[1].reshape(D, HEADS, HEAD),
        grad_key_low,
        preferred_element_type=wide_type,
    )
    grad_query = grad_query.reshape(D).astype(narrow_type)
    grad_query_wide = grad_query.astype(wide_type)
    grad_w_query = agg_query.astype(wide_type)[:, None] * grad_query_wide[None, :]
    grad_agg_query = product(weights[0], grad_query[:, None])[:, 0]
    grad_bank = jnp.concatenate([grad_w_query, grad_w_key, grad_w_value, grad_w_out], axis=0)
    smalls = (
        grad_patch_w,
        grad_constant,
        grad_constant,
        grad_agg_query,
        jnp.stack([grad_query_wide, grad_bias_value, grad_bias_out]),
        grad_lead,
        jnp.zeros((2, D), wide_type),
        jnp.zeros((2, D), wide_type),
        jnp.zeros((3, D), wide_type),
        jnp.zeros((FF,), wide_type),
        jnp.zeros((D,), wide_type),
    )
    return (grad_bank, smalls)


def attention_scores(block_query, block_segment, key_heads, segment):
    raw_scores = jnp.einsum(
        "qhe,khe->hqk", block_query, key_heads, preferred_element_type=wide_type
    ) / math.sqrt(HEAD)
    allowed = (block_segment[:, None] == segment[None, :])[None]
    return jnp.where(allowed, raw_scores, -1e30)


def attention_forward(queries, key_rows, values, segment):
    row_count = queries.shape[0]
    block_rows = min(512, row_count)
    block_total = row_count // block_rows
    key_heads = key_rows.reshape(row_count, HEADS, HEAD)
    value_heads = values.reshape(row_count, HEADS, HEAD)

    def one_block(block_items):
        block_query, block_segment = block_items
        scores = attention_scores(block_query, block_segment, key_heads, segment)
        row_peak = jnp.max(scores, axis=-1, keepdims=True)
        exp_scores = jnp.exp(scores - row_peak)
        exp_total = jnp.sum(exp_scores, axis=-1, keepdims=True)
        probabilities = (exp_scores / exp_total).astype(narrow_type)
        mixed_heads = jnp.einsum(
            "hqk,khe->qhe", probabilities, value_heads, preferred_element_type=wide_type
        )
        return (mixed_heads.astype(narrow_type), (row_peak + jnp.log(exp_total))[:, :, 0])

    mixed_heads, log_totals = lax.map(
        one_block,
        (
            queries.reshape(block_total, block_rows, HEADS, HEAD),
            segment.reshape(block_total, block_rows),
        ),
    )
    return (mixed_heads.reshape(row_count, D), log_totals)


def attention_backward(queries, key_rows, values, segment, log_totals, grad_mixed):
    row_count = queries.shape[0]
    block_rows = min(512, row_count)
    block_total = row_count // block_rows
    key_heads = key_rows.reshape(row_count, HEADS, HEAD)
    value_heads = values.reshape(row_count, HEADS, HEAD)

    def one_block(carry_sums, block_items):
        grad_key_sum, grad_value_sum = carry_sums
        block_query, block_segment, block_log, block_grad = block_items
        scores = attention_scores(block_query, block_segment, key_heads, segment)
        probabilities = jnp.exp(scores - block_log[:, :, None])
        probs_low = probabilities.astype(narrow_type)
        grad_value_sum = grad_value_sum + jnp.einsum(
            "hqk,qhe->khe", probs_low, block_grad, preferred_element_type=wide_type
        )
        grad_probs = jnp.einsum(
            "qhe,khe->hqk", block_grad, value_heads, preferred_element_type=wide_type
        )
        grad_scores = probabilities * (
            grad_probs - jnp.sum(probabilities * grad_probs, axis=-1, keepdims=True)
        )
        grad_low = grad_scores.astype(narrow_type)
        grad_query = jnp.einsum(
            "hqk,khe->qhe", grad_low, key_heads, preferred_element_type=wide_type
        ) / math.sqrt(HEAD)
        grad_key_sum = grad_key_sum + jnp.einsum(
            "hqk,qhe->khe", grad_low, block_query, preferred_element_type=wide_type
        ) / math.sqrt(HEAD)
        return ((grad_key_sum, grad_value_sum), grad_query)

    zero_heads = jnp.zeros((row_count, HEADS, HEAD), wide_type)
    block_items = (
        queries.reshape(block_total, block_rows, HEADS, HEAD),
        segment.reshape(block_total, block_rows),
        log_totals,
        grad_mixed.reshape(block_total, block_rows, HEADS, HEAD),
    )
    (grad_key_sum, grad_value_sum), grad_queries = lax.scan(
        one_block, (zero_heads, zero_heads), block_items
    )
    return (
        grad_queries.reshape(row_count, D),
        grad_key_sum.reshape(row_count, D),
        grad_value_sum.reshape(row_count, D),
    )


def project_heads(normed_low, weights, attn_bias):
    queries = (product(normed_low, weights[0]) + attn_bias[0].astype(wide_type)).astype(narrow_type)
    key_rows = product(normed_low, weights[1]).astype(narrow_type)
    values = (product(normed_low, weights[2]) + attn_bias[1].astype(wide_type)).astype(narrow_type)
    return (queries, key_rows, values)


def feed_half(normed_low, weights, bias_in):
    inner_first = product(normed_low, weights[0]) + bias_in[:D].astype(wide_type)
    inner_second = product(normed_low, weights[1]) + bias_in[D:].astype(wide_type)
    active_first = gelu_exact(inner_first).astype(narrow_type)
    active_second = gelu_exact(inner_second).astype(narrow_type)
    partial_sum = product(active_first, weights[2]) + product(active_second, weights[3])
    return ((inner_first, inner_second), (active_first, active_second), partial_sum)


def feed_half_back(normed_low, weights, inners, actives, grad_rows):
    grad_inners = []
    for number in range(2):
        grad_active = product_right(grad_rows, weights[2 + number])
        value_out, gelu_pull = jax.vjp(gelu_exact, inners[number])
        grad_inners.append(gelu_pull(grad_active)[0].astype(narrow_type))
    grad_normed = product_right(grad_inners[0], weights[0]) + product_right(
        grad_inners[1], weights[1]
    )
    grad_bank = jnp.concatenate(
        [
            product_left(normed_low, grad_inners[0]),
            product_left(normed_low, grad_inners[1]),
            product_left(actives[0], grad_rows),
            product_left(actives[1], grad_rows),
        ],
        axis=0,
    )
    grad_bias_in = jnp.concatenate(
        [
            jnp.sum(grad_inners[0].astype(wide_type), axis=0),
            jnp.sum(grad_inners[1].astype(wide_type), axis=0),
        ]
    )
    return (grad_normed, grad_bank, grad_bias_in)


def on_device(
    patches,
    lead_times,
    short_lengths,
    cotangent,
    bank,
    patch_w,
    patch_b,
    var_emb,
    agg_query,
    agg_bias,
    lead_embed,
    norm_gain,
    norm_bias,
    attn_bias,
    fc1_bias,
    fc2_bias,
):
    params = (
        patch_w,
        patch_b,
        var_emb,
        agg_query,
        agg_bias,
        lead_embed,
        norm_gain,
        norm_bias,
        attn_bias,
        fc1_bias,
        fc2_bias,
    )
    micro_total = patches.shape[0]
    row_count = patches.shape[1]
    section_total = lax.axis_size("section")
    section_index = lax.axis_index("section")
    gathered = lax.all_gather(bank, "dp", axis=1, tiled=True)[0]
    weights = tuple((gathered[number * D : (number + 1) * D] for number in range(4)))
    short_segment, short_places = layout(short_lengths[0], row_count)
    segments = jnp.stack([short_segment, jnp.zeros((row_count,), jnp.int32)])
    places_all = jnp.stack([short_places, jnp.arange(row_count, dtype=jnp.int32)])
    valid_rows = jnp.stack([short_segment < short_lengths.shape[1], jnp.ones((row_count,), bool)])
    grad_out_all = jnp.where(valid_rows[:, :, None], cotangent, jnp.zeros_like(cotangent))
    block_rows = min(512, row_count)
    block_total = row_count // block_rows
    zeros_stream = jnp.zeros((row_count, D), narrow_type)
    zeros_final = jnp.zeros((row_count, D), wide_type)
    zeros_pixels = jnp.zeros((row_count, VARS * PIX), wide_type)
    stash_zero = (
        zeros_stream,
        zeros_stream,
        zeros_stream,
        zeros_stream,
        jnp.zeros((block_total, HEADS, block_rows), wide_type),
    )
    small_zero = tuple((jnp.zeros(array_item.shape, wide_type) for array_item in params))

    def forward_embed(operands):
        first_in, second_in, pixel_rows, places, lead_time, segment = operands
        setup = embed_setup(weights, params)

        def one_block(block_items):
            return embed_rows(block_items[0], block_items[1], lead_time, setup, weights, params)[0]

        streams = lax.map(
            one_block,
            (
                pixel_rows.reshape(block_total, block_rows, VARS * PIX),
                places.reshape(block_total, block_rows),
            ),
        )
        return (streams.reshape(row_count, D), zeros_stream, zeros_final, stash_zero)

    def forward_attend(operands):
        first_in, second_in, pixel_rows, places, lead_time, segment = operands
        stream = first_in.astype(wide_type)
        normed_low = norm_layer(
            stream, norm_gain[0].astype(wide_type), norm_bias[0].astype(wide_type)
        ).astype(narrow_type)
        queries, key_rows, values = project_heads(normed_low, weights, attn_bias)
        mixed_heads, log_totals = attention_forward(queries, key_rows, values, segment)
        new_stream = stream + product(mixed_heads, weights[3]) + attn_bias[2].astype(wide_type)
        return (new_stream.astype(narrow_type), zeros_stream, zeros_final, stash_zero)

    def forward_first(operands):
        first_in, second_in, pixel_rows, places, lead_time, segment = operands
        stream = first_in.astype(wide_type)
        normed_low = norm_layer(
            stream, norm_gain[1].astype(wide_type), norm_bias[1].astype(wide_type)
        ).astype(narrow_type)
        inners, actives, partial_sum = feed_half(normed_low, weights, fc1_bias[: 2 * D])
        return (normed_low, (stream + partial_sum).astype(narrow_type), zeros_final, stash_zero)

    def forward_second(operands):
        first_in, second_in, pixel_rows, places, lead_time, segment = operands
        inners, actives, partial_sum = feed_half(first_in, weights, fc1_bias[2 * D :])
        final_rows = second_in.astype(wide_type) + partial_sum + fc2_bias.astype(wide_type)
        return (zeros_stream, zeros_stream, final_rows, stash_zero)

    def forward_none(operands):
        return (zeros_stream, zeros_stream, zeros_final, stash_zero)

    def backward_embed(operands):
        (
            first_kept,
            second_kept,
            grad_in,
            pixel_rows,
            places,
            lead_time,
            segment,
            grad_rows,
            stash_items,
        ) = operands
        setup = embed_setup(weights, params)

        def one_block(totals, block_items):
            block_pixels, block_places, block_grad = block_items
            block_stream, saved_state = embed_rows(
                block_pixels, block_places, lead_time, setup, weights, params
            )
            block_dx, sums = embed_back(block_grad, lead_time, setup, saved_state, weights)
            return (
                tuple((total_item + sum_item for total_item, sum_item in zip(totals, sums))),
                block_dx,
            )

        zero_totals = (
            jnp.zeros((D, D), wide_type),
            jnp.zeros((D,), wide_type),
            jnp.zeros((D,), wide_type),
            jnp.zeros((D, D), wide_type),
            jnp.zeros((VARS * PIX + VARS, D), wide_type),
            jnp.zeros((VARS, PIX, HEADS), wide_type),
            jnp.zeros((VARS, HEADS), wide_type),
            jnp.zeros((2, D), wide_type),
        )
        block_items = (
            pixel_rows.reshape(block_total, block_rows, VARS * PIX),
            places.reshape(block_total, block_rows),
            grad_in.reshape(block_total, block_rows, D),
        )
        totals, grad_pixels = lax.scan(one_block, zero_totals, block_items)
        grad_bank, smalls = embed_finish(totals, setup, weights, params)
        return (zeros_stream, grad_bank, smalls, grad_pixels.reshape(row_count, VARS * PIX))

    def backward_attend(operands):
        (
            first_kept,
            second_kept,
            grad_in,
            pixel_rows,
            places,
            lead_time,
            segment,
            grad_rows,
            stash_items,
        ) = operands
        stream = first_kept.astype(wide_type)
        normed, norm_pull = jax.vjp(
            norm_layer, stream, norm_gain[0].astype(wide_type), norm_bias[0].astype(wide_type)
        )
        normed_low = normed.astype(narrow_type)
        queries, key_rows, values = project_heads(normed_low, weights, attn_bias)
        mixed_heads, log_totals = attention_forward(queries, key_rows, values, segment)
        grad_in_wide = grad_in.astype(wide_type)
        grad_w_out = product_left(mixed_heads, grad_in)
        grad_mixed = product_right(grad_in, weights[3]).astype(narrow_type)
        grad_queries, grad_keys, grad_values = attention_backward(
            queries, key_rows, values, segment, log_totals, grad_mixed
        )
        grad_queries = grad_queries.astype(narrow_type)
        grad_keys = grad_keys.astype(narrow_type)
        grad_values = grad_values.astype(narrow_type)
        grad_normed = (
            product_right(grad_queries, weights[0])
            + product_right(grad_keys, weights[1])
            + product_right(grad_values, weights[2])
        )
        grad_stream, grad_gain, grad_shift = norm_pull(grad_normed)
        grad_send = (grad_in_wide + grad_stream).astype(narrow_type)
        grad_bank = jnp.concatenate(
            [
                product_left(normed_low, grad_queries),
                product_left(normed_low, grad_keys),
                product_left(normed_low, grad_values),
                grad_w_out,
            ],
            axis=0,
        )
        bias_rows = jnp.stack(
            [
                jnp.sum(grad_queries.astype(wide_type), axis=0),
                jnp.sum(grad_values.astype(wide_type), axis=0),
                jnp.sum(grad_in_wide, axis=0),
            ]
        )
        smalls = (
            small_zero[:6]
            + (
                jnp.zeros((2, D), wide_type).at[0].set(grad_gain),
                jnp.zeros((2, D), wide_type).at[0].set(grad_shift),
                bias_rows,
            )
            + small_zero[9:]
        )
        return (grad_send, grad_bank, smalls, zeros_pixels)

    def backward_first(operands):
        (
            first_kept,
            second_kept,
            grad_in,
            pixel_rows,
            places,
            lead_time,
            segment,
            grad_rows,
            stash_items,
        ) = operands
        stream = first_kept.astype(wide_type)
        normed, norm_pull = jax.vjp(
            norm_layer, stream, norm_gain[1].astype(wide_type), norm_bias[1].astype(wide_type)
        )
        normed_low = normed.astype(narrow_type)
        inners, actives, partial_sum = feed_half(normed_low, weights, fc1_bias[: 2 * D])
        grad_normed, grad_bank, grad_bias_in = feed_half_back(
            normed_low, weights, inners, actives, grad_rows
        )
        grad_stream, grad_gain, grad_shift = norm_pull(grad_normed + grad_in.astype(wide_type))
        grad_send = (grad_rows.astype(wide_type) + grad_stream).astype(narrow_type)
        smalls = small_zero[:6] + (
            jnp.zeros((2, D), wide_type).at[1].set(grad_gain),
            jnp.zeros((2, D), wide_type).at[1].set(grad_shift),
            small_zero[8],
            jnp.zeros((FF,), wide_type).at[: 2 * D].set(grad_bias_in),
            small_zero[10],
        )
        return (grad_send, grad_bank, smalls, zeros_pixels)

    def backward_second(operands):
        (
            first_kept,
            second_kept,
            grad_in,
            pixel_rows,
            places,
            lead_time,
            segment,
            grad_rows,
            stash_items,
        ) = operands
        inners, actives, partial_sum = feed_half(first_kept, weights, fc1_bias[2 * D :])
        grad_normed, grad_bank, grad_bias_in = feed_half_back(
            first_kept, weights, inners, actives, grad_rows
        )
        smalls = small_zero[:9] + (
            jnp.zeros((FF,), wide_type).at[2 * D :].set(grad_bias_in),
            jnp.sum(grad_rows.astype(wide_type), axis=0),
        )
        return (grad_normed.astype(narrow_type), grad_bank, smalls, zeros_pixels)

    def backward_none(operands):
        return (zeros_stream, jnp.zeros((4 * D, D), wide_type), small_zero, zeros_pixels)

    forward_list = [forward_embed, forward_attend, forward_first, forward_second, forward_none]
    backward_list = [
        backward_embed,
        backward_attend,
        backward_first,
        backward_second,
        backward_none,
    ]
    tick_total = micro_total + section_total - 1
    first_message, second_message = (zeros_stream, zeros_stream)
    kept_first = jnp.zeros((micro_total, row_count, D), narrow_type)
    kept_second = jnp.zeros((micro_total, row_count, D), narrow_type)
    stash_all = tuple(
        (
            jnp.zeros((micro_total,) + array_item.shape, array_item.dtype)
            for array_item in stash_zero
        )
    )
    final_all = jnp.zeros((micro_total, row_count, D), wide_type)
    for tick_number in range(tick_total):
        micro_index = tick_number - section_index
        running = jnp.logical_and(micro_index >= 0, micro_index < micro_total)
        slot_index = jnp.clip(micro_index, 0, micro_total - 1)
        kept_first = kept_first.at[slot_index].set(
            jnp.where(running, first_message, kept_first[slot_index])
        )
        kept_second = kept_second.at[slot_index].set(
            jnp.where(running, second_message, kept_second[slot_index])
        )
        branch = jnp.where(running, section_index, section_total)
        operands = (
            first_message,
            second_message,
            patches[slot_index],
            places_all[slot_index],
            lead_times[slot_index, 0],
            segments[slot_index],
        )
        first_out, second_out, final_rows, stash_items = lax.switch(branch, forward_list, operands)
        final_all = final_all.at[slot_index].add(final_rows)
        stash_all = tuple(
            (
                buffer.at[slot_index].set(jnp.where(running, array_item, buffer[slot_index]))
                for buffer, array_item in zip(stash_all, stash_items)
            )
        )
        if tick_number < tick_total - 1:
            first_message, second_message = (
                from_behind(shortened(first_out), "section", 1).astype(first_out.dtype),
                from_behind(shortened(second_out), "section", 1).astype(second_out.dtype),
            )
    grad_message = zeros_stream
    bank_total = jnp.zeros((4 * D, D), wide_type)
    small_total = small_zero
    pixel_total = jnp.zeros((micro_total, row_count, VARS * PIX), wide_type)
    for tick_number in range(tick_total):
        micro_index = tick_number - (section_total - 1 - section_index)
        running = jnp.logical_and(micro_index >= 0, micro_index < micro_total)
        slot_index = jnp.clip(micro_index, 0, micro_total - 1)
        branch = jnp.where(running, section_index, section_total)
        operands = (
            kept_first[slot_index],
            kept_second[slot_index],
            grad_message,
            patches[slot_index],
            places_all[slot_index],
            lead_times[slot_index, 0],
            segments[slot_index],
            grad_out_all[slot_index],
            tuple((buffer[slot_index] for buffer in stash_all)),
        )
        grad_send, grad_bank, smalls, grad_pixels = lax.switch(branch, backward_list, operands)
        bank_total = bank_total + grad_bank
        small_total = tuple(
            (total_item + sum_item for total_item, sum_item in zip(small_total, smalls))
        )
        pixel_total = pixel_total.at[slot_index].add(grad_pixels)
        if tick_number < tick_total - 1:
            grad_message = jax.tree.map(
                lambda part, own: part.astype(own.dtype),
                from_behind(shortened(grad_send), "section", -1),
                grad_send,
            )
    bank_share = lax.psum_scatter(
        bank_total.astype(jnp.bfloat16), "dp", scatter_dimension=0, tiled=True
    ).astype(jnp.float32)[None]
    small_sums = lax.psum(small_total, ("section", "dp"))
    output_share, pixel_share = (
        lax.psum_scatter(
            final_all.astype(jnp.bfloat16), "section", scatter_dimension=2, tiled=True
        ).astype(jnp.float32),
        lax.psum_scatter(
            pixel_total.astype(jnp.bfloat16), "section", scatter_dimension=2, tiled=True
        ).astype(jnp.float32),
    )
    output_low = output_share.astype(narrow_type)
    return (output_low, pixel_share, bank_share) + tuple(small_sums)


def solution(mesh):
    return jax.shard_map(
        on_device,
        mesh=mesh,
        in_specs=(
            P(None, "dp", None),
            P(None, "dp"),
            P("dp", None),
            P(None, "dp", None),
            P("section", "dp", None),
            P(),
            P(),
            P(),
            P(),
            P(),
            P(),
            P(),
            P(),
            P(),
            P(),
            P(),
        ),
        out_specs=(
            P(None, "dp", "section"),
            P(None, "dp", "section"),
            P("section", "dp", None),
            P(),
            P(),
            P(),
            P(),
            P(),
            P(),
            P(),
            P(),
            P(),
            P(),
            P(),
        ),
        check_vma=False,
    )
```

profile of v0, /device:TPU:25, one launch (start us, length us, event | category | flops | bytes accessed | tf_op | source)
XLA Modules:
  0.0 1703.5 jit_solution(10608962958652592328)
XLA Ops:
  12.2 78.2 %all-gather.2.cloned.1.call-done = bf16[1,4096,1024]{2,1,0:T(8,128)(2,1)} async-done(((bf16[1,512,1024]{2,1,0:T(8,128)(2,1)}), bf16[1,4096,1024]{2,1,0:T(8,128)(2,1)}) %all-gather.2.cloned.1.call-update) | async-done | bytes 8388624 | tf_op jit(solution)/shard_map/all_gather | solution.py:401
  96.2 96.1 %conditional.10 = (bf16[256,1024]{1,0:T(8,128)(2,1)}, bf16[256,1024]{1,0:T(8,128)(2,1)}, f32[256,1024]{1,0:T(8,128)}) conditional(s32[]{:T(128)} %clamp.30, (bf16[1024]{0:T(1024)(128)(2,1)S(1)}, bf16[1024,1024]{1,0:T(8,128)(2,1)S(1)}, bf16[3,1024]{1,0:T(4,128)(2,1)S(1)}, bf16[1024,1024]{1,0:T(8,128)(2,1)}, ...), branch_computations={%region_4.7_spmd.clone.clone, %region_7.10_spmd.clone, %region_10.... | conditional | flops 3124019968 | bytes 69594296 | solution.py:668
  121.5 22.8 %convert_element_type.3087 = bf16[4096,192]{0,1:T(8,128)(2,1)} reshape(bf16[256,16,48,4]{1,0,3,2:T(8,128)(2,1)} %multiply_convert_fusion.45) | data formatting | bytes 3145728 | tf_op jit(solution)/shard_map/cond/branch_0_fun/while/body/eval_jaxpr/convert_element_type | solution.py:107
  216.5 99.8 %conditional.11 = (bf16[256,1024]{1,0:T(8,128)(2,1)}, bf16[256,1024]{1,0:T(8,128)(2,1)S(1)}, f32[1,256,1024]{2,1,0:T(8,128)}) conditional(s32[]{:T(128)} %clamp.31, (bf16[1024]{0:T(1024)(128)(2,1)S(1)}, bf16[1024,1024]{1,0:T(8,128)(2,1)S(1)}, bf16[3,1024]{1,0:T(4,128)(2,1)S(1)}, bf16[1024,1024]{1,0:T(8,128)(2,1)}, ...), branch_computations={%region_14.17_spmd.clone.clone, %region_17.22_spmd, %region_22.25_... | conditional | flops 3124019968 | bytes 69819688 | solution.py:668
  245.7 22.8 %convert_element_type.3113 = bf16[4096,192]{0,1:T(8,128)(2,1)} reshape(bf16[256,16,48,4]{1,0,3,2:T(8,128)(2,1)} %multiply_convert_fusion.46) | data formatting | bytes 3145728 | tf_op jit(solution)/shard_map/cond/branch_0_fun/while/body/eval_jaxpr/convert_element_type | solution.py:107
  340.9 17.9 %conditional.12 = (bf16[256,1024]{1,0:T(8,128)(2,1)}, bf16[256,1024]{1,0:T(8,128)(2,1)}, f32[1,256,1024]{2,1,0:T(8,128)}) conditional(s32[]{:T(128)} %clamp.32, (bf16[1024]{0:T(1024)(128)(2,1)}, bf16[1024,1024]{1,0:T(8,128)(2,1)S(1)}, bf16[3,1024]{1,0:T(4,128)(2,1)S(1)}, bf16[1024,1024]{1,0:T(8,128)(2,1)}, ...), branch_computations={%region_28.31_spmd.clone.clone, %region_31.36_spmd, %region_36.39_... | conditional | flops 3124019968 | bytes 69446952 | solution.py:668
  358.8 33.8 %collective-permute-start.4 = (bf16[256,1024]{1,0:T(8,128)(2,1)}, bf16[256,1024]{1,0:T(8,128)(2,1)}, u32[]{:S(2)}, u32[]{:S(2)}) collective-permute-start(bf16[256,1024]{1,0:T(8,128)(2,1)} %get-tuple-element.3168), channel_id=1, source_target_pairs={{0,8},{8,16},{16,24},{1,9},{9,17},{17,25},{2,10},{10,18},{18,26},{... | collective-permute-start | bytes 1572872 | tf_op jit(solution)/shard_map/ppermute | solution.py:32
  447.2 37.0 %conditional.15 = (bf16[256,1024]{1,0:T(8,128)(2,1)}, f32[4096,1024]{1,0:T(8,128)}, f32[48,4,1024]{2,1,0:T(4,128)}, f32[48,1024]{1,0:T(8,128)}, f32[1024]{0:T(10...) conditional(s32[]{:T(128)} %clamp.35, ...), branch_computations={%region_63.69_spmd.clone.clone, %region_69.81_spmd, %region_81.90_... | conditional | flops 8908246016 | bytes 368269440 | solution.py:701
  489.7 26.0 %collective-permute-done.8 = bf16[256,1024]{1,0:T(8,128)(2,1)S(1)} collective-permute-done((bf16[256,1024]{1,0:T(8,128)(2,1)}, bf16[256,1024]{1,0:T(8,128)(2,1)S(1)}, u32[]{:S(2)}, u32[]{:S(2)}) %collective-permute-start.8) | collective-permute-done | bytes 524320 | tf_op jit(solution)/shard_map/ppermute | solution.py:32
  516.5 36.7 %conditional.16 = (bf16[256,1024]{1,0:T(8,128)(2,1)}, f32[4096,1024]{1,0:T(8,128)}, f32[48,4,1024]{2,1,0:T(4,128)}, f32[48,1024]{1,0:T(8,128)}, f32[1024]{0:T(10...) conditional(s32[]{:T(128)} %clamp.36, ...), branch_computations={%region_96.103_spmd.clone.clone, %region_103.116_spmd, %region_116... | conditional | flops 8908772352 | bytes 370968448 | solution.py:701
  572.5 36.2 %conditional.17 = (bf16[256,1024]{1,0:T(8,128)(2,1)}, f32[4096,1024]{1,0:T(8,128)}, f32[48,4,1024]{2,1,0:T(4,128)}, f32[48,1024]{1,0:T(8,128)}, f32[1024]{0:T(10...) conditional(s32[]{:T(128)} %clamp.37, ...), branch_computations={%region_131.138_spmd.clone.clone, %region_138.151_spmd, %region_15... | conditional | flops 8908772352 | bytes 370968448 | solution.py:701
  617.9 77.2 %collective-permute-done.10 = bf16[256,1024]{1,0:T(8,128)(2,1)S(1)} collective-permute-done((bf16[256,1024]{1,0:T(8,128)(2,1)}, bf16[256,1024]{1,0:T(8,128)(2,1)S(1)}, u32[]{:S(2)}, u32[]{:S(2)}) %collective-permute-start.10) | collective-permute-done | bytes 524320 | tf_op jit(solution)/shard_map/ppermute | solution.py:32
  695.9 291.7 %conditional.18 = (bf16[256,1024]{1,0:T(8,128)(2,1)}, f32[4096,1024]{1,0:T(8,128)}, f32[48,4,1024]{2,1,0:T(4,128)}, f32[48,1024]{1,0:T(8,128)}, f32[1024]{0:T(10...) conditional(s32[]{:T(128)} %clamp.38, ...), branch_computations={%region_166.173_spmd.clone.clone, %region_173.186_spmd, %region_18... | conditional | flops 8908772352 | bytes 370968448 | solution.py:701
  757.3 14.8 reshape.3826
  773.7 17.7 %multiply_reduce_fusion.15 = f32[256,48,16]{2,0,1:T(8,128)} fusion(f32[256,16,48,4]{1,0,3,2:T(8,128)} %reshape.3826, f32[256,48,4]{0,2,1:T(4,128)} %convert.108), kind=kLoop, calls=%fused_computation.3038 | loop fusion | flops 1376256 | bytes 4128768 | tf_op jit(solution)/shard_map/cond
  849.9 22.8 %convert_element_type.3247 = bf16[4096,192]{0,1:T(8,128)(2,1)} reshape(bf16[256,16,48,4]{1,0,3,2:T(8,128)(2,1)} %multiply_convert_fusion.52) | data formatting | bytes 3145728 | tf_op jit(solution)/shard_map/cond/branch_0_fun/while/body/eval_jaxpr/convert_element_type | solution.py:107
  998.8 264.1 %conditional.19 = (f32[4096,1024]{1,0:T(8,128)}, f32[48,4,1024]{2,1,0:T(4,128)S(1)}, f32[48,1024]{1,0:T(8,128)}, f32[1024]{0:T(1024)S(1)}, f32[3,1024]{1,0:T(4,1...) conditional(s32[]{:T(128)} %clamp.39, ...), branch_computations={%region_201.208_spmd.clone.clone, %region_208.219_spmd, %region_21... | conditional | flops 8908772352 | bytes 363206592 | solution.py:701
  1064.9 17.6 %multiply_reduce_fusion.18 = f32[256,48,16]{2,0,1:T(8,128)} fusion(f32[256,16,48,4]{1,0,3,2:T(8,128)} %reshape.3835, f32[256,48,4]{0,2,1:T(4,128)S(1)} %convert.110), kind=kLoop, calls=%fused_computation.3108 | loop fusion | flops 1376256 | bytes 4128768 | tf_op jit(solution)/shard_map/cond
  1138.3 22.7 %convert_element_type.3273 = bf16[4096,192]{0,1:T(8,128)(2,1)} reshape(bf16[256,16,48,4]{1,0,3,2:T(8,128)(2,1)} %multiply_convert_fusion.53) | data formatting | bytes 3145728 | tf_op jit(solution)/shard_map/cond/branch_0_fun/while/body/eval_jaxpr/convert_element_type | solution.py:107
  1272.3 31.0 %add_convert_fusion.48 = bf16[4096,1024]{1,0:T(8,128)(2,1)} fusion(f32[4096,1024]{1,0:T(8,128)} %get-tuple-element.3186, f32[4096,1024]{1,0:T(8,128)} %get-tuple-element.3185, f32[4096,1024]{1,0:T(8,128)} %get-tuple-element.3184, f32[4096,1024]{1,0:T(8,128)} %get-tuple-element.3182, f32[4096,1024]{1,0:T(8,128)} %get-tuple-element.3183), kind=kLoop, calls=%fused_computation.3177 | loop fusion | flops 20971520 | bytes 92274688 | tf_op jit(solution)/shard_map/convert_element_type | solution.py:714
  1328.7 99.9 %all-reduce.40.cloned.1.call-done = (f32[48,4,1024]{2,1,0:T(4,128)}, f32[48,1024]{1,0:T(8,128)}) async-done(((f32[48,4,1024]{2,1,0:T(4,128)}, f32[48,1024]{1,0:T(8,128)}), (f32[48,4,1024]{2,1,0:T(4,128)}, f32[48,1024]{1,0:T(8,128)})) %all-reduce.40.cloned.1.call-update) | async-done | bytes 983056 | tf_op jit(solution)/shard_map/psum | solution.py:716
  1428.6 90.8 %reduce-scatter.8.cloned.1.call-done = bf16[512,1024]{1,0:T(8,128)(2,1)} async-done(((bf16[4096,1024]{1,0:T(8,128)(2,1)}), bf16[512,1024]{1,0:T(8,128)(2,1)}) %reduce-scatter.8.cloned.1.call-update) | async-done | bytes 1048592 | tf_op jit(solution)/shard_map/reduce_scatter | solution.py:713
  1522.2 29.7 %reduce-scatter.4.cloned.1.call-done = bf16[2,256,256]{2,1,0:T(8,128)(2,1)} async-done(((bf16[2,256,1024]{2,1,0:T(8,128)(2,1)}), bf16[2,256,256]{2,1,0:T(8,128)(2,1)}) %reduce-scatter.4.cloned.1.call-update) | async-done | bytes 262160 | tf_op jit(solution)/shard_map/reduce_scatter | solution.py:718
  1551.9 129.5 %all-reduce.38.cloned.1.call-done = (f32[1024]{0:T(1024)}, f32[3,1024]{1,0:T(4,128)}, f32[2,1024]{1,0:T(2,128)}, f32[2,1024]{1,0:T(2,128)}, f32[2,1024]{1,0:T(2,...) async-done(((f32[1024]{0:T(1024)}, f32[3,1024]{1,0:T(4,128)}, f32[2,1024]{1,0:T(2,128)}, f32[2,1024]{1,0:T(2,128)}, f32[2,1024]{1,0:T(2,128)}, ...) | async-done | bytes 73744 | tf_op jit(solution)/shard_map/psum | solution.py:716
  (710 shorter events, 780.7 us)
Async XLA Ops:
  7.2 83.2 %all-gather.2.cloned.1.call-start = ((), (), s32[]{:S(2)}) async-start(), calls=%async_computation.3 | async-start | bytes 9437184 | tf_op jit(solution)/shard_map/all_gather | solution.py:401
  7.9 1319.3 %reduce-scatter.6.cloned.1.call-start = ((), (), s32[]{:S(2)}) async-start(), calls=%async_computation.5 | async-start | bytes 245760 | tf_op jit(solution)/shard_map/reduce_scatter | solution.py:721
  12.1 84.0 %copy-start.162 = (bf16[2,256,192]{1,2,0:T(8,128)(2,1)S(1)}, bf16[2,256,192]{1,2,0:T(8,128)(2,1)}, u32[]{:S(2)}) copy-start(bf16[2,256,192]{1,2,0:T(8,128)(2,1)} %param.156) | copy-start | bytes 589828
  12.1 84.0 %copy-start.188 = (bf16[3,1024]{1,0:T(4,128)(2,1)S(1)}, bf16[3,1024]{1,0:T(4,128)(2,1)}, u32[]{:S(2)}) copy-start(bf16[3,1024]{1,0:T(4,128)(2,1)} %param.165) | copy-start | bytes 18436
  12.1 84.0 %copy-start.189 = (bf16[2,1024]{1,0:T(2,128)(2,1)S(1)}, bf16[2,1024]{1,0:T(2,128)(2,1)}, u32[]{:S(2)}) copy-start(bf16[2,1024]{1,0:T(2,128)(2,1)} %param.167) | copy-start | bytes 12292
  192.3 13.0 collective-permute-start
  193.6 22.9 %collective-permute-start.1 = (bf16[256,1024]{1,0:T(8,128)(2,1)}, bf16[256,1024]{1,0:T(8,128)(2,1)}, u32[]{:S(2)}, u32[]{:S(2)}) collective-permute-start(bf16[256,1024]{1,0:T(8,128)(2,1)} %get-tuple-element.3163), channel_id=1, source_target_pairs={{0,8},{8,16},{16,24},{1,9},{9,17},{17,25},{2,10},{10,18},{18,26},{... | collective-permute-start | bytes 1572872 | tf_op jit(solution)/shard_map/ppermute | solution.py:32
  317.1 12.5 collective-permute-start.2
  318.6 22.3 %collective-permute-start.3 = (bf16[256,1024]{1,0:T(8,128)(2,1)}, bf16[256,1024]{1,0:T(8,128)(2,1)}, u32[]{:S(2)}, u32[]{:S(2)}) collective-permute-start(bf16[256,1024]{1,0:T(8,128)(2,1)} %copy-done.226), channel_id=1, source_target_pairs={{0,8},{8,16},{16,24},{1,9},{9,17},{17,25},{2,10},{10,18},{18,26},{... | collective-permute-start | bytes 1572872 | tf_op jit(solution)/shard_map/ppermute | solution.py:32
  358.8 43.1 %collective-permute-start.4 = (bf16[256,1024]{1,0:T(8,128)(2,1)}, bf16[256,1024]{1,0:T(8,128)(2,1)}, u32[]{:S(2)}, u32[]{:S(2)}) collective-permute-start(bf16[256,1024]{1,0:T(8,128)(2,1)} %get-tuple-element.3168), channel_id=1, source_target_pairs={{0,8},{8,16},{16,24},{1,9},{9,17},{17,25},{2,10},{10,18},{18,26},{... | collective-permute-start | bytes 1572872 | tf_op jit(solution)/shard_map/ppermute | solution.py:32
  392.5 20.6 %collective-permute-start.5 = (bf16[256,1024]{1,0:T(8,128)(2,1)}, bf16[256,1024]{1,0:T(8,128)(2,1)}, u32[]{:S(2)}, u32[]{:S(2)}) collective-permute-start(bf16[256,1024]{1,0:T(8,128)(2,1)} %get-tuple-element.3169), channel_id=1, source_target_pairs={{0,8},{8,16},{16,24},{1,9},{9,17},{17,25},{2,10},{10,18},{18,26},{... | collective-permute-start | bytes 1572872 | tf_op jit(solution)/shard_map/ppermute | solution.py:32
  427.9 13.4 collective-permute-start.7
  488.4 27.3 %collective-permute-start.8 = (bf16[256,1024]{1,0:T(8,128)(2,1)}, bf16[256,1024]{1,0:T(8,128)(2,1)S(1)}, u32[]{:S(2)}, u32[]{:S(2)}) collective-permute-start(bf16[256,1024]{1,0:T(8,128)(2,1)} %get-tuple-element.3174), channel_id=1, source_target_pairs={{8,0},{16,8},{24,16},{9,1},{17,9},{25,17},{10,2},{18,10},{26,18},{... | collective-permute-start | bytes 1572872 | tf_op jit(solution)/shard_map/ppermute | solution.py:32
  558.0 13.7 collective-permute-start.9
  572.5 123.4 %copy-start.34 = (bf16[256,1024]{1,0:T(8,128)(2,1)S(1)}, bf16[256,1024]{1,0:T(8,128)(2,1)}, u32[]{:S(2)}) copy-start(bf16[256,1024]{1,0:T(8,128)(2,1)} %get-tuple-element.4981) | copy-start | bytes 1572868
  613.4 81.6 %collective-permute-start.10 = (bf16[256,1024]{1,0:T(8,128)(2,1)}, bf16[256,1024]{1,0:T(8,128)(2,1)S(1)}, u32[]{:S(2)}, u32[]{:S(2)}) collective-permute-start(bf16[256,1024]{1,0:T(8,128)(2,1)} %get-tuple-element.3178), channel_id=1, source_target_pairs={{8,0},{16,8},{24,16},{9,1},{17,9},{25,17},{10,2},{18,10},{26,18},{... | collective-permute-start | bytes 1572872 | tf_op jit(solution)/shard_map/ppermute | solution.py:32
  695.8 302.9 %copy-start.65 = (bf16[256,1024]{1,0:T(8,128)(2,1)S(1)}, bf16[256,1024]{1,0:T(8,128)(2,1)}, u32[]{:S(2)}) copy-start(bf16[256,1024]{1,0:T(8,128)(2,1)} %get-tuple-element.4980) | copy-start | bytes 1572868
  987.6 11.1 collective-permute-start.11
  1267.1 161.5 %all-reduce.40.cloned.1.call-start = ((), (), s32[]{:S(2)}) async-start(), calls=%async_computation.8 | async-start | bytes 1966080 | tf_op jit(solution)/shard_map/psum | solution.py:716
  1272.3 247.2 %reduce-scatter.8.cloned.1.call-start = ((), (), s32[]{:S(2)}) async-start(), calls=%async_computation.6 | async-start | bytes 9437184 | tf_op jit(solution)/shard_map/reduce_scatter | solution.py:713
  1303.3 248.6 %reduce-scatter.4.cloned.1.call-start = ((), (), s32[]{:S(2)}) async-start(), calls=%async_computation.4 | async-start | bytes 1310720 | tf_op jit(solution)/shard_map/reduce_scatter | solution.py:718
  1307.7 9.0 collective-permute-start.6
  1323.1 358.3 %all-reduce.38.cloned.1.call-start = ((), (), s32[]{:S(2)}) async-start(), calls=%async_computation.7 | async-start | bytes 163840 | tf_op jit(solution)/shard_map/psum | solution.py:716
  1428.6 256.5 %copy-start.222 = (f32[48,1024]{1,0:T(8,128)S(1)}, f32[48,1024]{1,0:T(8,128)}, u32[]{:S(2)}) copy-start(f32[48,1024]{1,0:T(8,128)} %get-tuple-element.5407) | copy-start | bytes 589828
  (156 other events, 1899.4 us)
Sparse Core Ops, SparseCore 0:
  9.6 80.7 all-gather.1
  1267.2 27.7 reduce-scatter.5
  1300.9 127.6 all-reduce.39
  1430.8 88.5 reduce-scatter.7
  1523.0 28.9 reduce-scatter.3
  1559.4 122.0 all-reduce.37
where the time goes:
time: 1720 us; the launch traced here: 1700 us
  waiting for transfers between devices  599 us (35%)
  local copies, waits for them, and re-layouts  428 us (25%)
  other arithmetic  255 us (15%)
  loops' own time  185 us (11%)
  matrix products  166 us (10%)
  starting transfers between devices  53.7 us (3%)
    psum x2, waiting for transfers between devices, on_device(): small_sums = lax.psum(small_total, ('section', 'dp'))  229 us
    ppermute x12, waiting for transfers between devices, from_behind(): return lax.ppermute(array, axis, pairs)  171 us
    another operation x5, loops' own time, on_device(): lax.switch(branch, backward_list, operands)  121 us
    convert_element_type x4, local copies, waits for them, and re-layouts, embed_rows(): (attend_low.astype(wide_type)[:, :, :, None] * pixels[:, :, None, :]).ast...  91.1 us
    reduce_scatter x1, waiting for transfers between devices, on_device(): lax.psum_scatter(bank_total.astype(jnp.bfloat16), 'dp', scatter_dimension...  90.8 us
    another operation x74, local copies, waits for them, and re-layouts  80 us
    all_gather x1, waiting for transfers between devices, on_device(): gathered = lax.all_gather(bank, 'dp', axis=1, tiled=True)[0]  78.2 us
    another operation x5, loops' own time, on_device(): lax.switch(branch, forward_list, operands)  63.8 us
  transfers between devices with their start and end apart: 18, of which 17 were waited for; matrix products, arithmetic and copies ran while one was open for 5% of the time, Pallas kernels for 0%

commit v1 on v0

--- a/solution.py
+++ b/solution.py
@@ -1,8 +1,11 @@
+import functools
 import math
 
 import jax
 import jax.numpy as jnp
 from jax import lax
+from jax.experimental import pallas as pl
+from jax.experimental.pallas import tpu as pltpu
 from jax.sharding import PartitionSpec as P
 
 D = 1024
@@ -11,6 +14,1303 @@
 FF = 4096
 VARS = 48
 PIX = 4
+F32 = jnp.float32
+BF = jnp.bfloat16
+MESH = pl.DeviceIdType.MESH
+ROWS = 512
+GROUP = 256
+OWN = 128
+
+
+def mm(a, b):
+    return jnp.dot(a, b, preferred_element_type=F32)
+
+
+def mm_nt(a, b):
+    return lax.dot_general(a, b, (((1,), (1,)), ((), ())), preferred_element_type=F32)
+
+
+def mm_tn(a, b):
+    return lax.dot_general(a, b, (((0,), (0,)), ((), ())), preferred_element_type=F32)
+
+
+def loop(count, body):
+    def step(i, carry):
+        body(i)
+        return carry
+
+    lax.fori_loop(0, count, step, 0)
+
+
+def at(start, size, unit):
+    return pl.ds(pl.multiple_of(start, unit), size)
+
+
+def iota(shape, axis):
+    return lax.broadcasted_iota(jnp.int32, shape, axis)
+
+
+def normed_rows(x, gain, shift):
+    centre = x - jnp.mean(x, axis=1, keepdims=True)
+    rs = lax.rsqrt(jnp.mean(centre * centre, axis=1, keepdims=True) + 1e-5)
+    return centre * rs * gain + shift
+
+
+def norm_back(x, g, gain):
+    centre = x - jnp.mean(x, axis=1, keepdims=True)
+    rs = lax.rsqrt(jnp.mean(centre * centre, axis=1, keepdims=True) + 1e-5)
+    xhat = centre * rs
+    q = g * gain
+    gx = rs * (q - jnp.mean(q, axis=1, keepdims=True) - xhat * jnp.mean(q * xhat, axis=1, keepdims=True))
+    return gx, jnp.sum(g * xhat, axis=0, keepdims=True), jnp.sum(g, axis=0, keepdims=True)
+
+
+def column_sum(x):
+    return jnp.sum(x, axis=0, keepdims=True)
+
+
+class Place:
+    def __init__(self):
+        self.s = lax.axis_index("section")
+        j = lax.axis_index("dp")
+        self.z = lax.div(j, 2)
+        self.c = lax.rem(j, 2)
+        self.outer = (self.z == 0) | (self.z == 3)
+        self.far = jnp.where(self.outer, self.z ^ 2, self.z ^ 3)
+
+    def dev(self, s, z, c):
+        return (s, z * 2 + c)
+
+
+def remote(src, dst, ss, rs, dev):
+    return pltpu.make_async_remote_copy(
+        src_ref=src, dst_ref=dst, send_sem=ss, recv_sem=rs, device_id=dev, device_id_type=MESH
+    )
+
+
+def arrived(dst, sem):
+    pltpu.make_async_copy(dst, dst, sem).wait()
+
+
+def sent(src, sem):
+    pltpu.make_async_copy(src, src, sem).wait()
+
+
+def barrier(devs):
+    sem = pltpu.get_barrier_semaphore()
+    for dev in devs:
+        pl.semaphore_signal(sem, 1, device_id=dev, device_id_type=MESH)
+    pl.semaphore_wait(sem, len(devs))
+
+
+SCRATCH = dict(
+    msgs=((4, 512, 256), BF),
+    W=((4, 4, 2, 512, 256), BF),
+    WF=((3, 4, 2, 512, 256), BF),
+    qbuf=((2, 8, 1024), F32),
+    qb=((16, 1024), BF),
+    kq=((2, 16, 512), BF),
+    mT=((1024, 256), BF),
+    patT=((192, 512), BF),
+    fill=((1536, 192), BF),
+    fo=((16, 256), F32),
+    foc=((256, 128), F32),
+    att=((768, 512), F32),
+    op=((256, 512), BF),
+    hT=((1024, 512), BF),
+    hrow=((512, 1024), BF),
+    acc=((512, 1024), F32),
+    st0=((512, 1024), BF),
+    nrm=((512, 1024), BF),
+    nrm2=((512, 1024), BF),
+    tr=((1024, 512), BF),
+    q=((512, 256), BF),
+    k=((512, 256), BF),
+    v=((512, 256), BF),
+    attp=((8, 256, 256), F32),
+    mix=((512, 1024), BF),
+    st1=((512, 1024), BF),
+    act=((4, 512, 256), BF),
+    gp=((4, 512, 256), F32),
+    gin=((4, 512, 256), BF),
+    rsS=((512, 1024), BF),
+    rsR=((4, 128, 1024), BF),
+    gs1=((512, 1024), BF),
+    gm=((512, 256), BF),
+    gq=((3, 512, 256), BF),
+    gs0=((512, 1024), BF),
+    ga=((512, 1024), BF),
+    CR=((4, 4, 512, 256), BF),
+    RC=((2, 4, 512, 256), BF),
+    RA=((4, 512, 256), BF),
+    RB=((4, 512, 256), BF),
+    FR=((4, 512, 256), BF),
+    outR=((4, 512, 256), BF),
+    gh=((512, 256), BF),
+    ghT=((256, 512), BF),
+    gpT=((192, 512), F32),
+    G=((256, 256), F32),
+    pixS=((4, 48, 512), BF),
+    pixR=((4, 48, 512), BF),
+)
+
+SEMS = dict(
+    rW=(4, 4, 2),
+    rF=(3, 4, 2),
+    sMsg=(4,),
+    sOwn=(4, 3),
+    sFwd=(4, 4, 2),
+    sFx=(3, 3),
+    sFc=(3, 4),
+    rQ=(2,),
+    sQ=(2,),
+    rK=(2,),
+    sK=(7,),
+    sMix=(3,),
+    rMix=(4,),
+    sOut=(4,),
+    rOut=(4,),
+    sR=(2, 4),
+    rR=(2, 4),
+    sG=(2, 4),
+    rG=(2, 4),
+    sC=(4, 4),
+    rC=(4, 4),
+    sZ=(4, 4),
+    rRC=(2, 4),
+    rRA=(4,),
+    rRB=(4,),
+    sFin=(4,),
+    rFin=(4,),
+    sP=(4,),
+    rP=(4,),
+)
+NAMES = list(SCRATCH) + list(SEMS)
+
+
+class Refs:
+    pass
+
+
+def block_kernel(
+    pat, lead, lens, cot, bank, table, vec, out, gpix, gbank, gtab, small, gfo, kq_out, q_out, *scratch
+):
+    R = Refs()
+    for name, ref in zip(NAMES, scratch):
+        setattr(R, name, ref)
+    here = Place()
+    s, z, c = here.s, here.z, here.c
+    dev = here.dev
+    outer = here.outer
+    inner = jnp.logical_not(outer)
+    sib = dev(s, z, 1 - c)
+    is_row = (s >= 2) & (z >= 2)
+    peers = [s ^ 1, s ^ 2, s ^ 3]
+
+    barrier(
+        [dev(p, z, c) for p in peers]
+        + [dev(p, z, 1 - c) for p in peers]
+        + [sib]
+        + [dev(s, z ^ i, c) for i in (1, 2, 3)]
+    )
+
+    first_owner = (s == 0) & (z == 0)
+    key_owner = (s == 0) & (z == 1)
+
+    @pl.when(first_owner)
+    def _():
+        part = vec[17:18, at(c * 512, 512, 512)].astype(BF)
+        part = jnp.broadcast_to(part, (16, 512))
+        R.qbuf[0] = mm(part, bank[...])[0:8]
+        remote(R.qbuf.at[0], R.qbuf.at[1], R.sQ.at[0], R.rQ.at[0], sib).start()
+
+    used = jnp.logical_not((s == 0) & (z < 2))
+
+    @pl.when(used & jnp.logical_not(is_row))
+    def _():
+        for p in range(4):
+            R.msgs[p] = bank[:, p * 256 : (p + 1) * 256]
+
+    @pl.when(used & is_row)
+    def _():
+        for m in range(4):
+            q, h = m // 2, m % 2
+            for n in range(2):
+                lo = (2 * h + n) * 256
+                R.msgs[m, n * 256 : (n + 1) * 256, :] = bank[q * 256 : (q + 1) * 256, lo : lo + 256]
+
+    for m in range(4):
+        tp = jnp.where(is_row, 2 * c + m // 2, m)
+        tc = jnp.where(is_row, m % 2, c)
+        own = (tp == s) & (tc == c)
+
+        @pl.when(used & own)
+        def _():
+            pltpu.make_async_copy(R.msgs.at[m], R.W.at[z, s, c], R.rW.at[z, s, c]).start()
+
+        @pl.when(used & jnp.logical_not(own))
+        def _():
+            remote(R.msgs.at[m], R.W.at[z, s, tc], R.sMsg.at[m], R.rW.at[z, s, tc], dev(tp, z, tc)).start()
+
+    @pl.when(first_owner)
+    def _():
+        arrived(R.qbuf.at[1], R.rQ.at[0])
+        total = R.qbuf[0] + R.qbuf[1] + vec[0:1, :]
+        total = total.astype(BF)
+        R.qb[...] = jnp.concatenate([total, total], axis=0)
+        remote(R.qb, R.qb, R.sQ.at[1], R.rQ.at[1], dev(0, 1, c)).start()
+
+    def has(zz, b):
+        return zz >= 2 if b == 0 else zz >= 0
+
+    def full_of(zz, b):
+        if b == 0:
+            return zz >= 2, jnp.maximum(zz - 2, 0)
+        if b == 1:
+            return zz == 3, 2
+        return None, None
+
+    def spread(zz, b, k):
+        block = R.W.at[zz, b, c]
+        whole, f = full_of(zz, b)
+
+        def to_sibling():
+            remote(block, block, R.sFwd.at[zz, b, 0], R.rW.at[zz, b, c], sib).start()
+
+        def to_layer():
+            pltpu.make_async_copy(block, R.WF.at[f, s, c], R.rF.at[f, s, c]).start()
+            for i, p in enumerate(peers):
+                remote(block, R.WF.at[f, s, c], R.sFx.at[f, i], R.rF.at[f, s, c], dev(p, z, c)).start()
+
+        if whole is None:
+            to_sibling()
+        else:
+            if b == 1:
+                pl.when(jnp.logical_not(whole))(to_sibling)
+            pl.when(whole)(to_layer)
+
+    def own_bundle(b):
+        @pl.when(has(z, b))
+        def _():
+            block = R.W.at[z, b, c]
+            arrived(block, R.rW.at[z, b, c])
+            remote(block, block, R.sOwn.at[b, 0], R.rW.at[z, b, c], dev(s, z ^ 1, c)).start()
+            remote(block, block, R.sOwn.at[b, 1], R.rW.at[z, b, c], dev(s, here.far, c)).start()
+            spread(z, b, 0)
+
+    def foreign(b, k):
+        zz = z ^ k
+
+        @pl.when(has(zz, b))
+        def _():
+            block = R.W.at[zz, b, c]
+            arrived(block, R.rW.at[zz, b, c])
+            if k > 1:
+
+                @pl.when(inner)
+                def _():
+                    remote(block, block, R.sFwd.at[zz, b, 1], R.rW.at[zz, b, c], dev(s, z ^ 1, c)).start()
+
+            spread(zz, b, k)
+
+    own_bundle(0)
+    own_bundle(1)
+
+    lens_f = lens[...].astype(F32)
+    tcol = iota((GROUP, 1), 0).astype(F32)
+    trow = iota((1, GROUP), 1).astype(F32)
+    lane4 = iota((1, 4), 1)
+    start_col = jnp.zeros((GROUP, 1), F32)
+    seg_col = jnp.zeros((GROUP, 1), F32)
+    seg_row = jnp.zeros((1, GROUP), F32)
+    for i in range(4):
+        end = jnp.sum(jnp.where(lane4 <= i, lens_f, 0.0), axis=1, keepdims=True)
+        past = tcol >= end
+        seg_col = seg_col + jnp.where(past, 1.0, 0.0)
+        seg_row = seg_row + jnp.where(trow >= end, 1.0, 0.0)
+        start_col = jnp.maximum(start_col, jnp.where(past, end, 0.0))
+    place_short = tcol - start_col
+    valid = seg_col < 3.5
+    lead_short = lead[0:1, 0:1]
+    lead_long = lead[1:2, 0:1]
+
+    freq = jnp.exp(-math.log(10000.0) * 2.0 * iota((1, 512), 1).astype(F32) / D)
+    for g in range(2):
+        place = place_short if g == 0 else tcol
+        lead_g = lead_short if g == 0 else lead_long
+        base = lead_g * vec[3:4, :] + vec[4:5, :] + vec[2:3, :]
+        angle = place * freq
+        R.acc[g * GROUP : (g + 1) * GROUP, 0:512] = jnp.sin(angle) + base[:, 0:512]
+        R.acc[g * GROUP : (g + 1) * GROUP, 512:1024] = jnp.cos(angle) + base[:, 512:1024]
+    R.gs1[0:GROUP, :] = jnp.where(valid, cot[0:GROUP, :].astype(F32), 0.0).astype(BF)
+    R.gs1[GROUP:ROWS, :] = cot[GROUP:ROWS, :]
+
+    own_bundle(2)
+    own_bundle(3)
+
+    @pl.when(key_owner)
+    def _():
+        arrived(R.qb, R.rQ.at[1])
+        head_of = iota((16, 1024), 1) // HEAD
+        masked = jnp.where(head_of == iota((16, 1024), 0), R.qb[...].astype(F32), 0.0).astype(BF)
+        R.kq[c] = mm_nt(masked, bank[...]).astype(BF)
+        for i in range(3):
+            remote(R.kq.at[c], R.kq.at[c], R.sK.at[i], R.rK.at[c], dev(s, z ^ (i + 1), c)).start()
+
+    @pl.when((s == 0) & (z != 1))
+    def _():
+        arrived(R.kq.at[c], R.rK.at[c])
+
+    @pl.when(s == 0)
+    def _():
+        for i, p in enumerate(peers):
+            remote(R.kq.at[c], R.kq.at[c], R.sK.at[3 + i], R.rK.at[c], dev(p, z, c)).start()
+
+    @pl.when(s != 0)
+    def _():
+        arrived(R.kq.at[c], R.rK.at[c])
+
+    remote(R.kq.at[c], R.kq.at[c], R.sK.at[6], R.rK.at[c], sib).start()
+
+    for b in (0, 1):
+        for k in (1, 2, 3):
+            foreign(b, k)
+
+    arrived(R.kq.at[1 - c], R.rK.at[1 - c])
+    kq_full = jnp.concatenate([R.kq[0], R.kq[1]], axis=1)
+    kq_out[...] = kq_full
+
+    @pl.when(key_owner)
+    def _():
+        q_out[...] = R.qb[...]
+
+    @pl.when(jnp.logical_not(key_owner))
+    def _():
+        q_out[...] = jnp.zeros((16, 1024), BF)
+
+    R.fo[...] = mm_nt(kq_full, table[...])
+    eye = iota((128, 16), 0) == iota((128, 16), 1)
+    fo16 = R.fo[...]
+    fo_wide = jnp.concatenate([fo16, jnp.zeros((112, 256), F32)], axis=0)
+    R.foc[...] = fo_wide.T
+    perm = jnp.where(
+        (iota((192, 192), 0) // 48 == iota((192, 192), 1) % 4) & (iota((192, 192), 0) % 48 == iota((192, 192), 1) // 4),
+        1.0,
+        0.0,
+    ).astype(BF)
+    R.patT[...] = mm_nt(perm, pat[...]).astype(BF)
+
+    def fill_head(h):
+        row = R.fo[pl.ds(h, 1), 0:192]
+        r = iota((48, 192), 0)
+        col = iota((48, 192), 1)
+        value = jnp.where(col % 48 == r, row, 0.0)
+        high = value.astype(BF)
+        R.fill[at(h * 48, 48, 16), :] = high
+        R.fill[at(768 + h * 48, 48, 16), :] = (value - high.astype(F32)).astype(BF)
+
+    loop(HEADS, fill_head)
+
+    def score_part(i):
+        lo = i * 256
+        R.att[at(lo, 256, 256), :] = mm(R.fill[at(lo, 256, 256), :], R.patT[...]) + mm(
+            R.fill[at(768 + lo, 256, 256), :], R.patT[...]
+        )
+
+    loop(3, score_part)
+
+    def pass_on(f):
+        for p in [s] + peers:
+            block = R.WF.at[f, p, c]
+            arrived(block, R.rF.at[f, p, c])
+            remote(block, block, R.sFc.at[f, p], R.rF.at[f, p, c], sib).start()
+
+    def wait_whole(f):
+        for p in range(4):
+            arrived(R.WF.at[f, p, 1 - c], R.rF.at[f, p, 1 - c])
+
+    pass_on(0)
+    wait_whole(0)
+
+    for i in range(4):
+        R.tr[i * 256 : (i + 1) * 256, 0:256] = table[:, i * 256 : (i + 1) * 256].T
+    bias_lane = iota((1, 256), 1) == 240
+
+    def table_part(p):
+        rows = at(p * 256, 256, 256)
+        value = mm_tn(R.WF[0, p, 0], R.tr[0:512, 0:256]) + mm_tn(R.WF[0, p, 1], R.tr[512:1024, 0:256])
+        bias = jnp.broadcast_to(vec[1:2, rows], (8, 256)).T[:, 0:1]
+        R.mT[rows, :] = jnp.where(bias_lane, bias, value).astype(BF)
+
+    loop(4, table_part)
+    pass_on(1)
+
+    R.op[240:256, :] = jnp.where(iota((16, 512), 0) == 0, 1.0, 0.0).astype(BF)
+    r48 = iota((48, 256), 0)
+    c48 = iota((48, 256), 1)
+
+    def weights_of(h, low):
+        lowf = low.astype(F32)
+        for p in range(4):
+            R.op[p * 48 : (p + 1) * 48, :] = (lowf * R.patT[p * 48 : (p + 1) * 48, :].astype(F32)).astype(BF)
+        R.op[192:240, :] = low
+
+    def embed_head(h):
+        offset = jnp.sum(jnp.where(c48 == r48 + 192, R.fo[pl.ds(h, 1), :], 0.0), axis=1, keepdims=True)
+        rows = at(h * 48, 48, 16)
+        scores = (R.att[rows, :] + offset) * (1.0 / math.sqrt(HEAD))
+        peak = jnp.max(scores, axis=0, keepdims=True)
+        e = jnp.exp(scores - peak)
+        prob = e / jnp.sum(e, axis=0, keepdims=True)
+        R.att[rows, :] = prob
+        weights_of(h, prob.astype(BF))
+        hrows = at(h * 64, 64, 64)
+        R.hT[hrows, :] = mm(R.mT[hrows, :], R.op[...]).astype(BF)
+
+    loop(HEADS, embed_head)
+
+    def turn_tile(i):
+        rows = at(i * 256, 256, 256)
+        R.hrow[:, rows] = R.hT[rows, :].T
+
+    loop(4, turn_tile)
+
+    wait_whole(1)
+
+    def stream0_part(i):
+        g = lax.div(i, 4)
+        n = lax.rem(i, 4)
+        rows = at(g * 256, 256, 256)
+        cols = at(n * 256, 256, 256)
+        value = mm(R.hrow[rows, 0:512], R.WF[1, n, 0]) + mm(R.hrow[rows, 512:1024], R.WF[1, n, 1])
+        R.st0[rows, cols] = (value + R.acc[rows, cols]).astype(BF)
+
+    loop(8, stream0_part)
+
+    def norm_into(src, dst, which):
+        def part(i):
+            rows = at(i * 64, 64, 64)
+            dst[rows, :] = normed_rows(
+                src[rows, :].astype(F32), vec[5 + which : 6 + which, :], vec[7 + which : 8 + which, :]
+            ).astype(BF)
+
+        loop(8, part)
+
+    norm_into(R.st0, R.nrm, 0)
+
+    own_cols = at(s * 256, 256, 256)
+    for zz in range(3):
+        arrived(R.W.at[zz, 1, 1 - c], R.rW.at[zz, 1, 1 - c])
+
+    def project(zz, dst, bias):
+        weight = R.W[zz, 1].reshape(1024, 256)
+        for g in range(2):
+            rows = slice(g * 256, (g + 1) * 256)
+            value = mm(R.nrm[rows, :], weight)
+            if bias is not None:
+                value = value + vec[bias : bias + 1, own_cols]
+            dst[rows, :] = value.astype(BF)
+
+    project(0, R.q, 9)
+    project(1, R.k, None)
+    project(2, R.v, 10)
+
+    pass_on(2)
+    for k in (1, 2, 3):
+        foreign(2, k)
+
+    lane_head = iota((1, 256), 1) // HEAD
+
+    def only(hh, x):
+        return jnp.where(lane_head == hh, x.astype(F32), 0.0).astype(BF)
+
+    allowed = seg_col == seg_row
+
+    def attend(g):
+        rows = slice(g * 256, (g + 1) * 256)
+        total = jnp.zeros((256, 256), F32)
+        for hh in range(4):
+            scores = mm_nt(R.q[rows, :], only(hh, R.k[rows, :])) * (1.0 / math.sqrt(HEAD))
+            if g == 0:
+                scores = jnp.where(allowed, scores, -1e30)
+            e = jnp.exp(scores - jnp.max(scores, axis=1, keepdims=True))
+            prob = e / jnp.sum(e, axis=1, keepdims=True)
+            R.attp[g * 4 + hh] = prob
+            total = total + mm(prob.astype(BF), only(hh, R.v[rows, :]))
+        R.mix[rows, own_cols] = total.astype(BF)
+
+    attend(0)
+    attend(1)
+    mine = R.mix.at[:, own_cols]
+    for i, p in enumerate(peers):
+        remote(mine, mine, R.sMix.at[i], R.rMix.at[s], dev(p, z, c)).start()
+    for k in (1, 2, 3):
+        foreign(3, k)
+    wait_whole(2)
+    for p in peers:
+        theirs = R.mix.at[:, at(p * 256, 256, 256)]
+        arrived(theirs, R.rMix.at[p])
+
+    def stream1_part(i):
+        g = lax.div(i, 4)
+        n = lax.rem(i, 4)
+        rows = at(g * 256, 256, 256)
+        cols = at(n * 256, 256, 256)
+        value = mm(R.mix[rows, 0:512], R.WF[2, n, 0]) + mm(R.mix[rows, 512:1024], R.WF[2, n, 1])
+        value = value + vec[11:12, cols] + R.st0[rows, cols].astype(F32)
+        R.st1[rows, cols] = value.astype(BF)
+
+    loop(8, stream1_part)
+    norm_into(R.st1, R.nrm2, 1)
+
+    gout = R.gs1
+
+    def wait_half(zz, b):
+        arrived(R.W.at[zz, b, 1 - c], R.rW.at[zz, b, 1 - c])
+
+    for zz in (0, 1):
+        for b in (2, 3):
+            wait_half(zz, b)
+
+    def feed_in(i):
+        b = lax.div(i, 2)
+        g = lax.rem(i, 2)
+        rows = at(g * 256, 256, 256)
+        bias = vec[pl.ds(12 + b, 1), own_cols]
+        weight = R.W[lax.rem(b, 2), 2 + lax.div(b, 2)].reshape(1024, 256)
+        x = mm(R.nrm2[rows, :], weight) + bias
+        half_cdf = 0.5 + 0.5 * lax.erf(x * math.sqrt(0.5))
+        R.act[b, rows, :] = (x * half_cdf).astype(BF)
+        R.gp[b, rows, :] = half_cdf + x * (jnp.exp(-0.5 * x * x) * (1.0 / math.sqrt(2.0 * math.pi)))
+
+    loop(8, feed_in)
+    for zz in (2, 3):
+        for b in (2, 3):
+            wait_half(zz, b)
+
+    def feed_back(i):
+        b = lax.div(i, 2)
+        g = lax.rem(i, 2)
+        rows = at(g * 256, 256, 256)
+        block = R.W.at[2 + lax.rem(b, 2), 2 + lax.div(b, 2)]
+        total = jnp.zeros((256, 256), F32)
+        for n in range(4):
+            tile = block[n // 2, (n % 2) * 256 : (n % 2 + 1) * 256, :]
+            total = total + mm_nt(gout[rows, n * 256 : (n + 1) * 256], tile)
+        gin = (total * R.gp[b, rows, :]).astype(BF)
+        R.gin[b, rows, :] = gin
+
+    loop(8, feed_back)
+
+    def reduce_rows(phase, make):
+        for i, p in enumerate(peers):
+            make(p)
+            block = R.rsS.at[at(p * OWN, OWN, OWN), :]
+            remote(block, R.rsR.at[s], R.sR.at[phase, i], R.rR.at[phase, s], dev(p, z, c)).start()
+        make(s)
+
+    own_rows = at(s * OWN, OWN, OWN)
+
+    def reduced(phase):
+        total = R.rsS[own_rows, :].astype(F32)
+        for p in peers:
+            arrived(R.rsR.at[p], R.rR.at[phase, p])
+            total = total + R.rsR[p].astype(F32)
+        return total
+
+    def gather_rows(phase, ref):
+        block = ref.at[own_rows, :]
+        for i, p in enumerate(peers):
+            remote(block, block, R.sG.at[phase, i], R.rG.at[phase, s], dev(p, z, c)).start()
+
+    def gathered(phase, ref):
+        for p in peers:
+            arrived(ref.at[at(p * OWN, OWN, OWN), :], R.rG.at[phase, p])
+
+    def feed_norm(p):
+        rows = at(p * OWN, OWN, OWN)
+        total = jnp.zeros((OWN, 1024), F32)
+        for b in range(4):
+            total = total + mm_nt(R.gin[b, rows, :], R.W[b % 2, 2 + b // 2].reshape(1024, 256))
+        R.rsS[rows, :] = total.astype(BF)
+
+    reduce_rows(0, feed_norm)
+
+    def out_part(i):
+        g = lax.div(i, 4)
+        n = lax.rem(i, 4)
+        rows = at(g * 256, 256, 256)
+        total = jnp.zeros((256, 256), F32)
+        for b in range(4):
+            tile = R.W[2 + b % 2, 2 + b // 2, lax.div(n, 2), at(lax.rem(n, 2) * 256, 256, 256), :]
+            total = total + mm(R.act[b, rows, :], tile)
+        R.hrow[rows, at(n * 256, 256, 256)] = total.astype(BF)
+
+    loop(8, out_part)
+    for i, p in enumerate(peers):
+        block = R.hrow.at[:, at(p * 256, 256, 256)]
+        remote(block, R.outR.at[s], R.sOut.at[i], R.rOut.at[s], dev(p, z, c)).start()
+
+    def drain(b):
+        @pl.when(has(z, b))
+        def _():
+            block = R.W.at[z, b, c]
+            sent(block, R.sOwn.at[b, 0])
+            sent(block, R.sOwn.at[b, 1])
+
+        for k in range(4):
+            zz = z ^ k
+            block = R.W.at[zz, b, c]
+            if k > 1:
+
+                @pl.when(inner & has(zz, b))
+                def _():
+                    sent(block, R.sFwd.at[zz, b, 1])
+
+            whole, f = full_of(zz, b)
+
+            def side():
+                sent(block, R.sFwd.at[zz, b, 0])
+
+            def layer():
+                for i in range(3):
+                    sent(block, R.sFx.at[f, i])
+
+            if whole is None:
+                side()
+            else:
+                if b == 1:
+                    pl.when(jnp.logical_not(whole))(side)
+                pl.when(whole)(layer)
+
+    drain(2)
+    drain(3)
+
+    def transposed(src):
+        def part(i):
+            a = lax.div(i, 2)
+            b = lax.rem(i, 2)
+            R.tr[at(a * 256, 256, 256), at(b * 256, 256, 256)] = src[
+                at(b * 256, 256, 256), at(a * 256, 256, 256)
+            ].T
+
+        loop(8, part)
+
+    def exchange(zz, b):
+        block = R.W.at[zz, b, 1 - c]
+        remote(block, R.CR.at[zz, b], R.sC.at[zz, b], R.rC.at[zz, b], sib).start()
+
+    def column_gradient(zz, b, left, right):
+        for h in range(2):
+            R.W[zz, b, h] = mm(left[h * 512 : (h + 1) * 512, :], right).astype(BF)
+        exchange(zz, b)
+
+    transposed(R.nrm2)
+
+    def first_gradient(b):
+        column_gradient(lax.rem(b, 2), 2 + lax.div(b, 2), R.tr, R.gin[b])
+
+    loop(4, first_gradient)
+
+    def second_gradient(b):
+        zz = 2 + lax.rem(b, 2)
+        bb = 2 + lax.div(b, 2)
+        for n in range(4):
+            tile = mm_tn(R.act[b], gout[:, n * 256 : (n + 1) * 256])
+            R.W[zz, bb, n // 2, (n % 2) * 256 : (n % 2 + 1) * 256, :] = tile.astype(BF)
+        exchange(zz, bb)
+
+    loop(4, second_gradient)
+
+    small[...] = jnp.zeros((16, 1024), F32)
+    for b in range(4):
+        small[10 + b : 11 + b, own_cols] = column_sum(R.gin[b].astype(F32))
+    small[14:15, :] = column_sum(gout[own_rows, :].astype(F32))
+
+    g2 = reduced(0)
+    gx, gw, gb = norm_back(R.st1[own_rows, :].astype(F32), g2, vec[6:7, :])
+    small[4:5, :] = gw
+    small[6:7, :] = gb
+    gs1_own = (gout[own_rows, :].astype(F32) + gx).astype(BF)
+    small[9:10, :] = column_sum(gs1_own.astype(F32))
+    R.ga[own_rows, :] = gs1_own
+    gather_rows(0, R.ga)
+
+    def summed(zz, b):
+        arrived(R.CR.at[zz, b], R.rC.at[zz, b])
+        sent(R.CR.at[zz, b], R.sC.at[zz, b])
+        R.W[zz, b, c] = (R.W[zz, b, c].astype(F32) + R.CR[zz, b].astype(F32)).astype(BF)
+
+    def first_sends(b):
+        for k in (0, 1, 2, 3):
+            zz = z ^ k
+
+            @pl.when(has(zz, b))
+            def _():
+                summed(zz, b)
+                block = R.W.at[zz, b, c]
+                if k == 1:
+                    remote(block, R.RA.at[b], R.sZ.at[zz, b], R.rRA.at[b], dev(s, z ^ 1, c)).start()
+                if k > 1:
+
+                    @pl.when(outer)
+                    def _():
+                        remote(
+                            block, R.RC.at[3 - k, b], R.sZ.at[zz, b], R.rRC.at[3 - k, b], dev(s, z ^ 1, c)
+                        ).start()
+
+    def second_sends(b):
+        for k in (2, 3):
+            zz = z ^ k
+
+            @pl.when(inner & has(zz, b))
+            def _():
+                block = R.W.at[zz, b, c]
+                arrived(R.RC.at[k - 2, b], R.rRC.at[k - 2, b])
+                R.W[zz, b, c] = (R.W[zz, b, c].astype(F32) + R.RC[k - 2, b].astype(F32)).astype(BF)
+                remote(block, R.RB.at[b], R.sZ.at[zz, b], R.rRB.at[b], dev(s, zz, c)).start()
+
+    row_b = [jnp.logical_and(z >= 2, b >= 2) for b in range(4)]
+
+    def last_sends(b):
+        @pl.when(has(z, b))
+        def _():
+            arrived(R.RA.at[b], R.rRA.at[b])
+            arrived(R.RB.at[b], R.rRB.at[b])
+            R.W[z, b, c] = (R.W[z, b, c].astype(F32) + R.RA[b].astype(F32) + R.RB[b].astype(F32)).astype(BF)
+            row = row_b[b]
+            tc = jnp.where(row, lax.div(s, 2), c)
+            m = jnp.where(row, lax.rem(s, 2) * 2 + c, s)
+            own = (s == b) & (tc == c)
+            block = R.W.at[z, b, c]
+
+            @pl.when(own)
+            def _():
+                pltpu.make_async_copy(block, R.FR.at[m], R.rFin.at[m]).start()
+
+            @pl.when(jnp.logical_not(own))
+            def _():
+                remote(block, R.FR.at[m], R.sFin.at[b], R.rFin.at[m], dev(b, z, tc)).start()
+
+    first_sends(2)
+    first_sends(3)
+
+    total = R.hrow[:, own_cols].astype(F32) + R.st1[:, own_cols].astype(F32) + vec[16:17, own_cols]
+    for p in peers:
+        arrived(R.outR.at[p], R.rOut.at[p])
+        total = total + R.outR[p].astype(F32)
+    out[...] = total.astype(BF)
+
+    gathered(0, R.ga)
+    gs1 = R.ga
+
+    def grad_mixed(g):
+        rows = at(g * 256, 256, 256)
+        total = jnp.zeros((256, 256), F32)
+        for n in range(4):
+            half = lax.div(s, 2)
+            tile = R.WF[2, n, half, at(lax.rem(s, 2) * 256, 256, 256), :]
+            total = total + mm_nt(gs1[rows, n * 256 : (n + 1) * 256], tile)
+        R.gm[rows, :] = total.astype(BF)
+
+    loop(2, grad_mixed)
+
+    def attend_back(g):
+        rows = at(g * 256, 256, 256)
+        qg, kg, vg, gmg = R.q[rows, :], R.k[rows, :], R.v[rows, :], R.gm[rows, :]
+        zero = jnp.zeros((256, 256), F32)
+        tq, tk, tv = zero, zero, zero
+        for hh in range(4):
+            prob = R.attp[g * 4 + hh]
+            gmh = only(hh, gmg)
+            dprob = mm_nt(gmh, vg)
+            tv = tv + mm_tn(prob.astype(BF), gmh)
+            ds = (prob * (dprob - jnp.sum(prob * dprob, axis=1, keepdims=True))).astype(BF)
+            tq = tq + mm(ds, only(hh, kg))
+            tk = tk + mm_tn(ds, only(hh, qg))
+        scale = 1.0 / math.sqrt(HEAD)
+        R.gq[0, rows, :] = (tq * scale).astype(BF)
+        R.gq[1, rows, :] = (tk * scale).astype(BF)
+        R.gq[2, rows, :] = tv.astype(BF)
+
+    loop(2, attend_back)
+
+    for i, p in enumerate(peers):
+        block = R.rsS.at[at(p * OWN, OWN, OWN), :]
+        sent(block, R.sR.at[0, i])
+
+    def attend_norm(p):
+        rows = at(p * OWN, OWN, OWN)
+        total = jnp.zeros((OWN, 1024), F32)
+        for i in range(3):
+            total = total + mm_nt(R.gq[i, rows, :], R.W[i, 1].reshape(1024, 256))
+        R.rsS[rows, :] = total.astype(BF)
+
+    reduce_rows(1, attend_norm)
+
+    second_sends(2)
+    second_sends(3)
+
+    transposed(R.nrm)
+    drain(1)
+    drain(0)
+
+    def attend_gradient(i):
+        column_gradient(i, 1, R.tr, R.gq[i])
+
+    loop(3, attend_gradient)
+    transposed(R.mix)
+    column_gradient(3, 1, R.tr, gs1[:, own_cols])
+    small[7:8, own_cols] = column_sum(R.gq[0].astype(F32))
+    small[8:9, own_cols] = column_sum(R.gq[2].astype(F32))
+
+    g1 = reduced(1)
+    gx, gw, gb = norm_back(R.st0[own_rows, :].astype(F32), g1, vec[5:6, :])
+    small[3:4, :] = gw
+    small[5:6, :] = gb
+    gs0_own = (R.ga[own_rows, :].astype(F32) + gx).astype(BF)
+    gs0_sum = column_sum(gs0_own.astype(F32))
+    small[1:2, :] = gs0_sum
+    small[2:3, :] = jnp.where(s < 2, lead_short, lead_long) * gs0_sum
+    R.gs0[own_rows, :] = gs0_own
+    gather_rows(1, R.gs0)
+    first_sends(1)
+    gathered(1, R.gs0)
+
+    gs0 = R.gs0
+    half_s = lax.div(s, 2)
+    row_s = at(lax.rem(s, 2) * 256, 256, 256)
+    total = jnp.zeros((256, 512), F32)
+    for n in range(4):
+        total = total + mm_nt(R.WF[1, n, half_s, row_s, :], gs0[:, n * 256 : (n + 1) * 256])
+    R.ghT[...] = total.astype(BF)
+    R.gh[...] = R.ghT[...].T
+    small[0:1, own_cols] = column_sum(R.gh[...].astype(F32))
+    column_gradient(3, 0, R.hT, gs0[:, own_cols])
+
+    R.gpT[...] = jnp.zeros((192, 512), F32)
+    R.G[...] = jnp.zeros((256, 256), F32)
+    gfo[...] = jnp.zeros((256, 128), F32)
+    lane128 = iota((1, 128), 1)
+
+    def embed_back(hh):
+        h = 4 * s + hh
+        prob = R.att[at(h * 48, 48, 16), :]
+        low = prob.astype(BF)
+        lowf = low.astype(F32)
+        weights_of(h, low)
+        gop = mm_tn(R.mT[at(h * 64, 64, 64), :], R.ghT[at(hh * 64, 64, 64), :])
+        keep = (iota((1, 256), 1) // HEAD) == hh
+        R.G[...] += jnp.where(keep, mm(R.op[...], R.gh[...]), 0.0)
+        gatt = gop[192:240, :]
+        for p in range(4):
+            gatt = gatt + gop[p * 48 : (p + 1) * 48, :] * R.patT[p * 48 : (p + 1) * 48, :].astype(F32)
+        gsc = prob * (gatt - jnp.sum(prob * gatt, axis=0, keepdims=True)) * (1.0 / math.sqrt(HEAD))
+        pick = jnp.where(lane128 == h, 1.0, 0.0)
+        for p in range(4):
+            rows = slice(p * 48, (p + 1) * 48)
+            fcol = jnp.sum(R.foc[rows, :] * pick, axis=1, keepdims=True)
+            R.gpT[rows, :] += gop[rows, :] * lowf + gsc * fcol
+            gcol = jnp.sum(R.patT[rows, :].astype(F32) * gsc, axis=1, keepdims=True)
+            gfo[rows, :] += gcol * pick
+        gfo[192:240, :] += jnp.sum(gsc, axis=1, keepdims=True) * pick
+
+    loop(4, embed_back)
+
+    gpt = R.gpT[...].astype(BF)
+    for p in range(4):
+        r = iota((48, 192), 0) + p * 48
+        col = iota((48, 192), 1)
+        select = jnp.where(col == (r % 4) * 48 + r // 4, 1.0, 0.0).astype(BF)
+        R.pixS[p] = mm(select, gpt).astype(BF)
+    for i, p in enumerate(peers):
+        remote(R.pixS.at[p], R.pixR.at[s], R.sP.at[i], R.rP.at[s], dev(p, z, c)).start()
+
+    G = R.G[...].astype(BF)
+    for h in range(2):
+        R.W[2, 0, h] = mm_tn(table[:, h * 512 : (h + 1) * 512], G).astype(BF)
+    exchange(2, 0)
+    gf = gfo[...]
+    gf_high = gf.astype(BF)
+    gf_low = (gf - gf_high.astype(F32)).astype(BF)
+    kq_wide = jnp.concatenate([kq_full, jnp.zeros((112, 1024), BF)], axis=0)
+    weight = R.WF[0, s].reshape(1024, 256)
+    gtab[...] = mm_nt(G, weight) + mm(gf_high, kq_wide) + mm(gf_low, kq_wide)
+
+    second_sends(1)
+    first_sends(0)
+    last_sends(2)
+    last_sends(3)
+    last_sends(1)
+    second_sends(0)
+
+    total = R.pixS[s].astype(F32)
+    for p in peers:
+        arrived(R.pixR.at[p], R.rP.at[p])
+        total = total + R.pixR[p].astype(F32)
+    gpix[...] = total.T
+
+    last_sends(0)
+
+    @pl.when(used)
+    def _():
+        for m in range(4):
+            arrived(R.FR.at[m], R.rFin.at[m])
+
+    @pl.when(used & jnp.logical_not(is_row))
+    def _():
+        for m in range(4):
+            gbank[:, m * 256 : (m + 1) * 256] = R.FR[m].astype(F32)
+
+    @pl.when(used & is_row)
+    def _():
+        for m in range(4):
+            q, h = m // 2, m % 2
+            for n in range(2):
+                lo = (2 * h + n) * 256
+                gbank[q * 256 : (q + 1) * 256, lo : lo + 256] = R.FR[m, n * 256 : (n + 1) * 256, :].astype(F32)
+
+    @pl.when(jnp.logical_not(used))
+    def _():
+        gbank[...] = jnp.zeros((512, 1024), F32)
+
+    for m in range(4):
+        tp = jnp.where(is_row, 2 * c + m // 2, m)
+        tc = jnp.where(is_row, m % 2, c)
+        own = (tp == s) & (tc == c)
+
+        @pl.when(used & jnp.logical_not(own))
+        def _():
+            sent(R.msgs.at[m], R.sMsg.at[m])
+
+    @pl.when(first_owner)
+    def _():
+        sent(R.qbuf.at[0], R.sQ.at[0])
+        sent(R.qb, R.sQ.at[1])
+
+    @pl.when(key_owner)
+    def _():
+        for i in range(3):
+            sent(R.kq.at[c], R.sK.at[i])
+
+    @pl.when(s == 0)
+    def _():
+        for i in range(3):
+            sent(R.kq.at[c], R.sK.at[3 + i])
+
+    sent(R.kq.at[c], R.sK.at[6])
+    for f in range(3):
+        for p in range(4):
+            sent(R.WF.at[f, p, c], R.sFc.at[f, p])
+    for i, p in enumerate(peers):
+        sent(mine, R.sMix.at[i])
+        sent(R.outR.at[p], R.sOut.at[i])
+        sent(R.rsR.at[p], R.sR.at[1, i])
+        sent(R.rsR.at[p], R.sG.at[0, i])
+        sent(R.rsR.at[p], R.sG.at[1, i])
+        sent(R.pixS.at[p], R.sP.at[i])
+    for b in range(4):
+        for k in (1, 2, 3):
+            zz = z ^ k
+
+            @pl.when(has(zz, b))
+            def _():
+                sent(R.W.at[zz, b, c], R.sZ.at[zz, b])
+
+        tc = jnp.where(row_b[b], lax.div(s, 2), c)
+        own = (s == b) & (tc == c)
+
+        @pl.when(has(z, b) & jnp.logical_not(own))
+        def _():
+            sent(R.W.at[z, b, c], R.sFin.at[b])
+
+
+def block_call(*args):
+    shape = jax.ShapeDtypeStruct
+    vmem = pl.BlockSpec(memory_space=pltpu.VMEM)
+    outs = [
+        shape((512, 256), BF),
+        shape((512, 48), F32),
+        shape((512, 1024), F32),
+        shape((256, 1024), F32),
+        shape((16, 1024), F32),
+        shape((256, 128), F32),
+        shape((16, 1024), BF),
+        shape((16, 1024), BF),
+    ]
+    return pl.pallas_call(
+        block_kernel,
+        out_shape=outs,
+        in_specs=[vmem] * len(args),
+        out_specs=[vmem] * len(outs),
+        scratch_shapes=[pltpu.VMEM(*v) for v in SCRATCH.values()]
+        + [pltpu.SemaphoreType.DMA(v) for v in SEMS.values()],
+        compiler_params=pltpu.CompilerParams(
+            collective_id=1, has_side_effects=True, vmem_limit_bytes=63 * 2**20
+        ),
+    )(*args)
+
+
+FINAL_SCRATCH = dict(
+    all_=((384, 1024), BF),
+    fin=((384, 1024), BF),
+    fromc=((192, 1024), BF),
+    fromp=((4, 48, 1024), BF),
+    part=((4, 48, 1024), BF),
+    gq=((16, 1024), BF),
+    qx=((2, 8, 1024), F32),
+    ga=((2, 8, 512), F32),
+)
+FINAL_SEMS = dict(
+    sA=(1,), rA=(1,), sB=(4,), rB=(4,), sD=(4,), rD=(4,), sE=(4,), rE=(4,), sH=(1,), rH=(1,),
+    sQ=(1,), rQ=(1,), sN=(6,), rN=(1,), sL=(7,), rL=(2,),
+)
+FINAL_NAMES = list(FINAL_SCRATCH) + list(FINAL_SEMS)
+
+
+def final_kernel(gtab, small, gfo, kq, q, bank, table, vec, tab_out, small_out, rows_out, bank_out, *scratch):
+    R = Refs()
+    for name, ref in zip(FINAL_NAMES, scratch):
+        setattr(R, name, ref)
+    here = Place()
+    s, z, c = here.s, here.z, here.c
+    dev = here.dev
+    sib = dev(s, z, 1 - c)
+    peers = [s ^ 1, s ^ 2, s ^ 3]
+    layers = [z ^ 1, z ^ 2, z ^ 3]
+    barrier([dev(p, z, c) for p in peers] + [sib] + [dev(s, i, c) for i in layers])
+
+    R.all_[0:256, :] = gtab[...].astype(BF)
+    R.all_[256:272, :] = small[...].astype(BF)
+    for i in range(8):
+        R.all_[272:304, i * 128 : (i + 1) * 128] = gfo[i * 32 : (i + 1) * 32, :].astype(BF)
+    R.all_[304:384, :] = jnp.zeros((80, 1024), BF)
+
+    half = at(c * 192, 192, 64)
+    other = R.all_.at[at((1 - c) * 192, 192, 64), :]
+    remote(other, R.fromc, R.sA.at[0], R.rA.at[0], sib).start()
+    arrived(R.fromc, R.rA.at[0])
+    R.all_[half, :] = (R.all_[half, :].astype(F32) + R.fromc[...].astype(F32)).astype(BF)
+
+    def piece(p):
+        return at(c * 192 + p * 48, 48, 16)
+
+    for i, p in enumerate(peers):
+        remote(R.all_.at[piece(p), :], R.fromp.at[s], R.sB.at[i], R.rB.at[s], dev(p, z, c)).start()
+    total = R.all_[piece(s), :].astype(F32)
+    for p in peers:
+        arrived(R.fromp.at[p], R.rB.at[p])
+        total = total + R.fromp[p].astype(F32)
+    R.part[z] = total.astype(BF)
+    for i, zz in enumerate(layers):
+        remote(R.part.at[z], R.part.at[z], R.sD.at[i], R.rD.at[z], dev(s, zz, c)).start()
+    for zz in layers:
+        arrived(R.part.at[zz], R.rD.at[zz])
+    total = R.part[0].astype(F32)
+    for zz in range(1, 4):
+        total = total + R.part[zz].astype(F32)
+    for i in range(3):
+        sent(R.part.at[0], R.sB.at[i])
+    R.fin[piece(s), :] = total.astype(BF)
+    mine = R.fin.at[piece(s), :]
+    for i, p in enumerate(peers):
+        remote(mine, mine, R.sE.at[i], R.rE.at[s], dev(p, z, c)).start()
+    for p in peers:
+        arrived(R.fin.at[piece(p), :], R.rE.at[p])
+    sent(R.fromc, R.sA.at[0])
+    whole = R.fin.at[half, :]
+    remote(whole, whole, R.sH.at[0], R.rH.at[0], sib).start()
+    arrived(R.fin.at[at((1 - c) * 192, 192, 64), :], R.rH.at[0])
+
+    tab_out[...] = R.fin[0:256, :].astype(F32)
+    small_out[...] = R.fin[256:272, :].astype(F32)
+    gf = jnp.concatenate([R.fin[272:304, i * 128 : (i + 1) * 128] for i in range(8)], axis=0)
+    gkq = mm_tn(gf, table[...])[0:16].astype(BF)
+
+    key_owner = (s == 0) & (z == 1)
+    first_owner = (s == 0) & (z == 0)
+
+    @pl.when(jnp.logical_not(key_owner | first_owner))
+    def _():
+        bank_out[...] = jnp.zeros((512, 1024), F32)
+
+    @pl.when(key_owner)
+    def _():
+        head_of = iota((16, 1024), 1) // HEAD
+        diag = head_of == iota((16, 1024), 0)
+        masked = jnp.where(diag, q[...].astype(F32), 0.0).astype(BF)
+        own = jnp.where(c == 0, gkq[:, 0:512].astype(F32), gkq[:, 512:1024].astype(F32)).astype(BF)
+        row = column_sum(jnp.where(diag, mm(own, bank[...]), 0.0))
+        R.qx[0] = jnp.broadcast_to(row, (8, 1024))
+        remote(R.qx.at[0], R.qx.at[1], R.sQ.at[0], R.rQ.at[0], sib).start()
+        bank_out[...] = mm_tn(own, masked)
+        arrived(R.qx.at[1], R.rQ.at[0])
+        row = (R.qx[0] + R.qx[1]).astype(BF)
+        R.gq[...] = jnp.concatenate([row, row], axis=0)
+        for i, zz in enumerate(layers):
+            remote(R.gq, R.gq, R.sN.at[i], R.rN.at[0], dev(s, zz, c)).start()
+        sent(R.qx.at[0], R.sQ.at[0])
+
+    @pl.when((s == 0) & (z != 1))
+    def _():
+        arrived(R.gq, R.rN.at[0])
+
+    @pl.when(s == 0)
+    def _():
+        for i, p in enumerate(peers):
+            remote(R.gq, R.gq, R.sN.at[3 + i], R.rN.at[0], dev(p, z, c)).start()
+
+    @pl.when(first_owner)
+    def _():
+        R.ga[c] = mm_nt(R.gq[...], bank[...])[0:8]
+        for i, zz in enumerate(layers):
+            remote(R.ga.at[c], R.ga.at[c], R.sL.at[i], R.rL.at[c], dev(s, zz, c)).start()
+        aq = jnp.where(c == 0, vec[17:18, 0:512], vec[17:18, 512:1024])
+        aq = jnp.where(iota((16, 512), 0) == 0, aq, 0.0).astype(BF)
+        bank_out[...] = mm_tn(aq, R.gq[...])
+
+    @pl.when((s == 0) & (z != 0))
+    def _():
+        arrived(R.ga.at[c], R.rL.at[c])
+
+    @pl.when(s == 0)
+    def _():
+        for i, p in enumerate(peers):
+            remote(R.ga.at[c], R.ga.at[c], R.sL.at[3 + i], R.rL.at[c], dev(p, z, c)).start()
+
+    @pl.when(s != 0)
+    def _():
+        arrived(R.gq, R.rN.at[0])
+        arrived(R.ga.at[c], R.rL.at[c])
+
+    remote(R.ga.at[c], R.ga.at[c], R.sL.at[6], R.rL.at[c], sib).start()
+    arrived(R.ga.at[1 - c], R.rL.at[1 - c])
+    rows_out[0:8, :] = R.gq[0:8, :].astype(F32)
+    rows_out[8:16, 0:512] = R.ga[0]
+    rows_out[8:16, 512:1024] = R.ga[1]
+
+    for i in range(3):
+        sent(R.part.at[0], R.sD.at[i])
+        sent(R.part.at[0], R.sE.at[i])
+    sent(R.fromc, R.sH.at[0])
+
+    @pl.when(key_owner)
+    def _():
+        for i in range(3):
+            sent(R.gq, R.sN.at[i])
+
+    @pl.when(first_owner)
+    def _():
+        for i in range(3):
+            sent(R.ga.at[c], R.sL.at[i])
+
+    @pl.when(s == 0)
+    def _():
+        for i in range(3):
+            sent(R.gq, R.sN.at[3 + i])
+            sent(R.ga.at[c], R.sL.at[3 + i])
+
+    sent(R.ga.at[c], R.sL.at[6])
+
+
+def final_call(*args):
+    shape = jax.ShapeDtypeStruct
+    vmem = pl.BlockSpec(memory_space=pltpu.VMEM)
+    outs = [
+        shape((256, 1024), F32),
+        shape((16, 1024), F32),
+        shape((16, 1024), F32),
+        shape((512, 1024), F32),
+    ]
+    return pl.pallas_call(
+        final_kernel,
+        out_shape=outs,
+        in_specs=[vmem] * len(args),
+        out_specs=[vmem] * len(outs),
+        scratch_shapes=[pltpu.VMEM(*v) for v in FINAL_SCRATCH.values()]
+        + [pltpu.SemaphoreType.DMA(v) for v in FINAL_SEMS.values()],
+        compiler_params=pltpu.CompilerParams(
+            collective_id=2, has_side_effects=True, vmem_limit_bytes=40 * 2**20
+        ),
+    )(*args)
+
+
+def on_device_fast(
+    patches,
+    lead_times,
+    short_lengths,
+    cotangent,
+    bank,
+    patch_w,
+    patch_b,
+    var_emb,
+    agg_query,
+    agg_bias,
+    lead_embed,
+    norm_gain,
+    norm_bias,
+    attn_bias,
+    fc1_bias,
+    fc2_bias,
+):
+    constant = (patch_b.astype(F32) + var_emb.astype(F32)).astype(BF)
+    table = jnp.concatenate(
+        [jnp.transpose(patch_w, (1, 0, 2)).reshape(VARS * PIX, D), constant, jnp.zeros((16, D), BF)], axis=0
+    )
+    vec = jnp.concatenate(
+        [
+            agg_bias,
+            lead_embed,
+            norm_gain,
+            norm_bias,
+            attn_bias,
+            fc1_bias.reshape(4, D),
+            fc2_bias[None],
+            agg_query[None],
+            jnp.zeros((6, D), BF),
+        ],
+        axis=0,
+    ).astype(F32)
+    own_bank = bank[0]
+    out, gpix, gbank, gtab, small, gfo, kq, q = block_call(
+        patches.reshape(ROWS, VARS * PIX),
+        lead_times,
+        short_lengths,
+        cotangent.reshape(ROWS, D),
+        own_bank,
+        table,
+        vec,
+    )
+    tab, sums, rows, bank_rows = final_call(gtab, small, gfo, kq, q, own_bank, table, vec)
+    vector_owner = (lax.axis_index("section") == 0) & (lax.axis_index("dp") < 4)
+    grad_bank = jnp.where(vector_owner, bank_rows, gbank)[None]
+    grad_patch_w = jnp.transpose(tab[: VARS * PIX].reshape(PIX, VARS, D), (1, 0, 2))
+    grad_constant = tab[VARS * PIX : VARS * PIX + VARS]
+    return (
+        out.reshape(2, GROUP, 256),
+        gpix.reshape(2, GROUP, 48),
+        grad_bank,
+        grad_patch_w,
+        grad_constant,
+        grad_constant,
+        rows[8],
+        jnp.stack([rows[0], sums[0], sums[1]]),
+        jnp.stack([sums[2], sums[1]]),
+        sums[3:5],
+        sums[5:7],
+        sums[7:10],
+        sums[10:14].reshape(FF),
+        sums[14],
+    )
+
+
+def specs():
+    ins = (
+        (P(None, "dp", None), P(None, "dp"), P("dp", None), P(None, "dp", None), P("section", "dp", None))
+        + (P(),) * 11
+    )
+    outs = (P(None, "dp", "section"), P(None, "dp", "section"), P("section", "dp", None)) + (P(),) * 11
+    return ins, outs
 
 
 wide_type = jnp.float32
@@ -727,42 +2027,7 @@
 
 
 def solution(mesh):
-    return jax.shard_map(
-        on_device,
-        mesh=mesh,
-        in_specs=(
-            P(None, "dp", None),
-            P(None, "dp"),
-            P("dp", None),
-            P(None, "dp", None),
-            P("section", "dp", None),
-            P(),
-            P(),
-            P(),
-            P(),
-            P(),
-            P(),
-            P(),
-            P(),
-            P(),
-            P(),
-            P(),
-        ),
-        out_specs=(
-            P(None, "dp", "section"),
-            P(None, "dp", "section"),
-            P("section", "dp", None),
-            P(),
-            P(),
-            P(),
-            P(),
-            P(),
-            P(),
-            P(),
-            P(),
-            P(),
-            P(),
-            P(),
-        ),
-        check_vma=False,
-    )
+    ins, outs = specs()
+    small_slice = mesh.shape["section"] == 4 and mesh.shape["dp"] == 8
+    body = on_device_fast if small_slice else on_device
+    return jax.shard_map(body, mesh=mesh, in_specs=ins, out_specs=outs, check_vma=False)

time: 1720 us -> 291 us (0.17)
  waiting for transfers between devices: 599 us -> 0 us
  local copies, waits for them, and re-layouts: 428 us -> 21.4 us
  Pallas kernels: 0 us -> 260 us
  other arithmetic: 255 us -> 5.67 us
  loops' own time: 185 us -> 0 us
  matrix products: 166 us -> 0 us
  starting transfers between devices: 53.7 us -> 0 us
    pallas_call x0 -> x2, Pallas kernels: none -> 260 us  [the longest x1 217 us: block_call(): pl.pallas_call(block_kernel, out_shape=outs, in_specs=[vmem] * len(args),...]
    psum x2 -> x0, waiting for transfers between devices: 229 us -> none  [on_device(): small_sums = lax.psum(small_total, ('section', 'dp'))]
    another operation x10 -> x0, loops' own time: 185 us -> none  [the longest x5 121 us: on_device(): lax.switch(branch, backward_list, operands)]
    ppermute x12 -> x0, waiting for transfers between devices: 171 us -> none  [from_behind(): return lax.ppermute(array, axis, pairs)]
    dot_general x58 -> x0, matrix products: 166 us -> none  [the longest x4 35.7 us: embed_rows(): jnp.einsum('thd,dhe->the', pooled, weights[2].reshape(D, HEADS, HEAD), pr...]
    convert_element_type x26 -> x0, local copies, waits for them, and re-layouts: 147 us -> none  [the longest x4 91.1 us: embed_rows(): (attend_low.astype(wide_type)[:, :, :, None] * pixels[:, :, None, :]).ast...]
    reduce_scatter x3 -> x0, waiting for transfers between devices: 121 us -> none  [the longest x1 90.8 us: on_device(): lax.psum_scatter(bank_total.astype(jnp.bfloat16), 'dp', scatter_dimension...]
    convert_element_type x42 -> x2, other arithmetic: 91.6 us -> 1.62 us  [the longest x1 0.97 us: on_device_fast(): constant = (patch_b.astype(F32) + var_emb.astype(F32)).astype(BF)]
  transfers between devices with their start and end apart: 18 -> 0, of which waited for: 17 -> 0; matrix products, arithmetic and copies ran while one was open for 5% -> 0% of each run, Pallas kernels for 0% -> 0%
where the time goes in v1:
time: 291 us; the launch traced here: 288 us
  Pallas kernels  260 us (89%)
  local copies, waits for them, and re-layouts  21.4 us (7%)
  other arithmetic  5.67 us (2%)
    pallas_call x1, Pallas kernels, block_call(): pl.pallas_call(block_kernel, out_shape=outs, in_specs=[vmem] * len(args),...  217 us
    pallas_call x1, Pallas kernels, final_call(): pl.pallas_call(final_kernel, out_shape=outs, in_specs=[vmem] * len(args),...  42.6 us
    unnamed x29, local copies, waits for them, and re-layouts  12.5 us

profile of v1, /device:TPU:25, one launch (start us, length us, event | category | flops | bytes accessed | tf_op | source)
XLA Modules:
  0.0 287.8 jit_solution(15753603248775940248)
XLA Ops:
  0.7 1.3 copy.32.lead
  2.0 0.7 broadcast_in_dim.17
  2.7 0.7 broadcast_in_dim.16
  3.4 0.7 reshape.55
  4.1 2.3 concatenate.7
  6.4 0.7 convert_element_type.15.vec
  7.1 1.0 add_convert_fusion
  8.0 1.8 copy.30
  9.8 1.1 copy.31
  10.9 0.9 maximum_maximum_fusion.table
  11.9 217.5 %shard_map.263 = (bf16[512,256]{1,0:T(8,128)(2,1)}, f32[512,48]{1,0:T(8,128)}, f32[512,1024]{1,0:T(8,128)}, f32[256,1024]{1,0:T(8,128)}, f32[16,1024]{1,0:T(8,12...) custom-call(bf16[512,192]{1,0:T(8,128)(2,1)} %bitcast.24, f32[2,1]{1,0:T(2,128)} %copy.32.lead, ...), custom_call_target="tpu_custom_call" | custom-call | tf_op jit(solution)/shard_map/pallas_call | solution.py:1041
  229.4 1.7 copy.34
  231.1 1.2 copy-done.1
  232.3 1.2 copy-done.2
  233.5 0.9 copy-done.4
  234.4 0.8 copy-done.5
  235.3 0.8 copy-done.6
  236.0 0.8 copy-done.7
  236.8 42.6 %shard_map.264 = (f32[256,1024]{1,0:T(8,128)S(1)}, f32[16,1024]{1,0:T(8,128)S(1)}, f32[16,1024]{1,0:T(8,128)S(1)}, f32[512,1024]{1,0:T(8,128)S(1)}) custom-call(f32[256,1024]{1,0:T(8,128)S(1)} %copy-done.2, f32[16,1024]{1,0:T(8,128)S(1)} %copy-done.5, f32[256,128]{1,0:T(8,128)S(1)} %copy-done.4, bf16[16,1024]{1,0:T(8,128)(2,1)S(1)} %copy-done.6, ...), custom_call_target="tpu_custom_call" | custom-call | tf_op jit(solution)/shard_map/pallas_call | solution.py:1225
  279.4 1.9 select_bitcast_fusion
  284.3 0.6 pad_maximum_fusion
  285.1 1.4 copy.38
  286.5 0.7 copy.42
  287.1 0.7 copy.43
  (27 shorter events, 3.3 us)
Async XLA Ops:
  10.9 220.1 %copy-start.3 = (f32[24,1024]{1,0:T(8,128)S(1)}, f32[24,1024]{1,0:T(8,128)}, u32[]{:S(2)}) copy-start(f32[24,1024]{1,0:T(8,128)} %convert_element_type.15.vec) | copy-start | bytes 294916
  11.9 219.2 %copy-start = (bf16[256,1024]{1,0:T(8,128)(2,1)S(1)}, bf16[256,1024]{1,0:T(8,128)(2,1)}, u32[]{:S(2)}) copy-start(bf16[256,1024]{1,0:T(8,128)(2,1)} %maximum_maximum_fusion.table) | copy-start | bytes 1572868
  231.1 1.2 copy-start.1
  232.3 1.2 copy-start.2
  233.5 0.9 copy-start.4
  234.4 0.8 copy-start.5
  235.3 0.8 copy-start.6
  236.0 0.8 copy-start.7
  236.8 42.6 %copy-start.8 = (f32[512,1024]{1,0:T(8,128)S(1)}, f32[512,1024]{1,0:T(8,128)}, u32[]{:S(2)}) copy-start(f32[512,1024]{1,0:T(8,128)} %get-tuple-element.34) | copy-start | bytes 6291460
  281.3 5.9 %copy-start.10 = (bf16[512,256]{1,0:T(8,128)(2,1)S(1)}, bf16[512,256]{1,0:T(8,128)(2,1)}, u32[]{:S(2)}) copy-start(bf16[512,256]{1,0:T(8,128)(2,1)} %get-tuple-element.26) | copy-start | bytes 786436
  285.0 2.9 copy-start.9

commit v2 on v0

--- a/solution.py
+++ b/solution.py
@@ -1,8 +1,11 @@
+import functools
 import math
 
 import jax
 import jax.numpy as jnp
 from jax import lax
+from jax.experimental import pallas as pl
+from jax.experimental.pallas import tpu as pltpu
 from jax.sharding import PartitionSpec as P
 
 D = 1024
@@ -11,6 +14,1457 @@
 FF = 4096
 VARS = 48
 PIX = 4
+F32 = jnp.float32
+BF = jnp.bfloat16
+MESH = pl.DeviceIdType.MESH
+ROWS = 512
+GROUP = 256
+OWN = 128
+
+
+def mm(a, b):
+    return jnp.dot(a, b, preferred_element_type=F32)
+
+
+def mm_nt(a, b):
+    return lax.dot_general(a, b, (((1,), (1,)), ((), ())), preferred_element_type=F32)
+
+
+def mm_tn(a, b):
+    return lax.dot_general(a, b, (((0,), (0,)), ((), ())), preferred_element_type=F32)
+
+
+def loop(count, body):
+    def step(i, carry):
+        body(i)
+        return carry
+
+    lax.fori_loop(0, count, step, 0)
+
+
+def at(start, size, unit):
+    return pl.ds(pl.multiple_of(start, unit), size)
+
+
+def iota(shape, axis):
+    return lax.broadcasted_iota(jnp.int32, shape, axis)
+
+
+def normed_rows(x, gain, shift):
+    centre = x - jnp.mean(x, axis=1, keepdims=True)
+    rs = lax.rsqrt(jnp.mean(centre * centre, axis=1, keepdims=True) + 1e-5)
+    return centre * rs * gain + shift
+
+
+def norm_back(x, g, gain):
+    centre = x - jnp.mean(x, axis=1, keepdims=True)
+    rs = lax.rsqrt(jnp.mean(centre * centre, axis=1, keepdims=True) + 1e-5)
+    xhat = centre * rs
+    q = g * gain
+    gx = rs * (q - jnp.mean(q, axis=1, keepdims=True) - xhat * jnp.mean(q * xhat, axis=1, keepdims=True))
+    return gx, jnp.sum(g * xhat, axis=0, keepdims=True), jnp.sum(g, axis=0, keepdims=True)
+
+
+def column_sum(x):
+    return jnp.sum(x, axis=0, keepdims=True)
+
+
+class Place:
+    def __init__(self):
+        self.s = lax.axis_index("section")
+        j = lax.axis_index("dp")
+        self.z = lax.div(j, 2)
+        self.c = lax.rem(j, 2)
+        self.outer = (self.z == 0) | (self.z == 3)
+        self.far = jnp.where(self.outer, self.z ^ 2, self.z ^ 3)
+
+    def dev(self, s, z, c):
+        return (s, z * 2 + c)
+
+
+def remote(src, dst, ss, rs, dev):
+    return pltpu.make_async_remote_copy(
+        src_ref=src, dst_ref=dst, send_sem=ss, recv_sem=rs, device_id=dev, device_id_type=MESH
+    )
+
+
+def arrived(dst, sem):
+    pltpu.make_async_copy(dst, dst, sem).wait()
+
+
+def sent(src, sem):
+    pltpu.make_async_copy(src, src, sem).wait()
+
+
+def barrier(devs):
+    sem = pltpu.get_barrier_semaphore()
+    for dev in devs:
+        pl.semaphore_signal(sem, 1, device_id=dev, device_id_type=MESH)
+    pl.semaphore_wait(sem, len(devs))
+
+
+SCRATCH = dict(
+    vec=((24, 1024), F32),
+    table=((256, 1024), BF),
+    tabT=((1024, 256), BF),
+    msgs=((4, 512, 256), BF),
+    W=((4, 4, 2, 512, 256), BF),
+    WF=((3, 4, 2, 512, 256), BF),
+    qbuf=((2, 8, 1024), F32),
+    qb=((16, 1024), BF),
+    kq=((2, 16, 512), BF),
+    mT=((1024, 256), BF),
+    mS=((512, 256), BF),
+    patT=((192, 512), BF),
+    fill=((1536, 192), BF),
+    fo=((16, 256), F32),
+    att=((768, 512), F32),
+    op=((256, 512), BF),
+    op1=((256, 128), BF),
+    hT=((1024, 512), BF),
+    hrow=((512, 1024), BF),
+    acc=((512, 1024), F32),
+    st0=((512, 1024), BF),
+    nrm=((512, 1024), BF),
+    nrm2=((512, 1024), BF),
+    tr=((1024, 512), BF),
+    q=((512, 256), BF),
+    k=((512, 256), BF),
+    v=((512, 256), BF),
+    attp=((8, 256, 256), F32),
+    mix=((512, 1024), BF),
+    st1=((512, 1024), BF),
+    act=((4, 512, 256), BF),
+    gact=((4, 512, 256), F32),
+    gin=((4, 512, 256), BF),
+    gout=((512, 1024), BF),
+    rsS=((512, 1024), BF),
+    rsR=((4, 128, 1024), BF),
+    gs=((2, 128, 1024), BF),
+    gmS=((4, 128, 256), BF),
+    gm=((512, 256), BF),
+    ga=((512, 256), BF),
+    gb=((512, 256), BF),
+    gq=((3, 512, 256), BF),
+    CR=((13, 512, 256), BF),
+    RC=((2, 4, 512, 256), BF),
+    RA=((4, 512, 256), BF),
+    RB=((4, 512, 256), BF),
+    FR=((4, 512, 256), BF),
+    outR=((4, 512, 256), BF),
+    gh=((128, 1024), BF),
+    ghT=((1024, 128), BF),
+    gpT=((192, 128), F32),
+    gsc=((768, 128), F32),
+    small=((16, 1024), F32),
+    pixS=((4, 48, 128), BF),
+    pixR=((4, 48, 128), BF),
+    gall=((256, 1024), BF),
+    fin=((256, 1024), BF),
+    fromc=((128, 1024), BF),
+    fromp=((4, 32, 1024), BF),
+    fromz=((4, 32, 1024), BF),
+    fc=((2, 16, 256), F32),
+    fp=((4, 16, 256), F32),
+    fz=((4, 16, 256), F32),
+    gqv=((16, 1024), BF),
+    qx=((2, 8, 1024), F32),
+    gaq=((2, 8, 512), F32),
+)
+
+SEMS = dict(
+    rW=(4, 4, 2),
+    rF=(3, 4, 2),
+    sMsg=(4,),
+    sOwn=(4, 2),
+    sFwd=(4, 4, 2),
+    sFx=(3, 3),
+    sFc=(3, 4),
+    rQ=(2,),
+    sQ=(2,),
+    rK=(2,),
+    sK=(16,),
+    rMx=(1,),
+    sMx=(1,),
+    rM=(4, 2),
+    sMa=(4,),
+    sMz=(3,),
+    sMp=(3,),
+    sMc=(4,),
+    sMix=(3,),
+    rMix=(4,),
+    sOut=(4,),
+    rOut=(4,),
+    sR=(2, 4),
+    rR=(2, 4),
+    sG=(3, 4),
+    rG=(3, 4),
+    sC=(4, 4),
+    rC=(4, 4),
+    sZ=(4, 4),
+    rRC=(2, 4),
+    rRA=(4,),
+    rRB=(4,),
+    sFin=(4,),
+    rFin=(4,),
+    sP=(4,),
+    rP=(4,),
+    sAll=(14,),
+    rAll=(14,),
+    sFo=(8,),
+    rFo=(12,),
+    sGq=(18,),
+    rGq=(2,),
+    sGa=(16,),
+    rGa=(2,),
+)
+NAMES = list(SCRATCH) + list(SEMS)
+
+
+class Refs:
+    pass
+
+
+def block_kernel(
+    pat,
+    lead,
+    lens,
+    cot,
+    bank,
+    patch,
+    patch_b,
+    var_emb,
+    agg_query,
+    agg_bias,
+    lead_embed,
+    norm_gain,
+    norm_bias,
+    attn_bias,
+    fc1,
+    fc2,
+    out,
+    gpix,
+    gbank,
+    gtab,
+    sums,
+    rows_out,
+    *scratch,
+):
+    R = Refs()
+    for name, ref in zip(NAMES, scratch):
+        setattr(R, name, ref)
+    here = Place()
+    s, z, c = here.s, here.z, here.c
+    dev = here.dev
+    outer = here.outer
+    inner = jnp.logical_not(outer)
+    sib = dev(s, z, 1 - c)
+    is_row = (s >= 2) & (z >= 2)
+    peers = [s ^ 1, s ^ 2, s ^ 3]
+    layers = [z ^ 1, z ^ 2, z ^ 3]
+    others = [(s ^ i, z ^ k) for k in range(4) for i in range(4) if (i, k) != (0, 0)]
+    vec, table = R.vec, R.table
+    when = pl.when
+    no = jnp.logical_not
+
+    barrier([dev(p, k, c) for p, k in others] + [dev(p, z, 1 - c) for p in peers] + [sib])
+
+    first_owner = (s == 0) & (z == 0)
+    key_owner = (s == 0) & (z == 1)
+    value_owner = (s == 0) & (z == 2)
+
+    late = value_owner
+    used = no((s == 0) & (z < 3))
+
+    @when(no(is_row) & (used | late))
+    def _():
+        for p in range(4):
+            R.msgs[p] = bank[:, p * 256 : (p + 1) * 256]
+
+    @when(is_row)
+    def _():
+        for m in range(4):
+            q, h = m // 2, m % 2
+            for n in range(2):
+                lo = (2 * h + n) * 256
+                R.msgs[m, n * 256 : (n + 1) * 256, :] = bank[q * 256 : (q + 1) * 256, lo : lo + 256]
+
+    def message(m):
+        tp = jnp.where(is_row, 2 * c + m // 2, m)
+        tc = jnp.where(is_row, m % 2, c)
+        return tp, tc, (tp == s) & (tc == c)
+
+    def scatter(cond):
+        for m in range(4):
+            tp, tc, own = message(m)
+
+            @when(cond & own)
+            def _():
+                pltpu.make_async_copy(R.msgs.at[m], R.W.at[z, s, c], R.rW.at[z, s, c]).start()
+
+            @when(cond & no(own))
+            def _():
+                remote(R.msgs.at[m], R.W.at[z, s, tc], R.sMsg.at[m], R.rW.at[z, s, tc], dev(tp, z, tc)).start()
+
+    scatter(used)
+
+    vec[0:3, :] = agg_bias[...].astype(F32)
+    vec[3:5, :] = lead_embed[...].astype(F32)
+    vec[5:7, :] = norm_gain[...].astype(F32)
+    vec[7:9, :] = norm_bias[...].astype(F32)
+    vec[9:12, :] = attn_bias[...].astype(F32)
+    vec[12:16, :] = fc1[...].astype(F32)
+    vec[16:17, :] = fc2[...].astype(F32)
+    vec[17:18, :] = agg_query[...].astype(F32)
+
+    @when(first_owner)
+    def _():
+        part = jnp.broadcast_to(vec[17:18, at(c * 512, 512, 512)].astype(BF), (16, 512))
+        R.qbuf[0] = mm(part, bank[...])[0:8]
+        remote(R.qbuf.at[0], R.qbuf.at[1], R.sQ.at[0], R.rQ.at[0], sib).start()
+
+    perm = jnp.where(
+        (iota((192, 192), 0) // 48 == iota((192, 192), 1) % 4) & (iota((192, 192), 0) % 48 == iota((192, 192), 1) // 4),
+        1.0,
+        0.0,
+    ).astype(BF)
+    for i in range(4):
+        cols = slice(i * 256, (i + 1) * 256)
+        table[0:192, cols] = mm(perm, patch[:, cols]).astype(BF)
+    table[192:240, :] = (patch_b[...].astype(F32) + var_emb[...].astype(F32)).astype(BF)
+    table[240:256, :] = jnp.zeros((16, 1024), BF)
+
+    other_rows = at((1 - c) * 512, 512, 512)
+    half_rows = at(c * 512, 512, 512)
+
+    @when(value_owner)
+    def _():
+        for i in range(4):
+            R.tabT[i * 256 : (i + 1) * 256, :] = table[:, i * 256 : (i + 1) * 256].T
+        for h in range(2):
+            R.gact[h] = mm_tn(bank[:, h * 512 : (h + 1) * 512], R.tabT[half_rows, :])
+        remote(R.gact.at[1 - c], R.gact.at[2], R.sMx.at[0], R.rMx.at[0], sib).start()
+
+    @when(first_owner)
+    def _():
+        arrived(R.qbuf.at[1], R.rQ.at[0])
+        total = R.qbuf[0] + R.qbuf[1] + vec[0:1, :]
+        total = total.astype(BF)
+        R.qb[...] = jnp.concatenate([total, total], axis=0)
+        remote(R.qb, R.qb, R.sQ.at[1], R.rQ.at[1], dev(0, 1, c)).start()
+
+    def piece_of(p, h):
+        return R.mT.at[at(p * 256 + h * 128, 128, 128), :]
+
+    def my_piece(m):
+        return R.mS.at[(m // 2) * 256 + (m % 2) * 128 : (m // 2) * 256 + (m % 2) * 128 + 128, :]
+
+    @when(value_owner)
+    def _():
+        arrived(R.gact.at[2], R.rMx.at[0])
+        sent(R.gact.at[2], R.sMx.at[0])
+        bias = jnp.broadcast_to(vec[1:2, half_rows], (8, 512)).T[:, 0:1]
+        total = R.gact[c] + R.gact[2]
+        R.mS[...] = jnp.where(iota((1, 256), 1) == 240, bias, total).astype(BF)
+        for m in range(4):
+            q, h = m // 2, m % 2
+            tp = 2 * c + q
+            own = (tp == s) & (c == h)
+
+            @when(own)
+            def _():
+                pltpu.make_async_copy(my_piece(m), piece_of(tp, h), R.rM.at[tp, h]).start()
+
+            @when(no(own))
+            def _():
+                remote(my_piece(m), piece_of(tp, h), R.sMa.at[m], R.rM.at[tp, h], dev(tp, z, h)).start()
+
+    @when(key_owner)
+    def _():
+        arrived(R.qb, R.rQ.at[1])
+        masked = jnp.where(iota((16, 1024), 1) // HEAD == iota((16, 1024), 0), R.qb[...].astype(F32), 0.0).astype(BF)
+        R.kq[c] = mm_nt(masked, bank[...]).astype(BF)
+        for i, (p, k) in enumerate(others):
+            remote(R.kq.at[c], R.kq.at[c], R.sK.at[i], R.rK.at[c], dev(p, k, c)).start()
+
+    def at_least(zz, b):
+        return zz == 3 if b == 0 else zz >= 0
+
+    def full_of(zz, b):
+        if b == 0:
+            return True, zz - 2
+        if b == 1:
+            return zz == 3, 2
+        return None, None
+
+    def spread(zz, b):
+        block = R.W.at[zz, b, c]
+        whole, f = full_of(zz, b)
+
+        def to_sibling():
+            remote(block, block, R.sFwd.at[zz, b, 0], R.rW.at[zz, b, c], sib).start()
+
+        def to_layer():
+            pltpu.make_async_copy(block, R.WF.at[f, s, c], R.rF.at[f, s, c]).start()
+            for i, p in enumerate(peers):
+                remote(block, R.WF.at[f, s, c], R.sFx.at[f, i], R.rF.at[f, s, c], dev(p, z, c)).start()
+
+        if whole is None:
+            to_sibling()
+        elif whole is True:
+            to_layer()
+        else:
+            when(no(whole))(to_sibling)
+            when(whole)(to_layer)
+
+    def near(cond, b):
+        block = R.W.at[z, b, c]
+
+        @when(cond)
+        def _():
+            remote(block, block, R.sOwn.at[b, 0], R.rW.at[z, b, c], dev(s, z ^ 1, c)).start()
+
+    def step(cond, b, side=True, hold=False):
+        block = R.W.at[z, b, c]
+
+        @when(cond)
+        def _():
+            arrived(block, R.rW.at[z, b, c])
+
+        @when(cond & outer)
+        def _():
+            remote(block, block, R.sOwn.at[b, 1], R.rW.at[z, b, c], dev(s, z ^ 2, c)).start()
+            remote(block, block, R.sOwn.at[b, 0], R.rW.at[z, b, c], dev(s, z ^ 1, c)).start()
+
+        if not hold:
+            near(cond & inner, b)
+
+        @when(cond & inner)
+        def _():
+            remote(block, block, R.sOwn.at[b, 1], R.rW.at[z, b, c], dev(s, z ^ 3, c)).start()
+
+        if side:
+
+            @when(cond)
+            def _():
+                spread(z, b)
+
+    def foreign(zz, b, cond=True):
+        block = R.W.at[zz, b, c]
+
+        @when(cond & (z != zz))
+        def _():
+            arrived(block, R.rW.at[zz, b, c])
+
+        @when(cond & (z != zz) & inner & (z ^ 1 != zz))
+        def _():
+            remote(block, block, R.sFwd.at[zz, b, 1], R.rW.at[zz, b, c], dev(s, z ^ 1, c)).start()
+
+        @when(cond & (z != zz))
+        def _():
+            spread(zz, b)
+
+    always = z >= 0
+    top = z == 3
+    @when(z == 2)
+    def _():
+        arrived(piece_of(s, c), R.rM.at[s, c])
+        for i, zz in enumerate(layers):
+            remote(piece_of(s, c), piece_of(s, c), R.sMz.at[i], R.rM.at[s, c], dev(s, zz, c)).start()
+        for i, p in enumerate(peers):
+            remote(piece_of(s, c), piece_of(s, c), R.sMp.at[i], R.rM.at[s, c], dev(p, z, c)).start()
+
+    step(top & (s == 0), 0, False)
+    step(no(top) & (s == 1), 1)
+    for b in (2, 3):
+        step(s == b, b)
+
+    tcol = iota((GROUP, 1), 0).astype(F32)
+    trow = iota((1, GROUP), 1).astype(F32)
+    start_col = jnp.zeros((GROUP, 1), F32)
+    seg_col = jnp.zeros((GROUP, 1), F32)
+    seg_row = jnp.zeros((1, GROUP), F32)
+    end = jnp.float32(0.0)
+    for i in range(4):
+        end = end + lens[0, i].astype(F32)
+        past = tcol >= end
+        seg_col = seg_col + jnp.where(past, 1.0, 0.0)
+        seg_row = seg_row + jnp.where(trow >= end, 1.0, 0.0)
+        start_col = jnp.maximum(start_col, jnp.where(past, end, 0.0))
+    place_short = tcol - start_col
+    valid = seg_col < 3.5
+    lead_short = lead[0, 0]
+    lead_long = lead[1, 0]
+    freq = jnp.exp(-math.log(10000.0) * 2.0 * iota((1, 512), 1).astype(F32) / D)
+
+    def positions(g):
+        place = place_short if g == 0 else tcol
+        lead_g = lead_short if g == 0 else lead_long
+        base = lead_g * vec[3:4, :] + vec[4:5, :] + vec[2:3, :]
+        angle = place * freq
+        R.acc[g * GROUP : (g + 1) * GROUP, 0:512] = jnp.sin(angle) + base[:, 0:512]
+        R.acc[g * GROUP : (g + 1) * GROUP, 512:1024] = jnp.cos(angle) + base[:, 512:1024]
+
+    positions(0)
+    step(top & (s != 0), 0, False)
+    step(no(top) & (s != 1), 1)
+    step(top, 1, False)
+
+    positions(1)
+
+    gout = R.gout
+    gout[0:GROUP, :] = jnp.where(valid, cot[0:GROUP, :].astype(F32), 0.0).astype(BF)
+    gout[GROUP:ROWS, :] = cot[GROUP:ROWS, :]
+
+    @when(no(key_owner))
+    def _():
+        arrived(R.kq.at[c], R.rK.at[c])
+
+    remote(R.kq.at[c], R.kq.at[c], R.sK.at[15], R.rK.at[c], sib).start()
+    R.patT[...] = mm_nt(perm, pat[...]).astype(BF)
+
+    @when(z != 2)
+    def _():
+        arrived(piece_of(s, c), R.rM.at[s, c])
+        for i, p in enumerate(peers):
+            remote(piece_of(s, c), piece_of(s, c), R.sMp.at[i], R.rM.at[s, c], dev(p, z, c)).start()
+
+    @when(top)
+    def _():
+        spread(3, 0)
+
+    for b in (2, 3):
+        step(s != b, b, hold=True)
+    scatter(late)
+
+    arrived(R.kq.at[1 - c], R.rK.at[1 - c])
+    kq_full = jnp.concatenate([R.kq[0], R.kq[1]], axis=1)
+    R.fo[...] = mm_nt(kq_full, table[...])
+
+    def fill_head(h):
+        row = R.fo[pl.ds(h, 1), 0:192]
+        value = jnp.where(iota((48, 192), 1) % 48 == iota((48, 192), 0), row, 0.0)
+        high = value.astype(BF)
+        R.fill[at(h * 48, 48, 16), :] = high
+        R.fill[at(768 + h * 48, 48, 16), :] = (value - high.astype(F32)).astype(BF)
+
+    loop(HEADS, fill_head)
+
+    def score_part(i):
+        lo = i * 256
+        R.att[at(lo, 256, 256), :] = mm(R.fill[at(lo, 256, 256), :], R.patT[...]) + mm(
+            R.fill[at(768 + lo, 256, 256), :], R.patT[...]
+        )
+
+    loop(3, score_part)
+
+    foreign(3, 0)
+
+    for i, p in enumerate([s] + peers):
+        if i > 0:
+            arrived(piece_of(p, c), R.rM.at[p, c])
+        remote(piece_of(p, c), piece_of(p, c), R.sMc.at[p], R.rM.at[p, c], sib).start()
+
+    for p in range(4):
+        arrived(piece_of(p, 1 - c), R.rM.at[p, 1 - c])
+
+    for zz in range(3):
+        foreign(zz, 1, inner)
+    for b in (2, 3):
+        near(inner & (s != b), b)
+    R.op[240:256, :] = jnp.where(iota((16, 512), 0) == 0, 1.0, 0.0).astype(BF)
+    r48 = iota((48, 256), 0)
+    c48 = iota((48, 256), 1)
+
+    def weights_of(op, low, cols):
+        lowf = low.astype(F32)
+        for p in range(4):
+            op[p * 48 : (p + 1) * 48, :] = (lowf * R.patT[p * 48 : (p + 1) * 48, cols].astype(F32)).astype(BF)
+        op[192:240, :] = low
+
+    def embed_head(h):
+        offset = jnp.sum(jnp.where(c48 == r48 + 192, R.fo[pl.ds(h, 1), :], 0.0), axis=1, keepdims=True)
+        rows = at(h * 48, 48, 16)
+        scores = (R.att[rows, :] + offset) * (1.0 / math.sqrt(HEAD))
+        peak = jnp.max(scores, axis=0, keepdims=True)
+        e = jnp.exp(scores - peak)
+        prob = e / jnp.sum(e, axis=0, keepdims=True)
+        R.att[rows, :] = prob
+        weights_of(R.op, prob.astype(BF), slice(None))
+        hrows = at(h * 64, 64, 64)
+        R.hT[hrows, :] = mm(R.mT[hrows, :], R.op[...]).astype(BF)
+
+    loop(HEADS, embed_head)
+
+    def pass_on(f):
+        for p in [s] + peers:
+            block = R.WF.at[f, p, c]
+            arrived(block, R.rF.at[f, p, c])
+            remote(block, block, R.sFc.at[f, p], R.rF.at[f, p, c], sib).start()
+
+    def wait_whole(f):
+        for p in range(4):
+            arrived(R.WF.at[f, p, 1 - c], R.rF.at[f, p, 1 - c])
+
+    pass_on(1)
+
+    def turn_tile(i):
+        rows = at(i * 256, 256, 256)
+        R.hrow[:, rows] = R.hT[rows, :].T
+
+    loop(4, turn_tile)
+    for zz in range(3):
+        foreign(zz, 1, outer)
+    foreign(3, 1, inner)
+
+    @when(top)
+    def _():
+        spread(3, 1)
+
+    foreign(z ^ 3, 2, inner)
+    wait_whole(1)
+
+    def stream0_part(i):
+        g = lax.div(i, 4)
+        n = lax.rem(i, 4)
+        rows = at(g * 256, 256, 256)
+        cols = at(n * 256, 256, 256)
+        value = mm(R.hrow[rows, 0:512], R.WF[1, n, 0]) + mm(R.hrow[rows, 512:1024], R.WF[1, n, 1])
+        R.st0[rows, cols] = (value + R.acc[rows, cols]).astype(BF)
+
+    loop(8, stream0_part)
+
+    def norm_into(src, dst, which):
+        def part(i):
+            rows = at(i * 64, 64, 64)
+            dst[rows, :] = normed_rows(
+                src[rows, :].astype(F32), vec[5 + which : 6 + which, :], vec[7 + which : 8 + which, :]
+            ).astype(BF)
+
+        loop(8, part)
+
+    norm_into(R.st0, R.nrm, 0)
+    foreign(z ^ 3, 3, inner)
+
+    foreign(3, 1, outer)
+
+    own_cols = at(s * 256, 256, 256)
+    own_rows = at(s * OWN, OWN, OWN)
+
+    def wait_half(zz, b):
+        arrived(R.W.at[zz, b, 1 - c], R.rW.at[zz, b, 1 - c])
+
+    def project(zz, dst, bias):
+        wait_half(zz, 1)
+        weight = R.W[zz, 1].reshape(1024, 256)
+        for g in range(2):
+            rows = slice(g * 256, (g + 1) * 256)
+            value = mm(R.nrm[rows, :], weight)
+            if bias is not None:
+                value = value + vec[bias : bias + 1, own_cols]
+            dst[rows, :] = value.astype(BF)
+
+    project(0, R.q, 9)
+    project(1, R.k, None)
+    project(2, R.v, 10)
+
+    lane_head = iota((1, 256), 1) // HEAD
+
+    def only(hh, x):
+        return jnp.where(lane_head == hh, x.astype(F32), 0.0).astype(BF)
+
+    allowed = seg_col == seg_row
+
+    def attend(g):
+        rows = slice(g * 256, (g + 1) * 256)
+        total = jnp.zeros((256, 256), F32)
+        for hh in range(4):
+            scores = mm_nt(R.q[rows, :], only(hh, R.k[rows, :])) * (1.0 / math.sqrt(HEAD))
+            if g == 0:
+                scores = jnp.where(allowed, scores, -1e30)
+            e = jnp.exp(scores - jnp.max(scores, axis=1, keepdims=True))
+            prob = e / jnp.sum(e, axis=1, keepdims=True)
+            R.attp[g * 4 + hh] = prob
+            total = total + mm(prob.astype(BF), only(hh, R.v[rows, :]))
+        R.mix[rows, own_cols] = total.astype(BF)
+
+    attend(0)
+    attend(1)
+    mine = R.mix.at[:, own_cols]
+    for i, p in enumerate(peers):
+        remote(mine, mine, R.sMix.at[i], R.rMix.at[s], dev(p, z, c)).start()
+
+    step(z == 2, 0)
+    for b in (2, 3):
+        foreign(z ^ 2, b, inner)
+    pass_on(2)
+    for b in (2, 3):
+        for k in (1, 2, 3):
+            foreign(z ^ k, b, outer if k > 1 else True)
+
+    def feed_out_grad(b):
+        def part(g):
+            rows = at(g * 256, 256, 256)
+            block = R.W.at[2 + b % 2, 2 + b // 2]
+            total = jnp.zeros((256, 256), F32)
+            for n in range(4):
+                tile = block[n // 2, (n % 2) * 256 : (n % 2 + 1) * 256, :]
+                total = total + mm_nt(gout[rows, n * 256 : (n + 1) * 256], tile)
+            R.gact[b, rows, :] = total
+
+        loop(2, part)
+
+    wait_half(2, 2)
+    feed_out_grad(0)
+    wait_half(3, 2)
+    feed_out_grad(1)
+    wait_whole(2)
+    for p in peers:
+        arrived(R.mix.at[:, at(p * 256, 256, 256)], R.rMix.at[p])
+    foreign(2, 0)
+
+    def stream1_part(i):
+        g = lax.div(i, 4)
+        n = lax.rem(i, 4)
+        rows = at(g * 256, 256, 256)
+        cols = at(n * 256, 256, 256)
+        value = mm(R.mix[rows, 0:512], R.WF[2, n, 0]) + mm(R.mix[rows, 512:1024], R.WF[2, n, 1])
+        value = value + vec[11:12, cols] + R.st0[rows, cols].astype(F32)
+        R.st1[rows, cols] = value.astype(BF)
+
+    loop(8, stream1_part)
+    norm_into(R.st1, R.nrm2, 1)
+    wait_half(2, 3)
+    feed_out_grad(2)
+    wait_half(3, 3)
+    feed_out_grad(3)
+    for b in (2, 3):
+        for zz in (0, 1):
+            wait_half(zz, b)
+
+    def feed_in(i):
+        b = lax.div(i, 2)
+        g = lax.rem(i, 2)
+        rows = at(g * 256, 256, 256)
+        bias = vec[pl.ds(12 + b, 1), own_cols]
+        weight = R.W[lax.rem(b, 2), 2 + lax.div(b, 2)].reshape(1024, 256)
+        x = mm(R.nrm2[rows, :], weight) + bias
+        half_cdf = 0.5 + 0.5 * lax.erf(x * math.sqrt(0.5))
+        R.act[b, rows, :] = (x * half_cdf).astype(BF)
+        slope = half_cdf + x * (jnp.exp(-0.5 * x * x) * (1.0 / math.sqrt(2.0 * math.pi)))
+        R.gin[b, rows, :] = (R.gact[b, rows, :] * slope).astype(BF)
+
+    loop(8, feed_in)
+
+    def reduce_rows(phase, make):
+        for i, p in enumerate(peers):
+            make(p)
+            block = R.rsS.at[at(p * OWN, OWN, OWN), :]
+            remote(block, R.rsR.at[s], R.sR.at[phase, i], R.rR.at[phase, s], dev(p, z, c)).start()
+        make(s)
+
+    def reduced(phase):
+        total = R.rsS[own_rows, :].astype(F32)
+        for p in peers:
+            arrived(R.rsR.at[p], R.rR.at[phase, p])
+            total = total + R.rsR[p].astype(F32)
+        return total
+
+    def feed_norm(p):
+        rows = at(p * OWN, OWN, OWN)
+        total = jnp.zeros((OWN, 1024), F32)
+        for b in range(4):
+            total = total + mm_nt(R.gin[b, rows, :], R.W[b % 2, 2 + b // 2].reshape(1024, 256))
+        R.rsS[rows, :] = total.astype(BF)
+
+    reduce_rows(0, feed_norm)
+
+    def drain_own(cond, b):
+        @when(cond)
+        def _():
+            for i in range(2):
+                sent(R.msgs.at[0], R.sOwn.at[b, i])
+
+    def drain_spread(zz, b):
+        whole, f = full_of(zz, b)
+
+        def side():
+            sent(R.msgs.at[0], R.sFwd.at[zz, b, 0])
+
+        def layer():
+            for i in range(3):
+                sent(R.msgs.at[0], R.sFx.at[f, i])
+
+        if whole is None or zz < 3:
+            (layer if whole is True else side)()
+        else:
+            layer()
+
+        @when((z != zz) & inner & (z ^ 1 != zz))
+        def _():
+            sent(R.msgs.at[0], R.sFwd.at[zz, b, 1])
+
+    for b in (2, 3):
+        drain_own(always, b)
+        for zz in range(4):
+            drain_spread(zz, b)
+
+    def transposed(src):
+        def part(i):
+            a = lax.div(i, 2)
+            b = lax.rem(i, 2)
+            R.tr[at(a * 256, 256, 256), at(b * 256, 256, 256)] = src[
+                at(b * 256, 256, 256), at(a * 256, 256, 256)
+            ].T
+
+        loop(8, part)
+
+    def slot(zz, b):
+        return 12 if isinstance(b, int) and b == 0 else (b - 1) * 4 + zz
+
+    def exchange(zz, b):
+        block = R.W.at[zz, b, 1 - c]
+        remote(block, R.CR.at[slot(zz, b)], R.sC.at[zz, b], R.rC.at[zz, b], sib).start()
+
+    def column_gradient(zz, b, left, right):
+        for h in range(2):
+            R.W[zz, b, h] = mm(left[h * 512 : (h + 1) * 512, :], right).astype(BF)
+        exchange(zz, b)
+
+    transposed(R.nrm2)
+
+    def first_gradient(b):
+        column_gradient(lax.rem(b, 2), 2 + lax.div(b, 2), R.tr, R.gin[b])
+
+    loop(4, first_gradient)
+
+    def out_part(i):
+        g = lax.div(i, 4)
+        n = lax.rem(i, 4)
+        rows = at(g * 256, 256, 256)
+        total = jnp.zeros((256, 256), F32)
+        for b in range(4):
+            tile = R.W[2 + b % 2, 2 + b // 2, lax.div(n, 2), at(lax.rem(n, 2) * 256, 256, 256), :]
+            total = total + mm(R.act[b, rows, :], tile)
+        R.hrow[rows, at(n * 256, 256, 256)] = total.astype(BF)
+
+    loop(8, out_part)
+
+    def second_gradient(b):
+        zz = 2 + lax.rem(b, 2)
+        bb = 2 + lax.div(b, 2)
+        for n in range(4):
+            tile = mm_tn(R.act[b], gout[:, n * 256 : (n + 1) * 256])
+            R.W[zz, bb, n // 2, (n % 2) * 256 : (n % 2 + 1) * 256, :] = tile.astype(BF)
+        exchange(zz, bb)
+
+    loop(4, second_gradient)
+
+    def summed(zz, b):
+        arrived(R.CR.at[slot(zz, b)], R.rC.at[zz, b])
+        sent(R.CR.at[slot(zz, b)], R.sC.at[zz, b])
+        R.W[zz, b, c] = (R.W[zz, b, c].astype(F32) + R.CR[slot(zz, b)].astype(F32)).astype(BF)
+
+    def first_send(k, b, cond=True):
+        zz = z ^ k
+        block = R.W.at[zz, b, c]
+
+        @when(cond)
+        def _():
+            summed(zz, b)
+            if k == 1:
+                remote(block, R.RA.at[b], R.sZ.at[zz, b], R.rRA.at[b], dev(s, z ^ 1, c)).start()
+
+        if k > 1:
+
+            @when(cond & outer)
+            def _():
+                remote(block, R.RC.at[3 - k, b], R.sZ.at[zz, b], R.rRC.at[3 - k, b], dev(s, z ^ 1, c)).start()
+
+    def second_send(zz, b):
+        block = R.W.at[zz, b, c]
+
+        @when(inner & (z != zz) & (z ^ 1 != zz))
+        def _():
+            k = (z ^ zz) - 2
+            arrived(R.RC.at[k, b], R.rRC.at[k, b])
+            R.W[zz, b, c] = (R.W[zz, b, c].astype(F32) + R.RC[k, b].astype(F32)).astype(BF)
+            remote(block, R.RB.at[b], R.sZ.at[zz, b], R.rRB.at[b], dev(s, zz, c)).start()
+
+    def owner_of(b):
+        row = (z >= 2) if b >= 2 else (z < 0)
+        tc = jnp.where(row, lax.div(s, 2), c)
+        m = jnp.where(row, lax.rem(s, 2) * 2 + c, s)
+        return tc, m, (s == b) & (tc == c)
+
+    def last_send(cond, b):
+        tc, m, own = owner_of(b)
+        block = R.W.at[z, b, c]
+
+        @when(cond)
+        def _():
+            arrived(R.RA.at[b], R.rRA.at[b])
+            arrived(R.RB.at[b], R.rRB.at[b])
+            R.W[z, b, c] = (R.W[z, b, c].astype(F32) + R.RA[b].astype(F32) + R.RB[b].astype(F32)).astype(BF)
+
+        @when(cond & own)
+        def _():
+            pltpu.make_async_copy(block, R.FR.at[m], R.rFin.at[m]).start()
+
+        @when(cond & no(own))
+        def _():
+            remote(block, R.FR.at[m], R.sFin.at[b], R.rFin.at[m], dev(b, z, tc)).start()
+
+    for k in (2, 3, 1, 0):
+        for b in (2, 3):
+            first_send(k, b)
+
+    R.small[...] = jnp.zeros((16, 1024), F32)
+    for b in range(4):
+        R.small[10 + b : 11 + b, own_cols] = column_sum(R.gin[b].astype(F32))
+    R.small[14:15, :] = column_sum(gout[own_rows, :].astype(F32))
+
+    g2 = reduced(0)
+    gx, gw, gb = norm_back(R.st1[own_rows, :].astype(F32), g2, vec[6:7, :])
+    R.small[4:5, :] = gw
+    R.small[6:7, :] = gb
+    gs1_own = (gout[own_rows, :].astype(F32) + gx).astype(BF)
+    R.small[9:10, :] = column_sum(gs1_own.astype(F32))
+    R.gs[0] = gs1_own
+
+    def mixed_grad(p):
+        total = jnp.zeros((OWN, 256), F32)
+        for n in range(4):
+            tile = R.WF[2, n, lax.div(p, 2), at(lax.rem(p, 2) * 256, 256, 256), :]
+            total = total + mm_nt(R.gs[0, :, n * 256 : (n + 1) * 256], tile)
+        return total.astype(BF)
+
+    def swap(phase, src_of, dst):
+        for i, p in enumerate(peers):
+            remote(src_of(p), dst.at[own_rows, :], R.sG.at[phase, i], R.rG.at[phase, s], dev(p, z, c)).start()
+
+    def swapped(phase, dst):
+        for p in peers:
+            arrived(dst.at[at(p * OWN, OWN, OWN), :], R.rG.at[phase, p])
+
+    for i, p in enumerate(peers):
+        R.gmS[i] = mixed_grad(p)
+        remote(R.gmS.at[i], R.gm.at[own_rows, :], R.sG.at[0, i], R.rG.at[0, s], dev(p, z, c)).start()
+    R.gm[own_rows, :] = mixed_grad(s)
+    swap(1, lambda p: R.gs.at[0, :, at(p * 256, 256, 256)], R.ga)
+    R.ga[own_rows, :] = R.gs[0, :, own_cols]
+
+    def send_out(i):
+        p = peers[i]
+        block = R.hrow.at[:, at(p * 256, 256, 256)]
+        remote(block, R.outR.at[s], R.sOut.at[i], R.rOut.at[s], dev(p, z, c)).start()
+
+    send_out(0)
+    send_out(1)
+    pass_on(0)
+
+    swapped(0, R.gm)
+
+    def attend_back(g):
+        rows = at(g * 256, 256, 256)
+        qg, kg, vg, gmg = R.q[rows, :], R.k[rows, :], R.v[rows, :], R.gm[rows, :]
+        zero = jnp.zeros((256, 256), F32)
+        tq, tk, tv = zero, zero, zero
+        for hh in range(4):
+            prob = R.attp[g * 4 + hh]
+            gmh = only(hh, gmg)
+            dprob = mm_nt(gmh, vg)
+            tv = tv + mm_tn(prob.astype(BF), gmh)
+            ds = (prob * (dprob - jnp.sum(prob * dprob, axis=1, keepdims=True))).astype(BF)
+            tq = tq + mm(ds, only(hh, kg))
+            tk = tk + mm_tn(ds, only(hh, qg))
+        scale = 1.0 / math.sqrt(HEAD)
+        R.gq[0, rows, :] = (tq * scale).astype(BF)
+        R.gq[1, rows, :] = (tk * scale).astype(BF)
+        R.gq[2, rows, :] = tv.astype(BF)
+
+    loop(2, attend_back)
+
+    for i in range(3):
+        sent(R.rsR.at[0], R.sR.at[0, i])
+
+    def attend_norm(p):
+        rows = at(p * OWN, OWN, OWN)
+        total = jnp.zeros((OWN, 1024), F32)
+        for i in range(3):
+            total = total + mm_nt(R.gq[i, rows, :], R.W[i, 1].reshape(1024, 256))
+        R.rsS[rows, :] = total.astype(BF)
+
+    reduce_rows(1, attend_norm)
+
+    transposed(R.nrm)
+    drain_own(always, 1)
+    drain_own(top, 0)
+    for zz in range(4):
+        drain_spread(zz, 1)
+    drain_spread(3, 0)
+
+    def attend_gradient(i):
+        column_gradient(i, 1, R.tr, R.gq[i])
+
+    loop(3, attend_gradient)
+    transposed(R.mix)
+    swapped(1, R.ga)
+    column_gradient(3, 1, R.tr, R.ga[...])
+    R.small[7:8, own_cols] = column_sum(R.gq[0].astype(F32))
+    R.small[8:9, own_cols] = column_sum(R.gq[2].astype(F32))
+    for k in (2, 3, 1, 0):
+        first_send(k, 1)
+
+    g1 = reduced(1)
+    gx, gw, gb = norm_back(R.st0[own_rows, :].astype(F32), g1, vec[5:6, :])
+    R.small[3:4, :] = gw
+    R.small[5:6, :] = gb
+    gs0_own = (R.gs[0].astype(F32) + gx).astype(BF)
+    gs0_sum = column_sum(gs0_own.astype(F32))
+    R.small[1:2, :] = gs0_sum
+    R.small[2:3, :] = jnp.where(s < 2, lead_short, lead_long) * gs0_sum
+    R.gs[1] = gs0_own
+    swap(2, lambda p: R.gs.at[1, :, at(p * 256, 256, 256)], R.gb)
+    R.gb[own_rows, :] = R.gs[1, :, own_cols]
+    def heads_grad(i):
+        rows = at(lax.rem(i, 2) * 256, 256, 256)
+        total = jnp.zeros((256, OWN), F32)
+        for n in range(4):
+            total = total + mm_nt(R.WF[1, n, lax.div(i, 2), rows, :], R.gs[1, :, n * 256 : (n + 1) * 256])
+        block = at(i * 256, 256, 256)
+        R.ghT[block, :] = total.astype(BF)
+        R.gh[:, block] = total.astype(BF).T
+
+    loop(4, heads_grad)
+    R.G = R.acc.at[0:256, :]
+    R.gpT[...] = jnp.zeros((192, OWN), F32)
+    R.G[...] = jnp.zeros((256, 1024), F32)
+    R.op1[240:256, :] = jnp.where(iota((16, OWN), 0) == 0, 1.0, 0.0).astype(BF)
+
+    def embed_back(h):
+        rows = at(h * 48, 48, 16)
+        prob = R.att[rows, own_rows]
+        low = prob.astype(BF)
+        lowf = low.astype(F32)
+        weights_of(R.op1, low, own_rows)
+        hrows = at(h * 64, 64, 64)
+        gop = mm_tn(R.mT[hrows, :], R.ghT[hrows, :])
+        cols = at(lax.div(h, 4) * 256, 256, 256)
+        keep = lane_head == lax.rem(h, 4)
+        R.G[:, cols] += jnp.where(keep, mm(R.op1[...], R.gh[:, cols]), 0.0)
+        gatt = gop[192:240, :]
+        for p in range(4):
+            gatt = gatt + gop[p * 48 : (p + 1) * 48, :] * R.patT[p * 48 : (p + 1) * 48, own_rows].astype(F32)
+        R.gsc[rows, :] = prob * (gatt - jnp.sum(prob * gatt, axis=0, keepdims=True)) * (1.0 / math.sqrt(HEAD))
+        for p in range(4):
+            prow = slice(p * 48, (p + 1) * 48)
+            R.gpT[prow, :] += gop[prow, :] * lowf
+
+    loop(HEADS, embed_back)
+
+    gsc = R.gsc[...]
+    gsc_high = gsc.astype(BF)
+    gsc_low = (gsc - gsc_high.astype(F32)).astype(BF)
+    fold = jnp.where(iota((16, 768), 0) == iota((16, 768), 1) // 48, 1.0, 0.0).astype(BF)
+
+    def folded(x, right):
+        x_high = x.astype(BF)
+        x_low = (x - x_high.astype(F32)).astype(BF)
+        return mm(fold, x_high) + mm(fold, x_low)
+
+    ones = jnp.ones((192, OWN), BF)
+    pat_own = R.patT[:, own_rows]
+    same = iota((768, 192), 0) % 48 == iota((768, 192), 1) % 48
+    cross = mm_nt(gsc_high, pat_own) + mm_nt(gsc_low, pat_own)
+    plain = mm_nt(gsc_high, ones) + mm_nt(gsc_low, ones)
+    R.fc[0, :, 0:192] = folded(jnp.where(same, cross, 0.0), None)
+    R.fc[0, :, 192:256] = folded(jnp.where(same, plain, 0.0), None)[:, 0:64] * jnp.where(
+        iota((1, 64), 1) < 48, 1.0, 0.0
+    )
+    remote(R.fc.at[0], R.fc.at[1], R.sFo.at[0], R.rFo.at[0], sib).start()
+
+    R.G[240:256, :] += R.small[...]
+    R.gall[...] = R.G[...].astype(BF)
+    half = at(c * 128, 128, 128)
+    other = at((1 - c) * 128, 128, 128)
+    remote(R.gall.at[other, :], R.fromc, R.sAll.at[0], R.rAll.at[0], sib).start()
+
+    gpt = (R.gpT[...] + mm_tn(R.fill[0:768, :], gsc_high)).astype(BF)
+    for p in range(4):
+        r = iota((48, 192), 0) + p * 48
+        select = jnp.where(iota((48, 192), 1) == (r % 4) * 48 + r // 4, 1.0, 0.0).astype(BF)
+        R.pixS[p] = mm(select, gpt).astype(BF)
+    for i, p in enumerate(peers):
+        remote(R.pixS.at[p], R.pixR.at[s], R.sP.at[i], R.rP.at[s], dev(p, z, c)).start()
+
+    for b in (2, 3):
+        for zz in range(4):
+            second_send(zz, b)
+    arrived(R.fc.at[1], R.rFo.at[0])
+    R.fp[s] = R.fc[0] + R.fc[1]
+    for i, p in enumerate(peers):
+        remote(R.fp.at[s], R.fp.at[s], R.sFo.at[1 + i], R.rFo.at[1 + s], dev(p, z, c)).start()
+
+    arrived(R.fromc, R.rAll.at[0])
+    R.gall[half, :] = (R.gall[half, :].astype(F32) + R.fromc[...].astype(F32)).astype(BF)
+
+    def part_of(p):
+        return at(c * 128 + p * 32, 32, 32)
+
+    for i, p in enumerate(peers):
+        remote(R.gall.at[part_of(p), :], R.fromp.at[s], R.sAll.at[1 + i], R.rAll.at[1 + s], dev(p, z, c)).start()
+
+    swapped(2, R.gb)
+    column_gradient(3, 0, R.hT, R.gb[...])
+
+    for p in peers:
+        arrived(R.fp.at[p], R.rFo.at[1 + p])
+    R.fz[z] = R.fp[0] + R.fp[1] + R.fp[2] + R.fp[3]
+    for i, zz in enumerate(layers):
+        remote(R.fz.at[z], R.fz.at[z], R.sFo.at[4 + i], R.rFo.at[5 + z], dev(s, zz, c)).start()
+
+    total = R.gall[part_of(s), :].astype(F32)
+    for p in peers:
+        arrived(R.fromp.at[p], R.rAll.at[1 + p])
+        total = total + R.fromp[p].astype(F32)
+    R.fromz[z] = total.astype(BF)
+    for i, zz in enumerate(layers):
+        remote(R.fromz.at[z], R.fromz.at[z], R.sAll.at[4 + i], R.rAll.at[5 + z], dev(s, zz, c)).start()
+
+    for zz in range(4):
+        second_send(zz, 1)
+    for k in (2, 3, 1, 0):
+        first_send(k, 0, z ^ k == 3)
+    send_out(2)
+
+    for zz in layers:
+        arrived(R.fz.at[zz], R.rFo.at[5 + zz])
+    fo_grad = (R.fz[0] + R.fz[1]) + (R.fz[2] + R.fz[3])
+    fo_high = fo_grad.astype(BF)
+    fo_low = (fo_grad - fo_high.astype(F32)).astype(BF)
+    gkq = (mm(fo_high, table[...]) + mm(fo_low, table[...])).astype(BF)
+
+    @when(key_owner)
+    def _():
+        diag = iota((16, 1024), 1) // HEAD == iota((16, 1024), 0)
+        own = jnp.where(c == 0, gkq[:, 0:512].astype(F32), gkq[:, 512:1024].astype(F32)).astype(BF)
+        row = column_sum(jnp.where(diag, mm(own, bank[...]), 0.0))
+        R.qx[0] = jnp.broadcast_to(row, (8, 1024))
+        remote(R.qx.at[0], R.qx.at[1], R.sGq.at[15], R.rGq.at[0], sib).start()
+        masked = jnp.where(diag, R.qb[...].astype(F32), 0.0).astype(BF)
+        gbank[...] = mm_tn(own, masked).astype(BF)
+        arrived(R.qx.at[1], R.rGq.at[0])
+        row = (R.qx[0] + R.qx[1]).astype(BF)
+        R.gqv[...] = jnp.concatenate([row, row], axis=0)
+        for i, (p, k) in enumerate(others):
+            remote(R.gqv, R.gqv, R.sGq.at[i], R.rGq.at[1], dev(p, k, c)).start()
+
+    for zz in layers:
+        arrived(R.fromz.at[zz], R.rAll.at[5 + zz])
+    total = R.fromz[0].astype(F32)
+    for zz in range(1, 4):
+        total = total + R.fromz[zz].astype(F32)
+    R.fin[part_of(s), :] = total.astype(BF)
+    for i, p in enumerate(peers):
+        block = R.fin.at[part_of(s), :]
+        remote(block, block, R.sAll.at[7 + i], R.rAll.at[9 + s], dev(p, z, c)).start()
+
+    @when(first_owner)
+    def _():
+        arrived(R.gqv, R.rGq.at[1])
+        R.gaq[c] = mm_nt(R.gqv[...], bank[...])[0:8]
+        for i, (p, k) in enumerate(others):
+            remote(R.gaq.at[c], R.gaq.at[c], R.sGa.at[i], R.rGa.at[c], dev(p, k, c)).start()
+        aq = jnp.where(c == 0, vec[17:18, 0:512], vec[17:18, 512:1024])
+        aq = jnp.where(iota((16, 512), 0) == 0, aq, 0.0).astype(BF)
+        gbank[...] = mm_tn(aq, R.gqv[...]).astype(BF)
+
+    last_send(always, 2)
+    last_send(always, 3)
+
+    for p in peers:
+        arrived(R.fin.at[part_of(p), :], R.rAll.at[9 + p])
+    remote(R.fin.at[half, :], R.fin.at[half, :], R.sAll.at[10], R.rAll.at[13], sib).start()
+
+    second_send(3, 0)
+    last_send(always, 1)
+
+    total = R.hrow[:, own_cols].astype(F32) + R.st1[:, own_cols].astype(F32) + vec[16:17, own_cols]
+    for p in peers:
+        arrived(R.outR.at[p], R.rOut.at[p])
+        total = total + R.outR[p].astype(F32)
+    out[...] = total.astype(BF)
+
+    for i, p in enumerate(peers):
+        arrived(R.pixR.at[p], R.rP.at[p])
+    R.pixR[s] = R.pixS[s]
+    for p in range(4):
+        gpix[p * OWN : (p + 1) * OWN, :] = R.pixR[p].astype(F32).T
+
+    wait_whole(0)
+    arrived(R.fin.at[other, :], R.rAll.at[13])
+    sums[...] = R.fin[240:256, :].astype(F32)
+    kq_wide = jnp.concatenate([kq_full, jnp.zeros((112, 1024), BF)], axis=0)
+    wide = jnp.zeros((112, 256), BF)
+    gfh = jnp.concatenate([fo_high, wide], axis=0)
+    gfl = jnp.concatenate([fo_low, wide], axis=0)
+
+    def table_grad(h):
+        value = jnp.zeros((256, 512), F32)
+        for p in range(4):
+            value = value + mm_nt(R.fin[:, p * 256 : (p + 1) * 256], R.WF[0, p, h])
+        return value
+
+    for h in range(2):
+        cols = slice(h * 512, (h + 1) * 512)
+        gtab[:, cols] = (table_grad(h) + mm_tn(gfh, kq_wide[:, cols]) + mm_tn(gfl, kq_wide[:, cols])).astype(BF)
+
+    @when(value_owner)
+    def _():
+        gbank[...] = mm_tn(table[:, half_rows], R.fin[...]).astype(BF)
+
+    last_send(top, 0)
+
+    @when(no(first_owner))
+    def _():
+        arrived(R.gaq.at[c], R.rGa.at[c])
+
+    @when(no(key_owner | first_owner))
+    def _():
+        arrived(R.gqv, R.rGq.at[1])
+
+    remote(R.gaq.at[c], R.gaq.at[c], R.sGa.at[15], R.rGa.at[c], sib).start()
+    arrived(R.gaq.at[1 - c], R.rGa.at[1 - c])
+    rows_out[0:8, :] = R.gqv[0:8, :].astype(F32)
+    rows_out[8:16, 0:512] = R.gaq[0]
+    rows_out[8:16, 512:1024] = R.gaq[1]
+
+    @when(used)
+    def _():
+        for m in range(4):
+            arrived(R.FR.at[m], R.rFin.at[m])
+
+    @when(used & no(is_row))
+    def _():
+        for m in range(4):
+            gbank[:, m * 256 : (m + 1) * 256] = R.FR[m]
+
+    @when(is_row)
+    def _():
+        for m in range(4):
+            q, h = m // 2, m % 2
+            for n in range(2):
+                lo = (2 * h + n) * 256
+                gbank[q * 256 : (q + 1) * 256, lo : lo + 256] = R.FR[m, n * 256 : (n + 1) * 256, :]
+
+    for m in range(4):
+        tp, tc, own = message(m)
+
+        @when((used | late) & no(own))
+        def _():
+            sent(R.msgs.at[m], R.sMsg.at[m])
+
+        @when(value_owner & no((2 * c + m // 2 == s) & (c == m % 2)))
+        def _():
+            sent(my_piece(m), R.sMa.at[m])
+
+    @when(first_owner)
+    def _():
+        sent(R.qbuf.at[0], R.sQ.at[0])
+        sent(R.qb, R.sQ.at[1])
+        for i in range(15):
+            sent(R.gaq.at[c], R.sGa.at[i])
+
+    @when(key_owner)
+    def _():
+        sent(R.qx.at[0], R.sGq.at[15])
+        for i in range(15):
+            sent(R.kq.at[c], R.sK.at[i])
+            sent(R.gqv, R.sGq.at[i])
+
+    @when(z == 2)
+    def _():
+        for i in range(3):
+            sent(R.mS.at[0:128, :], R.sMz.at[i])
+
+    drain_own(z == 2, 0)
+    drain_spread(2, 0)
+    sent(R.kq.at[c], R.sK.at[15])
+    sent(R.gaq.at[c], R.sGa.at[15])
+    for f in range(3):
+        for p in range(4):
+            sent(R.msgs.at[0], R.sFc.at[f, p])
+    for p in range(4):
+        sent(R.mS.at[0:128, :], R.sMc.at[p])
+    sent(R.fc.at[0], R.sFo.at[0])
+    sent(R.fromc, R.sAll.at[0])
+    sent(R.fromc, R.sAll.at[10])
+    for i in range(3):
+        sent(R.mS.at[0:128, :], R.sMp.at[i])
+        sent(mine, R.sMix.at[i])
+        sent(R.msgs.at[0], R.sOut.at[i])
+        sent(R.rsR.at[0], R.sR.at[1, i])
+        for phase in range(3):
+            sent(R.gmS.at[0], R.sG.at[phase, i])
+        sent(R.pixS.at[0], R.sP.at[i])
+        sent(R.fp.at[0], R.sFo.at[1 + i])
+        sent(R.fp.at[0], R.sFo.at[4 + i])
+        for phase in range(3):
+            sent(R.fromp.at[0], R.sAll.at[1 + 3 * phase + i])
+    for b in range(4):
+        for zz in range(4):
+
+            @when(at_least(jnp.int32(zz), b) & (z != zz) & (always if b > 0 or zz == 3 else z < 0))
+            def _():
+                sent(R.msgs.at[0], R.sZ.at[zz, b])
+
+        tc, m, own = owner_of(b)
+
+        @when((top if b == 0 else always) & no(own))
+        def _():
+            sent(R.msgs.at[0], R.sFin.at[b])
+
+
+VMEM = pl.BlockSpec(memory_space=pltpu.VMEM)
+SMEM = pl.BlockSpec(memory_space=pltpu.SMEM)
+ARG_SHAPES = (
+    [((512, 192), BF), ((2, 1), F32), ((1, 4), jnp.int32), ((512, 1024), BF), ((512, 1024), BF), ((192, 1024), BF)]
+    + [((48, 1024), BF)] * 2
+    + [((n, 1024), BF) for n in (1, 3, 2, 2, 2, 3, 4, 1)]
+)
+
+
+def block_call(*args):
+    shape = jax.ShapeDtypeStruct
+    outs = [
+        shape((512, 256), BF),
+        shape((512, 48), F32),
+        shape((512, 1024), BF),
+        shape((256, 1024), BF),
+        shape((16, 1024), F32),
+        shape((16, 1024), F32),
+    ]
+    return pl.pallas_call(
+        block_kernel,
+        out_shape=outs,
+        in_specs=[VMEM, SMEM, SMEM] + [VMEM] * (len(args) - 3),
+        out_specs=[VMEM] * len(outs),
+        scratch_shapes=[pltpu.VMEM(*v) for v in SCRATCH.values()]
+        + [pltpu.SemaphoreType.DMA(v) for v in SEMS.values()],
+        compiler_params=pltpu.CompilerParams(
+            collective_id=1, has_side_effects=True, vmem_limit_bytes=63 * 2**20
+        ),
+    )(*args)
+
+
+def finish_kernel(
+    out,
+    gpix,
+    gbank,
+    gtab,
+    sums,
+    rows,
+    o_out,
+    o_pix,
+    o_bank,
+    o_patch,
+    o_patch_b,
+    o_var,
+    o_query,
+    o_agg,
+    o_lead,
+    o_gain,
+    o_bias,
+    o_attn,
+    o_fc1,
+    o_fc2,
+):
+    o_out[...] = out[...]
+    o_pix[...] = gpix[...]
+    o_bank[...] = gbank[...].astype(F32)
+    for p in range(PIX):
+        o_patch[:, p, :] = gtab[p * VARS : (p + 1) * VARS, :].astype(F32)
+    o_patch_b[...] = gtab[192:240, :].astype(F32)
+    o_var[...] = gtab[192:240, :].astype(F32)
+    o_query[...] = rows[8:9, :]
+    o_agg[0:1, :] = rows[0:1, :]
+    o_agg[1:3, :] = sums[0:2, :]
+    o_lead[0:1, :] = sums[2:3, :]
+    o_lead[1:2, :] = sums[1:2, :]
+    o_gain[...] = sums[3:5, :]
+    o_bias[...] = sums[5:7, :]
+    o_attn[...] = sums[7:10, :]
+    o_fc1[...] = sums[10:14, :]
+    o_fc2[...] = sums[14:15, :]
+
+
+def finish_call(*args):
+    shape = jax.ShapeDtypeStruct
+    outs = [shape((512, 256), BF), shape((512, 48), F32), shape((512, 1024), F32), shape((48, 4, 1024), F32)]
+    outs += [shape((48, 1024), F32)] * 2 + [shape((n, 1024), F32) for n in (1, 3, 2, 2, 2, 3, 4, 1)]
+    return pl.pallas_call(
+        finish_kernel,
+        out_shape=outs,
+        in_specs=[VMEM] * len(args),
+        out_specs=[VMEM] * len(outs),
+        compiler_params=pltpu.CompilerParams(vmem_limit_bytes=40 * 2**20),
+    )(*args)
+
+
+def on_device_fast(
+    patches,
+    lead_times,
+    short_lengths,
+    cotangent,
+    bank,
+    patch_w,
+    patch_b,
+    var_emb,
+    agg_query,
+    agg_bias,
+    lead_embed,
+    norm_gain,
+    norm_bias,
+    attn_bias,
+    fc1_bias,
+    fc2_bias,
+):
+    parts = block_call(
+        patches.reshape(ROWS, VARS * PIX),
+        lead_times,
+        short_lengths,
+        cotangent.reshape(ROWS, D),
+        bank[0],
+        patch_w.reshape(VARS * PIX, D),
+        patch_b,
+        var_emb,
+        agg_query[None],
+        agg_bias,
+        lead_embed,
+        norm_gain,
+        norm_bias,
+        attn_bias,
+        fc1_bias.reshape(4, D),
+        fc2_bias[None],
+    )
+    o = finish_call(*parts)
+    return (
+        (o[0].reshape(2, GROUP, 256), o[1].reshape(2, GROUP, 48), o[2][None])
+        + tuple(o[3:6])
+        + (o[6][0],)
+        + tuple(o[7:12])
+        + (o[12].reshape(FF), o[13][0])
+    )
+
+
+def specs():
+    ins = (
+        (P(None, "dp", None), P(None, "dp"), P("dp", None), P(None, "dp", None), P("section", "dp", None))
+        + (P(),) * 11
+    )
+    outs = (P(None, "dp", "section"), P(None, "dp", "section"), P("section", "dp", None)) + (P(),) * 11
+    return ins, outs
 
 
 wide_type = jnp.float32
@@ -727,42 +2181,7 @@
 
 
 def solution(mesh):
-    return jax.shard_map(
-        on_device,
-        mesh=mesh,
-        in_specs=(
-            P(None, "dp", None),
-            P(None, "dp"),
-            P("dp", None),
-            P(None, "dp", None),
-            P("section", "dp", None),
-            P(),
-            P(),
-            P(),
-            P(),
-            P(),
-            P(),
-            P(),
-            P(),
-            P(),
-            P(),
-            P(),
-        ),
-        out_specs=(
-            P(None, "dp", "section"),
-            P(None, "dp", "section"),
-            P("section", "dp", None),
-            P(),
-            P(),
-            P(),
-            P(),
-            P(),
-            P(),
-            P(),
-            P(),
-            P(),
-            P(),
-            P(),
-        ),
-        check_vma=False,
-    )
+    ins, outs = specs()
+    small_slice = mesh.shape["section"] == 4 and mesh.shape["dp"] == 8
+    body = on_device_fast if small_slice else on_device
+    return jax.shard_map(body, mesh=mesh, in_specs=ins, out_specs=outs, check_vma=False)

time: 1720 us -> 213 us (0.12)
  waiting for transfers between devices: 599 us -> 0 us
  local copies, waits for them, and re-layouts: 428 us -> 15.9 us
  other arithmetic: 255 us -> 0 us
  Pallas kernels: 0 us -> 193 us
  loops' own time: 185 us -> 0 us
  matrix products: 166 us -> 0 us
  starting transfers between devices: 53.7 us -> 0 us
    psum x2 -> x0, waiting for transfers between devices: 229 us -> none  [on_device(): small_sums = lax.psum(small_total, ('section', 'dp'))]
    pallas_call x0 -> x2, Pallas kernels: none -> 193 us  [the longest x1 191 us: block_call(): pl.pallas_call(block_kernel, out_shape=outs, in_specs=[VMEM, SMEM, SMEM]...]
    another operation x10 -> x0, loops' own time: 185 us -> none  [the longest x5 121 us: on_device(): lax.switch(branch, backward_list, operands)]
    ppermute x12 -> x0, waiting for transfers between devices: 171 us -> none  [from_behind(): return lax.ppermute(array, axis, pairs)]
    dot_general x58 -> x0, matrix products: 166 us -> none  [the longest x4 35.7 us: embed_rows(): jnp.einsum('thd,dhe->the', pooled, weights[2].reshape(D, HEADS, HEAD), pr...]
    convert_element_type x26 -> x0, local copies, waits for them, and re-layouts: 147 us -> none  [the longest x4 91.1 us: embed_rows(): (attend_low.astype(wide_type)[:, :, :, None] * pixels[:, :, None, :]).ast...]
    reduce_scatter x3 -> x0, waiting for transfers between devices: 121 us -> none  [the longest x1 90.8 us: on_device(): lax.psum_scatter(bank_total.astype(jnp.bfloat16), 'dp', scatter_dimension...]
    convert_element_type x42 -> x0, other arithmetic: 91.6 us -> none  [the longest x4 41 us: embed_rows(): (attend_low.astype(wide_type)[:, :, :, None] * pixels[:, :, None, :]).ast...]
  transfers between devices with their start and end apart: 18 -> 0, of which waited for: 17 -> 0; matrix products, arithmetic and copies ran while one was open for 5% -> 0% of each run, Pallas kernels for 0% -> 0%
where the time goes in v2:
time: 213 us; the launch traced here: 210 us
  Pallas kernels  193 us (91%)
  local copies, waits for them, and re-layouts  15.9 us (7%)
    pallas_call x1, Pallas kernels, block_call(): pl.pallas_call(block_kernel, out_shape=outs, in_specs=[VMEM, SMEM, SMEM]...  191 us
    unnamed x16, local copies, waits for them, and re-layouts  10.3 us

profile of v2, /device:TPU:25, one launch (start us, length us, event | category | flops | bytes accessed | tf_op | source)
XLA Modules:
  0.0 209.5 jit_solution(12956479333481305855)
XLA Ops:
  0.6 1.3 copy.31.lead
  1.9 1.3 broadcast_in_dim.9.agg_query
  3.2 1.3 broadcast_in_dim.10.fc2
  4.5 1.3 reshape.52.fc1
  5.8 1.8 copy.30
  7.6 1.8 reshape.51.patch
  9.4 191.0 %shard_map.263 = (bf16[512,256]{1,0:T(8,128)(2,1)}, f32[512,48]{1,0:T(8,128)}, bf16[512,1024]{1,0:T(8,128)(2,1)}, bf16[256,1024]{1,0:T(8,128)(2,1)}, f32[16,1024]{1,0:T(8,128)}, /*index=5*/f32[16,1024]{1,0:T(8,128)}) custom-call(bf16[512,192]{1,0:T(8,128)(2,1)} %bitcast.16, f32[2,1]{1,0:T(2,128)} %copy.31.lead, s32[1,4]{1,0:T(1,128)} %lens.1, ...), custom_call_target="tpu_custom_call" | custom-call | tf_op jit(solution)/shard_map/pallas_call | solution.py:1348
  200.4 0.0 copy-start
  200.4 1.2 copy-done
  201.6 0.0 copy-start.1
  201.6 1.0 copy-done.1
  202.6 0.0 copy-start.2
  202.6 0.9 copy-done.2
  203.6 0.0 copy-start.3
  203.6 0.9 copy-done.3
  204.5 0.0 copy-start.4
  204.5 0.8 copy-done.4
  205.4 0.0 copy-start.5
  205.4 0.8 copy-done.5
  206.2 2.0 shard_map.264
  208.2 0.8 copy.32
  208.9 0.6 copy.35
Async XLA Ops:
  200.4 1.2 copy-start
  201.6 1.0 copy-start.1
  202.6 0.9 copy-start.2
  203.6 0.9 copy-start.3
  204.5 0.8 copy-start.4
  205.4 0.8 copy-start.5

commit v3 on v2

--- a/solution.py
+++ b/solution.py
@@ -120,7 +120,7 @@
     fo=((16, 256), F32),
     att=((768, 512), F32),
     op=((256, 512), BF),
-    op1=((256, 128), BF),
+    op1=((4, 256, 128), BF),
     hT=((1024, 512), BF),
     hrow=((512, 1024), BF),
     acc=((512, 1024), F32),
@@ -313,9 +313,10 @@
     vec[5:7, :] = norm_gain[...].astype(F32)
     vec[7:9, :] = norm_bias[...].astype(F32)
     vec[9:12, :] = attn_bias[...].astype(F32)
-    vec[12:16, :] = fc1[...].astype(F32)
-    vec[16:17, :] = fc2[...].astype(F32)
-    vec[17:18, :] = agg_query[...].astype(F32)
+    for i in range(4):
+        vec[12 + i : 13 + i, :] = fc1[i * 1024 : (i + 1) * 1024][None].astype(F32)
+    vec[16:17, :] = fc2[...][None].astype(F32)
+    vec[17:18, :] = agg_query[...][None].astype(F32)
 
     @when(first_owner)
     def _():
@@ -328,9 +329,8 @@
         1.0,
         0.0,
     ).astype(BF)
-    for i in range(4):
-        cols = slice(i * 256, (i + 1) * 256)
-        table[0:192, cols] = mm(perm, patch[:, cols]).astype(BF)
+    for p in range(PIX):
+        table[p * 48 : (p + 1) * 48, :] = patch[:, p, :]
     table[192:240, :] = (patch_b[...].astype(F32) + var_emb[...].astype(F32)).astype(BF)
     table[240:256, :] = jnp.zeros((16, 1024), BF)
 
@@ -417,37 +417,30 @@
             when(no(whole))(to_sibling)
             when(whole)(to_layer)
 
-    def near(cond, b):
+    def along(cond, b, way):
         block = R.W.at[z, b, c]
+        zz = z ^ 1 if way == 0 else here.far
 
         @when(cond)
         def _():
-            remote(block, block, R.sOwn.at[b, 0], R.rW.at[z, b, c], dev(s, z ^ 1, c)).start()
-
-    def step(cond, b, side=True, hold=False):
-        block = R.W.at[z, b, c]
-
+            remote(block, block, R.sOwn.at[b, way], R.rW.at[z, b, c], dev(s, zz, c)).start()
+
+    def ready(cond, b):
         @when(cond)
         def _():
-            arrived(block, R.rW.at[z, b, c])
-
-        @when(cond & outer)
+            arrived(R.W.at[z, b, c], R.rW.at[z, b, c])
+
+    def aside(cond, b):
+        @when(cond)
         def _():
-            remote(block, block, R.sOwn.at[b, 1], R.rW.at[z, b, c], dev(s, z ^ 2, c)).start()
-            remote(block, block, R.sOwn.at[b, 0], R.rW.at[z, b, c], dev(s, z ^ 1, c)).start()
-
-        if not hold:
-            near(cond & inner, b)
-
-        @when(cond & inner)
-        def _():
-            remote(block, block, R.sOwn.at[b, 1], R.rW.at[z, b, c], dev(s, z ^ 3, c)).start()
-
+            spread(z, b)
+
+    def step(cond, b, side=True):
+        ready(cond, b)
+        along(cond, b, 1)
+        along(cond, b, 0)
         if side:
-
-            @when(cond)
-            def _():
-                spread(z, b)
+            aside(cond, b)
 
     def foreign(zz, b, cond=True):
         block = R.W.at[zz, b, c]
@@ -476,8 +469,13 @@
 
     step(top & (s == 0), 0, False)
     step(no(top) & (s == 1), 1)
+    first_feed = z != 2
     for b in (2, 3):
-        step(s == b, b)
+        mine_first = (s == b) & first_feed
+        ready(mine_first, b)
+        along(mine_first, b, 1)
+        along(mine_first & inner, b, 0)
+        aside(mine_first, b)
 
     tcol = iota((GROUP, 1), 0).astype(F32)
     trow = iota((1, GROUP), 1).astype(F32)
@@ -494,7 +492,7 @@
     place_short = tcol - start_col
     valid = seg_col < 3.5
     lead_short = lead[0, 0]
-    lead_long = lead[1, 0]
+    lead_long = lead[0, 1]
     freq = jnp.exp(-math.log(10000.0) * 2.0 * iota((1, 512), 1).astype(F32) / D)
 
     def positions(g):
@@ -521,7 +519,8 @@
         arrived(R.kq.at[c], R.rK.at[c])
 
     remote(R.kq.at[c], R.kq.at[c], R.sK.at[15], R.rK.at[c], sib).start()
-    R.patT[...] = mm_nt(perm, pat[...]).astype(BF)
+    for g in range(2):
+        R.patT[:, g * 256 : (g + 1) * 256] = mm(perm, pat[g]).astype(BF)
 
     @when(z != 2)
     def _():
@@ -534,7 +533,13 @@
         spread(3, 0)
 
     for b in (2, 3):
-        step(s != b, b, hold=True)
+        mine_first = (s == b) & first_feed
+        ready(no(mine_first), b)
+        along(no(mine_first), b, 1)
+        aside(no(mine_first), b)
+    along(outer, 2, 0)
+    along(outer, 3, 0)
+    along(inner & no((s == 2) & first_feed), 2, 0)
     scatter(late)
 
     arrived(R.kq.at[1 - c], R.rK.at[1 - c])
@@ -570,8 +575,6 @@
 
     for zz in range(3):
         foreign(zz, 1, inner)
-    for b in (2, 3):
-        near(inner & (s != b), b)
     R.op[240:256, :] = jnp.where(iota((16, 512), 0) == 0, 1.0, 0.0).astype(BF)
     r48 = iota((48, 256), 0)
     c48 = iota((48, 256), 1)
@@ -622,17 +625,15 @@
         spread(3, 1)
 
     foreign(z ^ 3, 2, inner)
+    along(inner & no((s == 3) & first_feed), 3, 0)
+    foreign(3, 1, outer)
     wait_whole(1)
 
-    def stream0_part(i):
-        g = lax.div(i, 4)
-        n = lax.rem(i, 4)
-        rows = at(g * 256, 256, 256)
+    def stream0_part(n):
         cols = at(n * 256, 256, 256)
-        value = mm(R.hrow[rows, 0:512], R.WF[1, n, 0]) + mm(R.hrow[rows, 512:1024], R.WF[1, n, 1])
-        R.st0[rows, cols] = (value + R.acc[rows, cols]).astype(BF)
-
-    loop(8, stream0_part)
+        R.st0[:, cols] = (mm(R.hrow[...], R.WF[1, n].reshape(1024, 256)) + R.acc[:, cols]).astype(BF)
+
+    loop(4, stream0_part)
 
     def norm_into(src, dst, which):
         def part(i):
@@ -646,7 +647,6 @@
     norm_into(R.st0, R.nrm, 0)
     foreign(z ^ 3, 3, inner)
 
-    foreign(3, 1, outer)
 
     own_cols = at(s * 256, 256, 256)
     own_rows = at(s * OWN, OWN, OWN)
@@ -697,117 +697,65 @@
     step(z == 2, 0)
     for b in (2, 3):
         foreign(z ^ 2, b, inner)
+        foreign(z ^ 1, b)
     pass_on(2)
-    for b in (2, 3):
-        for k in (1, 2, 3):
-            foreign(z ^ k, b, outer if k > 1 else True)
-
-    def feed_out_grad(b):
-        def part(g):
-            rows = at(g * 256, 256, 256)
-            block = R.W.at[2 + b % 2, 2 + b // 2]
-            total = jnp.zeros((256, 256), F32)
-            for n in range(4):
-                tile = block[n // 2, (n % 2) * 256 : (n % 2 + 1) * 256, :]
-                total = total + mm_nt(gout[rows, n * 256 : (n + 1) * 256], tile)
-            R.gact[b, rows, :] = total
-
-        loop(2, part)
-
-    wait_half(2, 2)
-    feed_out_grad(0)
-    wait_half(3, 2)
-    feed_out_grad(1)
     wait_whole(2)
     for p in peers:
         arrived(R.mix.at[:, at(p * 256, 256, 256)], R.rMix.at[p])
-    foreign(2, 0)
-
-    def stream1_part(i):
-        g = lax.div(i, 4)
-        n = lax.rem(i, 4)
-        rows = at(g * 256, 256, 256)
+    def stream1_part(n):
         cols = at(n * 256, 256, 256)
-        value = mm(R.mix[rows, 0:512], R.WF[2, n, 0]) + mm(R.mix[rows, 512:1024], R.WF[2, n, 1])
-        value = value + vec[11:12, cols] + R.st0[rows, cols].astype(F32)
-        R.st1[rows, cols] = value.astype(BF)
-
-    loop(8, stream1_part)
+        value = mm(R.mix[...], R.WF[2, n].reshape(1024, 256)) + vec[11:12, cols]
+        R.st1[:, cols] = (value + R.st0[:, cols].astype(F32)).astype(BF)
+
+    loop(4, stream1_part)
     norm_into(R.st1, R.nrm2, 1)
-    wait_half(2, 3)
-    feed_out_grad(2)
-    wait_half(3, 3)
-    feed_out_grad(3)
-    for b in (2, 3):
-        for zz in (0, 1):
-            wait_half(zz, b)
-
-    def feed_in(i):
-        b = lax.div(i, 2)
-        g = lax.rem(i, 2)
-        rows = at(g * 256, 256, 256)
-        bias = vec[pl.ds(12 + b, 1), own_cols]
-        weight = R.W[lax.rem(b, 2), 2 + lax.div(b, 2)].reshape(1024, 256)
-        x = mm(R.nrm2[rows, :], weight) + bias
-        half_cdf = 0.5 + 0.5 * lax.erf(x * math.sqrt(0.5))
-        R.act[b, rows, :] = (x * half_cdf).astype(BF)
-        slope = half_cdf + x * (jnp.exp(-0.5 * x * x) * (1.0 / math.sqrt(2.0 * math.pi)))
-        R.gin[b, rows, :] = (R.gact[b, rows, :] * slope).astype(BF)
-
-    loop(8, feed_in)
-
-    def reduce_rows(phase, make):
-        for i, p in enumerate(peers):
-            make(p)
-            block = R.rsS.at[at(p * OWN, OWN, OWN), :]
-            remote(block, R.rsR.at[s], R.sR.at[phase, i], R.rR.at[phase, s], dev(p, z, c)).start()
-        make(s)
-
-    def reduced(phase):
-        total = R.rsS[own_rows, :].astype(F32)
-        for p in peers:
-            arrived(R.rsR.at[p], R.rR.at[phase, p])
-            total = total + R.rsR[p].astype(F32)
+    early = jnp.where(z < 2, 0, 1)
+
+    def feed(par):
+        def part(i):
+            bb = lax.div(i, 2)
+            b = par + 2 * bb
+            rows = at(lax.rem(i, 2) * 256, 256, 256)
+            block = R.W.at[2 + par, 2 + bb]
+            grad = jnp.zeros((256, 256), F32)
+            for n in range(4):
+                tile = block[n // 2, (n % 2) * 256 : (n % 2 + 1) * 256, :]
+                grad = grad + mm_nt(gout[rows, n * 256 : (n + 1) * 256], tile)
+            bias = vec[pl.ds(12 + b, 1), own_cols]
+            x = mm(R.nrm2[rows, :], R.W[par, 2 + bb].reshape(1024, 256)) + bias
+            half_cdf = 0.5 + 0.5 * lax.erf(x * math.sqrt(0.5))
+            R.act[b, rows, :] = (x * half_cdf).astype(BF)
+            slope = half_cdf + x * (jnp.exp(-0.5 * x * x) * (1.0 / math.sqrt(2.0 * math.pi)))
+            R.gin[b, rows, :] = (grad * slope).astype(BF)
+
+        loop(4, part)
+
+    def feed_norm(par, rows):
+        total = mm_nt(R.gin[par, rows, :], R.W[par, 2].reshape(1024, 256))
+        return total + mm_nt(R.gin[par + 2, rows, :], R.W[par, 3].reshape(1024, 256))
+
+    def feed_out(par, n, rows):
+        total = jnp.zeros((256, 256), F32)
+        for bb in range(2):
+            tile = R.W[2 + par, 2 + bb, lax.div(n, 2), at(lax.rem(n, 2) * 256, 256, 256), :]
+            total = total + mm(R.act[par + 2 * bb, rows, :], tile)
         return total
 
-    def feed_norm(p):
-        rows = at(p * OWN, OWN, OWN)
-        total = jnp.zeros((OWN, 1024), F32)
-        for b in range(4):
-            total = total + mm_nt(R.gin[b, rows, :], R.W[b % 2, 2 + b // 2].reshape(1024, 256))
-        R.rsS[rows, :] = total.astype(BF)
-
-    reduce_rows(0, feed_norm)
-
-    def drain_own(cond, b):
-        @when(cond)
-        def _():
-            for i in range(2):
-                sent(R.msgs.at[0], R.sOwn.at[b, i])
-
-    def drain_spread(zz, b):
-        whole, f = full_of(zz, b)
-
-        def side():
+    def tiles(body):
+        loop(8, lambda i: body(lax.rem(i, 4), at(lax.div(i, 4) * 256, 256, 256)))
+
+    def drain_feed(zz):
+        for b in (2, 3):
             sent(R.msgs.at[0], R.sFwd.at[zz, b, 0])
 
-        def layer():
-            for i in range(3):
-                sent(R.msgs.at[0], R.sFx.at[f, i])
-
-        if whole is None or zz < 3:
-            (layer if whole is True else side)()
-        else:
-            layer()
-
-        @when((z != zz) & inner & (z ^ 1 != zz))
-        def _():
-            sent(R.msgs.at[0], R.sFwd.at[zz, b, 1])
-
-    for b in (2, 3):
-        drain_own(always, b)
-        for zz in range(4):
-            drain_spread(zz, b)
+            @when((z != zz) & inner & (z ^ 1 != zz))
+            def _():
+                sent(R.msgs.at[0], R.sFwd.at[zz, b, 1])
+
+            @when(z == zz)
+            def _():
+                for i in range(2):
+                    sent(R.msgs.at[0], R.sOwn.at[b, i])
 
     def transposed(src):
         def part(i):
@@ -831,34 +779,19 @@
             R.W[zz, b, h] = mm(left[h * 512 : (h + 1) * 512, :], right).astype(BF)
         exchange(zz, b)
 
-    transposed(R.nrm2)
-
-    def first_gradient(b):
-        column_gradient(lax.rem(b, 2), 2 + lax.div(b, 2), R.tr, R.gin[b])
-
-    loop(4, first_gradient)
-
-    def out_part(i):
-        g = lax.div(i, 4)
-        n = lax.rem(i, 4)
-        rows = at(g * 256, 256, 256)
-        total = jnp.zeros((256, 256), F32)
-        for b in range(4):
-            tile = R.W[2 + b % 2, 2 + b // 2, lax.div(n, 2), at(lax.rem(n, 2) * 256, 256, 256), :]
-            total = total + mm(R.act[b, rows, :], tile)
-        R.hrow[rows, at(n * 256, 256, 256)] = total.astype(BF)
-
-    loop(8, out_part)
-
-    def second_gradient(b):
-        zz = 2 + lax.rem(b, 2)
-        bb = 2 + lax.div(b, 2)
-        for n in range(4):
-            tile = mm_tn(R.act[b], gout[:, n * 256 : (n + 1) * 256])
-            R.W[zz, bb, n // 2, (n % 2) * 256 : (n % 2 + 1) * 256, :] = tile.astype(BF)
-        exchange(zz, bb)
-
-    loop(4, second_gradient)
+    def feed_gradients(par):
+        drain_feed(par)
+        drain_feed(2 + par)
+
+        def part(bb):
+            b = par + 2 * bb
+            for n in range(4):
+                tile = mm_tn(R.act[b], gout[:, n * 256 : (n + 1) * 256])
+                R.W[2 + par, 2 + bb, n // 2, (n % 2) * 256 : (n % 2 + 1) * 256, :] = tile.astype(BF)
+            exchange(2 + par, 2 + bb)
+            column_gradient(par, 2 + bb, R.tr, R.gin[b])
+
+        loop(2, part)
 
     def summed(zz, b):
         arrived(R.CR.at[slot(zz, b)], R.rC.at[zz, b])
@@ -881,14 +814,96 @@
             def _():
                 remote(block, R.RC.at[3 - k, b], R.sZ.at[zz, b], R.rRC.at[3 - k, b], dev(s, z ^ 1, c)).start()
 
-    def second_send(zz, b):
+    def gradient_sends(cond, ks):
+        for k in ks:
+            for b in (2, 3):
+                first_send(k, b, cond)
+
+    def wait_feed(par):
+        for b in (2, 3):
+            wait_half(par, b)
+            wait_half(2 + par, b)
+
+    for b in (2, 3):
+        foreign(z ^ 2, b, outer)
+    wait_feed(early)
+    feed(early)
+
+    def norm_start(g):
+        rows = at(g * 256, 256, 256)
+        R.acc[rows, :] = feed_norm(early, rows)
+
+    def out_start(n, rows):
+        R.gact[n, rows, :] = feed_out(early, n, rows)
+
+    loop(2, norm_start)
+    tiles(out_start)
+    transposed(R.nrm2)
+    feed_gradients(early)
+    for b in (2, 3):
+        foreign(z ^ 3, b, outer)
+    later = 1 - early
+    gradient_sends(outer, (2, 0))
+    foreign(2, 0)
+    wait_feed(later)
+    feed(later)
+
+    def reduce_rows(phase, make):
+        for i, p in enumerate(peers):
+            make(p)
+            block = R.rsS.at[at(p * OWN, OWN, OWN), :]
+            remote(block, R.rsR.at[s], R.sR.at[phase, i], R.rR.at[phase, s], dev(p, z, c)).start()
+        make(s)
+
+    def reduced(phase):
+        total = R.rsS[own_rows, :].astype(F32)
+        for p in peers:
+            arrived(R.rsR.at[p], R.rR.at[phase, p])
+            total = total + R.rsR[p].astype(F32)
+        return total
+
+    def norm_end(p):
+        rows = at(p * OWN, OWN, OWN)
+        R.rsS[rows, :] = (R.acc[rows, :] + feed_norm(later, rows)).astype(BF)
+
+    def out_end(n, rows):
+        R.hrow[rows, at(n * 256, 256, 256)] = (R.gact[n, rows, :] + feed_out(later, n, rows)).astype(BF)
+
+    reduce_rows(0, norm_end)
+
+    def drain_own(cond, b):
+        @when(cond)
+        def _():
+            for i in range(2):
+                sent(R.msgs.at[0], R.sOwn.at[b, i])
+
+    def drain_spread(zz, b):
+        whole, f = full_of(zz, b)
+
+        def side():
+            sent(R.msgs.at[0], R.sFwd.at[zz, b, 0])
+
+        def layer():
+            for i in range(3):
+                sent(R.msgs.at[0], R.sFx.at[f, i])
+
+        if whole is None or zz < 3:
+            (layer if whole is True else side)()
+        else:
+            layer()
+
+        @when((z != zz) & inner & (z ^ 1 != zz))
+        def _():
+            sent(R.msgs.at[0], R.sFwd.at[zz, b, 1])
+
+    def second_send(k, b, cond=True):
+        zz = z ^ k
         block = R.W.at[zz, b, c]
 
-        @when(inner & (z != zz) & (z ^ 1 != zz))
+        @when(inner & cond)
         def _():
-            k = (z ^ zz) - 2
-            arrived(R.RC.at[k, b], R.rRC.at[k, b])
-            R.W[zz, b, c] = (R.W[zz, b, c].astype(F32) + R.RC[k, b].astype(F32)).astype(BF)
+            arrived(R.RC.at[k - 2, b], R.rRC.at[k - 2, b])
+            R.W[zz, b, c] = (R.W[zz, b, c].astype(F32) + R.RC[k - 2, b].astype(F32)).astype(BF)
             remote(block, R.RB.at[b], R.sZ.at[zz, b], R.rRB.at[b], dev(s, zz, c)).start()
 
     def owner_of(b):
@@ -915,14 +930,17 @@
         def _():
             remote(block, R.FR.at[m], R.sFin.at[b], R.rFin.at[m], dev(b, z, tc)).start()
 
-    for k in (2, 3, 1, 0):
-        for b in (2, 3):
-            first_send(k, b)
+    gradient_sends(inner, (1, 3))
+    tiles(out_end)
+    feed_gradients(later)
 
     R.small[...] = jnp.zeros((16, 1024), F32)
     for b in range(4):
         R.small[10 + b : 11 + b, own_cols] = column_sum(R.gin[b].astype(F32))
     R.small[14:15, :] = column_sum(gout[own_rows, :].astype(F32))
+
+    gradient_sends(outer, (3, 1))
+    gradient_sends(inner, (2, 0))
 
     g2 = reduced(0)
     gx, gw, gb = norm_back(R.st1[own_rows, :].astype(F32), g2, vec[6:7, :])
@@ -1016,6 +1034,8 @@
     for k in (2, 3, 1, 0):
         first_send(k, 1)
 
+    for b in (2, 3):
+        second_send(3, b)
     g1 = reduced(1)
     gx, gw, gb = norm_back(R.st0[own_rows, :].astype(F32), g1, vec[5:6, :])
     R.small[3:4, :] = gw
@@ -1040,19 +1060,20 @@
     R.G = R.acc.at[0:256, :]
     R.gpT[...] = jnp.zeros((192, OWN), F32)
     R.G[...] = jnp.zeros((256, 1024), F32)
-    R.op1[240:256, :] = jnp.where(iota((16, OWN), 0) == 0, 1.0, 0.0).astype(BF)
-
-    def embed_back(h):
+    for hh in range(4):
+        R.op1[hh, 240:256, :] = jnp.where(iota((16, OWN), 0) == 0, 1.0, 0.0).astype(BF)
+
+    def embed_back(h, op1):
         rows = at(h * 48, 48, 16)
         prob = R.att[rows, own_rows]
         low = prob.astype(BF)
         lowf = low.astype(F32)
-        weights_of(R.op1, low, own_rows)
+        weights_of(op1, low, own_rows)
         hrows = at(h * 64, 64, 64)
         gop = mm_tn(R.mT[hrows, :], R.ghT[hrows, :])
         cols = at(lax.div(h, 4) * 256, 256, 256)
         keep = lane_head == lax.rem(h, 4)
-        R.G[:, cols] += jnp.where(keep, mm(R.op1[...], R.gh[:, cols]), 0.0)
+        R.G[:, cols] += jnp.where(keep, mm(op1[...], R.gh[:, cols]), 0.0)
         gatt = gop[192:240, :]
         for p in range(4):
             gatt = gatt + gop[p * 48 : (p + 1) * 48, :] * R.patT[p * 48 : (p + 1) * 48, own_rows].astype(F32)
@@ -1061,7 +1082,11 @@
             prow = slice(p * 48, (p + 1) * 48)
             R.gpT[prow, :] += gop[prow, :] * lowf
 
-    loop(HEADS, embed_back)
+    def embed_back_four(i):
+        for hh in range(4):
+            embed_back(4 * i + hh, R.op1.at[hh])
+
+    loop(4, embed_back_four)
 
     gsc = R.gsc[...]
     gsc_high = gsc.astype(BF)
@@ -1099,8 +1124,7 @@
         remote(R.pixS.at[p], R.pixR.at[s], R.sP.at[i], R.rP.at[s], dev(p, z, c)).start()
 
     for b in (2, 3):
-        for zz in range(4):
-            second_send(zz, b)
+        second_send(2, b)
     arrived(R.fc.at[1], R.rFo.at[0])
     R.fp[s] = R.fc[0] + R.fc[1]
     for i, p in enumerate(peers):
@@ -1132,11 +1156,10 @@
     for i, zz in enumerate(layers):
         remote(R.fromz.at[z], R.fromz.at[z], R.sAll.at[4 + i], R.rAll.at[5 + z], dev(s, zz, c)).start()
 
-    for zz in range(4):
-        second_send(zz, 1)
     for k in (2, 3, 1, 0):
         first_send(k, 0, z ^ k == 3)
-    send_out(2)
+    for k in (2, 3):
+        second_send(k, 1)
 
     for zz in layers:
         arrived(R.fz.at[zz], R.rFo.at[5 + zz])
@@ -1180,6 +1203,7 @@
         aq = jnp.where(iota((16, 512), 0) == 0, aq, 0.0).astype(BF)
         gbank[...] = mm_tn(aq, R.gqv[...]).astype(BF)
 
+    send_out(2)
     last_send(always, 2)
     last_send(always, 3)
 
@@ -1187,20 +1211,9 @@
         arrived(R.fin.at[part_of(p), :], R.rAll.at[9 + p])
     remote(R.fin.at[half, :], R.fin.at[half, :], R.sAll.at[10], R.rAll.at[13], sib).start()
 
-    second_send(3, 0)
+    for k in (2, 3):
+        second_send(k, 0, z ^ k == 3)
     last_send(always, 1)
-
-    total = R.hrow[:, own_cols].astype(F32) + R.st1[:, own_cols].astype(F32) + vec[16:17, own_cols]
-    for p in peers:
-        arrived(R.outR.at[p], R.rOut.at[p])
-        total = total + R.outR[p].astype(F32)
-    out[...] = total.astype(BF)
-
-    for i, p in enumerate(peers):
-        arrived(R.pixR.at[p], R.rP.at[p])
-    R.pixR[s] = R.pixS[s]
-    for p in range(4):
-        gpix[p * OWN : (p + 1) * OWN, :] = R.pixR[p].astype(F32).T
 
     wait_whole(0)
     arrived(R.fin.at[other, :], R.rAll.at[13])
@@ -1239,6 +1252,18 @@
     rows_out[0:8, :] = R.gqv[0:8, :].astype(F32)
     rows_out[8:16, 0:512] = R.gaq[0]
     rows_out[8:16, 512:1024] = R.gaq[1]
+
+    total = R.hrow[:, own_cols].astype(F32) + R.st1[:, own_cols].astype(F32) + vec[16:17, own_cols]
+    for p in peers:
+        arrived(R.outR.at[p], R.rOut.at[p])
+        total = total + R.outR[p].astype(F32)
+    out[...] = total.astype(BF)
+
+    for i, p in enumerate(peers):
+        arrived(R.pixR.at[p], R.rP.at[p])
+    R.pixR[s] = R.pixS[s]
+    for p in range(4):
+        gpix[p // 2, :, (p % 2) * OWN : (p % 2 + 1) * OWN] = R.pixR[p].astype(F32)
 
     @when(used)
     def _():
@@ -1329,9 +1354,11 @@
 VMEM = pl.BlockSpec(memory_space=pltpu.VMEM)
 SMEM = pl.BlockSpec(memory_space=pltpu.SMEM)
 ARG_SHAPES = (
-    [((512, 192), BF), ((2, 1), F32), ((1, 4), jnp.int32), ((512, 1024), BF), ((512, 1024), BF), ((192, 1024), BF)]
+    [((2, 192, 256), BF), ((1, 2), F32), ((1, 4), jnp.int32), ((512, 1024), BF), ((512, 1024), BF), ((48, 4, 1024), BF)]
     + [((48, 1024), BF)] * 2
-    + [((n, 1024), BF) for n in (1, 3, 2, 2, 2, 3, 4, 1)]
+    + [((1024,), BF)]
+    + [((n, 1024), BF) for n in (3, 2, 2, 2, 3)]
+    + [((4096,), BF), ((1024,), BF)]
 )
 
 
@@ -1339,7 +1366,7 @@
     shape = jax.ShapeDtypeStruct
     outs = [
         shape((512, 256), BF),
-        shape((512, 48), F32),
+        shape((2, 48, 256), F32),
         shape((512, 1024), BF),
         shape((256, 1024), BF),
         shape((16, 1024), F32),
@@ -1358,28 +1385,17 @@
     )(*args)
 
 
-def finish_kernel(
-    out,
-    gpix,
-    gbank,
-    gtab,
-    sums,
-    rows,
-    o_out,
-    o_pix,
-    o_bank,
-    o_patch,
-    o_patch_b,
-    o_var,
-    o_query,
-    o_agg,
-    o_lead,
-    o_gain,
-    o_bias,
-    o_attn,
-    o_fc1,
-    o_fc2,
-):
+def finish_kernel(*refs):
+    sources, rest = refs[:6], refs[6:]
+    outs, scratch = rest[:14], rest[14:]
+    out, gpix, gbank, gtab, sums, rows = scratch[:6]
+    sems = scratch[6]
+    copies = [pltpu.make_async_copy(a, b, sems.at[i]) for i, (a, b) in enumerate(zip(sources, scratch[:6]))]
+    for copy in copies:
+        copy.start()
+    for copy in copies:
+        copy.wait()
+    o_out, o_pix, o_bank, o_patch, o_patch_b, o_var, o_query, o_agg, o_lead, o_gain, o_bias, o_attn, o_fc1, o_fc2 = outs
     o_out[...] = out[...]
     o_pix[...] = gpix[...]
     o_bank[...] = gbank[...].astype(F32)
@@ -1387,7 +1403,7 @@
         o_patch[:, p, :] = gtab[p * VARS : (p + 1) * VARS, :].astype(F32)
     o_patch_b[...] = gtab[192:240, :].astype(F32)
     o_var[...] = gtab[192:240, :].astype(F32)
-    o_query[...] = rows[8:9, :]
+    o_query[...] = rows[8, :]
     o_agg[0:1, :] = rows[0:1, :]
     o_agg[1:3, :] = sums[0:2, :]
     o_lead[0:1, :] = sums[2:3, :]
@@ -1395,20 +1411,23 @@
     o_gain[...] = sums[3:5, :]
     o_bias[...] = sums[5:7, :]
     o_attn[...] = sums[7:10, :]
-    o_fc1[...] = sums[10:14, :]
-    o_fc2[...] = sums[14:15, :]
+    for i in range(4):
+        o_fc1[i * 1024 : (i + 1) * 1024] = sums[10 + i, :]
+    o_fc2[...] = sums[14, :]
 
 
 def finish_call(*args):
     shape = jax.ShapeDtypeStruct
-    outs = [shape((512, 256), BF), shape((512, 48), F32), shape((512, 1024), F32), shape((48, 4, 1024), F32)]
-    outs += [shape((48, 1024), F32)] * 2 + [shape((n, 1024), F32) for n in (1, 3, 2, 2, 2, 3, 4, 1)]
+    outs = [shape((512, 256), BF), shape((2, 48, 256), F32), shape((512, 1024), F32), shape((48, 4, 1024), F32)]
+    outs += [shape((48, 1024), F32)] * 2 + [shape((1024,), F32)]
+    outs += [shape((n, 1024), F32) for n in (3, 2, 2, 2, 3)] + [shape((FF,), F32), shape((1024,), F32)]
     return pl.pallas_call(
         finish_kernel,
         out_shape=outs,
-        in_specs=[VMEM] * len(args),
+        in_specs=[pl.BlockSpec(memory_space=pl.ANY)] * len(args),
         out_specs=[VMEM] * len(outs),
-        compiler_params=pltpu.CompilerParams(vmem_limit_bytes=40 * 2**20),
+        scratch_shapes=[pltpu.VMEM(a.shape, a.dtype) for a in args] + [pltpu.SemaphoreType.DMA((len(args),))],
+        compiler_params=pltpu.CompilerParams(vmem_limit_bytes=63 * 2**20),
     )(*args)
 
 
@@ -1431,30 +1450,27 @@
     fc2_bias,
 ):
     parts = block_call(
-        patches.reshape(ROWS, VARS * PIX),
-        lead_times,
+        jnp.transpose(patches, (0, 2, 1)),
+        lead_times.T,
         short_lengths,
         cotangent.reshape(ROWS, D),
         bank[0],
-        patch_w.reshape(VARS * PIX, D),
+        patch_w,
         patch_b,
         var_emb,
-        agg_query[None],
+        agg_query,
         agg_bias,
         lead_embed,
         norm_gain,
         norm_bias,
         attn_bias,
-        fc1_bias.reshape(4, D),
-        fc2_bias[None],
+        fc1_bias,
+        fc2_bias,
     )
     o = finish_call(*parts)
     return (
-        (o[0].reshape(2, GROUP, 256), o[1].reshape(2, GROUP, 48), o[2][None])
-        + tuple(o[3:6])
-        + (o[6][0],)
-        + tuple(o[7:12])
-        + (o[12].reshape(FF), o[13][0])
+        (o[0].reshape(2, GROUP, 256), jnp.transpose(o[1], (0, 2, 1)), o[2][None])
+        + tuple(o[3:])
     )
 
 

time: 213 us -> 198 us (0.930); the launches traced: 210 us -> 198 us
  local copies, waits for them, and re-layouts: 15.9 us -> 0 us
  Pallas kernels: 193 us -> 197 us
    unnamed x16 -> x0, local copies, waits for them, and re-layouts: 10.3 us -> none
    reshape x2 -> x0, local copies, waits for them, and re-layouts: 3.13 us -> none  [the longest x1 1.83 us: on_device_fast(): patch_w.reshape(VARS * PIX, D)]
    pallas_call x1, Pallas kernels: 191 us -> 194 us  [block_call(): pl.pallas_call(block_kernel, out_shape=outs, in_specs=[VMEM, SMEM, SMEM]...]
    broadcast_in_dim x2 -> x0, local copies, waits for them, and re-layouts: 2.55 us -> none  [the longest x1 1.28 us: on_device_fast(): agg_query[None]]
where the time goes in v3:
time: 198 us
  Pallas kernels  197 us (99%)
    pallas_call x1, Pallas kernels, block_call(): pl.pallas_call(block_kernel, out_shape=outs, in_specs=[VMEM, SMEM, SMEM]...  194 us

profile of v3, /device:TPU:25, one launch (start us, length us, event | category | flops | bytes accessed | tf_op | source)
XLA Modules:
  0.0 198.1 jit_solution(3953910683853225460)
XLA Ops:
  0.7 193.7 %shard_map.263 = (bf16[512,256]{1,0:T(8,128)(2,1)}, f32[2,48,256]{2,1,0:T(8,128)}, bf16[512,1024]{1,0:T(8,128)(2,1)}, bf16[256,1024]{1,0:T(8,128)(2,1)}, f32[16,1024]{1,0:T(8,128)}, /*index=5*/f32[16,1024]{1,0:T(8,128)}) custom-call(bf16[2,192,256]{2,1,0:T(8,128)(2,1)} %bitcast.9, f32[1,2]{1,0:T(1,128)} %bitcast.10, s32[1,4]{1,0:T(1,128)} %lens.1, ...), custom_call_target="tpu_custom_call" | custom-call | tf_op jit(solution)/shard_map/pallas_call | solution.py:1375
  194.4 3.5 %shard_map.264 = (bf16[512,256]{1,0:T(8,128)(2,1)}, f32[2,48,256]{2,1,0:T(8,128)}, f32[512,1024]{1,0:T(8,128)}, f32[48,4,1024]{2,1,0:T(4,128)}, f32[48,1024]{1,0...) custom-call(bf16[512,256]{1,0:T(8,128)(2,1)} %get-tuple-element.34.r, ...), custom_call_target="tpu_custom_call" | custom-call | tf_op jit(solution)/shard_map/pallas_call | solution.py:1424

commit v4 on v3

--- a/solution.py
+++ b/solution.py
@@ -109,7 +109,9 @@
     tabT=((1024, 256), BF),
     msgs=((4, 512, 256), BF),
     W=((4, 4, 2, 512, 256), BF),
-    WF=((3, 4, 2, 512, 256), BF),
+    WF=((2, 4, 2, 512, 256), BF),
+    kqF=((16, 1024), BF),
+    gt=((4, 256, 256), BF),
     qbuf=((2, 8, 1024), F32),
     qb=((16, 1024), BF),
     kq=((2, 16, 512), BF),
@@ -173,13 +175,17 @@
 )
 
 SEMS = dict(
+    sIn=(14,),
+    sRes=(6,),
     rW=(4, 4, 2),
-    rF=(3, 4, 2),
+    rF=(2, 4, 2),
     sMsg=(4,),
     sOwn=(4, 2),
     sFwd=(4, 4, 2),
-    sFx=(3, 3),
-    sFc=(3, 4),
+    sFx=(2, 3),
+    sFc=(2, 4),
+    sGt=(3,),
+    rGt=(4,),
     rQ=(2,),
     sQ=(2,),
     rK=(2,),
@@ -191,8 +197,8 @@
     sMz=(3,),
     sMp=(3,),
     sMc=(4,),
-    sMix=(3,),
-    rMix=(4,),
+    sMix=(2, 3),
+    rMix=(2, 4),
     sOut=(4,),
     rOut=(4,),
     sR=(2, 4),
@@ -225,41 +231,26 @@
     pass
 
 
-def block_kernel(
-    pat,
-    lead,
-    lens,
-    cot,
-    bank,
-    patch,
-    patch_b,
-    var_emb,
-    agg_query,
-    agg_bias,
-    lead_embed,
-    norm_gain,
-    norm_bias,
-    attn_bias,
-    fc1,
-    fc2,
-    out,
-    gpix,
-    gbank,
-    gtab,
-    sums,
-    rows_out,
-    *scratch,
-):
+def block_kernel(*refs):
+    sources, lead, lens = refs[0:14], refs[14], refs[15]
+    targets, rest = refs[16:22], refs[22:]
+    held, results, scratch = rest[0:14], rest[14:20], rest[20:]
+    pat, cot, bank, patch, patch_b, var_emb, agg_query, agg_bias, lead_embed = held[0:9]
+    norm_gain, norm_bias, attn_bias, fc1, fc2 = held[9:14]
+    out, gpix, gbank, gtab, sums, rows_out = results
     R = Refs()
     for name, ref in zip(NAMES, scratch):
         setattr(R, name, ref)
+    loads = [pltpu.make_async_copy(a, b, R.sIn.at[i]) for i, (a, b) in enumerate(zip(sources, held))]
+    for i in (2, *range(3, 14), 0, 1):
+        loads[i].start()
     here = Place()
     s, z, c = here.s, here.z, here.c
     dev = here.dev
     outer = here.outer
     inner = jnp.logical_not(outer)
     sib = dev(s, z, 1 - c)
-    is_row = (s >= 2) & (z >= 2)
+    is_row = (z >= 2) & ((s >= 2) | ((s == 0) & (z == 2)))
     peers = [s ^ 1, s ^ 2, s ^ 3]
     layers = [z ^ 1, z ^ 2, z ^ 3]
     others = [(s ^ i, z ^ k) for k in range(4) for i in range(4) if (i, k) != (0, 0)]
@@ -269,6 +260,7 @@
 
     barrier([dev(p, k, c) for p, k in others] + [dev(p, z, 1 - c) for p in peers] + [sib])
 
+    loads[2].wait()
     first_owner = (s == 0) & (z == 0)
     key_owner = (s == 0) & (z == 1)
     value_owner = (s == 0) & (z == 2)
@@ -276,7 +268,7 @@
     late = value_owner
     used = no((s == 0) & (z < 3))
 
-    @when(no(is_row) & (used | late))
+    @when(no(is_row) & used)
     def _():
         for p in range(4):
             R.msgs[p] = bank[:, p * 256 : (p + 1) * 256]
@@ -308,6 +300,8 @@
 
     scatter(used)
 
+    for i in range(3, 14):
+        loads[i].wait()
     vec[0:3, :] = agg_bias[...].astype(F32)
     vec[3:5, :] = lead_embed[...].astype(F32)
     vec[5:7, :] = norm_gain[...].astype(F32)
@@ -392,9 +386,9 @@
 
     def full_of(zz, b):
         if b == 0:
-            return True, zz - 2
+            return zz == 3, 0
         if b == 1:
-            return zz == 3, 2
+            return zz == 3, 1
         return None, None
 
     def spread(zz, b):
@@ -411,8 +405,8 @@
 
         if whole is None:
             to_sibling()
-        elif whole is True:
-            to_layer()
+        elif isinstance(whole, bool):
+            (to_layer if whole else to_sibling)()
         else:
             when(no(whole))(to_sibling)
             when(whole)(to_layer)
@@ -511,6 +505,7 @@
     positions(1)
 
     gout = R.gout
+    loads[1].wait()
     gout[0:GROUP, :] = jnp.where(valid, cot[0:GROUP, :].astype(F32), 0.0).astype(BF)
     gout[GROUP:ROWS, :] = cot[GROUP:ROWS, :]
 
@@ -519,6 +514,7 @@
         arrived(R.kq.at[c], R.rK.at[c])
 
     remote(R.kq.at[c], R.kq.at[c], R.sK.at[15], R.rK.at[c], sib).start()
+    loads[0].wait()
     for g in range(2):
         R.patT[:, g * 256 : (g + 1) * 256] = mm(perm, pat[g]).astype(BF)
 
@@ -543,7 +539,9 @@
     scatter(late)
 
     arrived(R.kq.at[1 - c], R.rK.at[1 - c])
-    kq_full = jnp.concatenate([R.kq[0], R.kq[1]], axis=1)
+    R.kqF[:, 0:512] = R.kq[0]
+    R.kqF[:, 512:1024] = R.kq[1]
+    kq_full = R.kqF[...]
     R.fo[...] = mm_nt(kq_full, table[...])
 
     def fill_head(h):
@@ -609,7 +607,7 @@
         for p in range(4):
             arrived(R.WF.at[f, p, 1 - c], R.rF.at[f, p, 1 - c])
 
-    pass_on(1)
+    pass_on(0)
 
     def turn_tile(i):
         rows = at(i * 256, 256, 256)
@@ -627,24 +625,25 @@
     foreign(z ^ 3, 2, inner)
     along(inner & no((s == 3) & first_feed), 3, 0)
     foreign(3, 1, outer)
-    wait_whole(1)
+    wait_whole(0)
 
     def stream0_part(n):
         cols = at(n * 256, 256, 256)
-        R.st0[:, cols] = (mm(R.hrow[...], R.WF[1, n].reshape(1024, 256)) + R.acc[:, cols]).astype(BF)
+        R.st0[:, cols] = (mm(R.hrow[...], R.WF[0, n].reshape(1024, 256)) + R.acc[:, cols]).astype(BF)
 
     loop(4, stream0_part)
 
-    def norm_into(src, dst, which):
+    def norm_into(src, dst, which, g):
         def part(i):
-            rows = at(i * 64, 64, 64)
+            rows = at(g * 256 + i * 64, 64, 64)
             dst[rows, :] = normed_rows(
                 src[rows, :].astype(F32), vec[5 + which : 6 + which, :], vec[7 + which : 8 + which, :]
             ).astype(BF)
 
-        loop(8, part)
-
-    norm_into(R.st0, R.nrm, 0)
+        loop(4, part)
+
+    norm_into(R.st0, R.nrm, 0, 0)
+    norm_into(R.st0, R.nrm, 0, 1)
     foreign(z ^ 3, 3, inner)
 
 
@@ -688,27 +687,32 @@
             total = total + mm(prob.astype(BF), only(hh, R.v[rows, :]))
         R.mix[rows, own_cols] = total.astype(BF)
 
-    attend(0)
-    attend(1)
-    mine = R.mix.at[:, own_cols]
-    for i, p in enumerate(peers):
-        remote(mine, mine, R.sMix.at[i], R.rMix.at[s], dev(p, z, c)).start()
+    def mixed_of(g, p):
+        return R.mix.at[g * 256 : (g + 1) * 256, at(p * 256, 256, 256)]
+
+    for g in range(2):
+        attend(g)
+        for i, p in enumerate(peers):
+            remote(mixed_of(g, s), mixed_of(g, s), R.sMix.at[g, i], R.rMix.at[g, s], dev(p, z, c)).start()
 
     step(z == 2, 0)
     for b in (2, 3):
         foreign(z ^ 2, b, inner)
         foreign(z ^ 1, b)
-    pass_on(2)
-    wait_whole(2)
-    for p in peers:
-        arrived(R.mix.at[:, at(p * 256, 256, 256)], R.rMix.at[p])
-    def stream1_part(n):
+    pass_on(1)
+    wait_whole(1)
+    def stream1_part(g, n):
+        rows = slice(g * 256, (g + 1) * 256)
         cols = at(n * 256, 256, 256)
-        value = mm(R.mix[...], R.WF[2, n].reshape(1024, 256)) + vec[11:12, cols]
-        R.st1[:, cols] = (value + R.st0[:, cols].astype(F32)).astype(BF)
-
-    loop(4, stream1_part)
-    norm_into(R.st1, R.nrm2, 1)
+        value = mm(R.mix[rows, :], R.WF[1, n].reshape(1024, 256)) + vec[11:12, cols]
+        R.st1[rows, cols] = (value + R.st0[rows, cols].astype(F32)).astype(BF)
+
+    for g in range(2):
+        for p in peers:
+            arrived(mixed_of(g, p), R.rMix.at[g, p])
+        loop(4, functools.partial(stream1_part, g))
+        norm_into(R.st1, R.nrm2, 1, g)
+
     early = jnp.where(z < 2, 0, 1)
 
     def feed(par):
@@ -887,10 +891,7 @@
             for i in range(3):
                 sent(R.msgs.at[0], R.sFx.at[f, i])
 
-        if whole is None or zz < 3:
-            (layer if whole is True else side)()
-        else:
-            layer()
+        (layer if whole else side)()
 
         @when((z != zz) & inner & (z ^ 1 != zz))
         def _():
@@ -953,7 +954,7 @@
     def mixed_grad(p):
         total = jnp.zeros((OWN, 256), F32)
         for n in range(4):
-            tile = R.WF[2, n, lax.div(p, 2), at(lax.rem(p, 2) * 256, 256, 256), :]
+            tile = R.WF[1, n, lax.div(p, 2), at(lax.rem(p, 2) * 256, 256, 256), :]
             total = total + mm_nt(R.gs[0, :, n * 256 : (n + 1) * 256], tile)
         return total.astype(BF)
 
@@ -979,7 +980,6 @@
 
     send_out(0)
     send_out(1)
-    pass_on(0)
 
     swapped(0, R.gm)
 
@@ -1014,6 +1014,9 @@
         R.rsS[rows, :] = total.astype(BF)
 
     reduce_rows(1, attend_norm)
+    send_out(2)
+    for b in (2, 3):
+        second_send(3, b)
 
     transposed(R.nrm)
     drain_own(always, 1)
@@ -1035,7 +1038,7 @@
         first_send(k, 1)
 
     for b in (2, 3):
-        second_send(3, b)
+        second_send(2, b)
     g1 = reduced(1)
     gx, gw, gb = norm_back(R.st0[own_rows, :].astype(F32), g1, vec[5:6, :])
     R.small[3:4, :] = gw
@@ -1051,7 +1054,7 @@
         rows = at(lax.rem(i, 2) * 256, 256, 256)
         total = jnp.zeros((256, OWN), F32)
         for n in range(4):
-            total = total + mm_nt(R.WF[1, n, lax.div(i, 2), rows, :], R.gs[1, :, n * 256 : (n + 1) * 256])
+            total = total + mm_nt(R.WF[0, n, lax.div(i, 2), rows, :], R.gs[1, :, n * 256 : (n + 1) * 256])
         block = at(i * 256, 256, 256)
         R.ghT[block, :] = total.astype(BF)
         R.gh[:, block] = total.astype(BF).T
@@ -1123,8 +1126,6 @@
     for i, p in enumerate(peers):
         remote(R.pixS.at[p], R.pixR.at[s], R.sP.at[i], R.rP.at[s], dev(p, z, c)).start()
 
-    for b in (2, 3):
-        second_send(2, b)
     arrived(R.fc.at[1], R.rFo.at[0])
     R.fp[s] = R.fc[0] + R.fc[1]
     for i, p in enumerate(peers):
@@ -1138,6 +1139,8 @@
 
     for i, p in enumerate(peers):
         remote(R.gall.at[part_of(p), :], R.fromp.at[s], R.sAll.at[1 + i], R.rAll.at[1 + s], dev(p, z, c)).start()
+    last_send(always, 2)
+    last_send(always, 3)
 
     swapped(2, R.gb)
     column_gradient(3, 0, R.hT, R.gb[...])
@@ -1203,9 +1206,6 @@
         aq = jnp.where(iota((16, 512), 0) == 0, aq, 0.0).astype(BF)
         gbank[...] = mm_tn(aq, R.gqv[...]).astype(BF)
 
-    send_out(2)
-    last_send(always, 2)
-    last_send(always, 3)
 
     for p in peers:
         arrived(R.fin.at[part_of(p), :], R.rAll.at[9 + p])
@@ -1213,30 +1213,26 @@
 
     for k in (2, 3):
         second_send(k, 0, z ^ k == 3)
-    last_send(always, 1)
-
-    wait_whole(0)
+
     arrived(R.fin.at[other, :], R.rAll.at[13])
     sums[...] = R.fin[240:256, :].astype(F32)
-    kq_wide = jnp.concatenate([kq_full, jnp.zeros((112, 1024), BF)], axis=0)
-    wide = jnp.zeros((112, 256), BF)
-    gfh = jnp.concatenate([fo_high, wide], axis=0)
-    gfl = jnp.concatenate([fo_low, wide], axis=0)
-
-    def table_grad(h):
-        value = jnp.zeros((256, 512), F32)
-        for p in range(4):
-            value = value + mm_nt(R.fin[:, p * 256 : (p + 1) * 256], R.WF[0, p, h])
-        return value
-
-    for h in range(2):
-        cols = slice(h * 512, (h + 1) * 512)
-        gtab[:, cols] = (table_grad(h) + mm_tn(gfh, kq_wide[:, cols]) + mm_tn(gfl, kq_wide[:, cols])).astype(BF)
+    wait_half(2, 0)
+    zero16 = jnp.zeros((112, 256), BF)
+    kq_wide = jnp.concatenate([R.kqF[:, own_cols], zero16], axis=0)
+    value = mm_tn(jnp.concatenate([fo_high, zero16], axis=0), kq_wide)
+    value = value + mm_tn(jnp.concatenate([fo_low, zero16], axis=0), kq_wide)
+    for n in range(4):
+        tile = R.W[2, 0, n // 2, (n % 2) * 256 : (n % 2 + 1) * 256, :]
+        value = value + mm_nt(R.fin[:, n * 256 : (n + 1) * 256], tile)
+    R.gt[s] = value.astype(BF)
+    for i, p in enumerate(peers):
+        remote(R.gt.at[s], R.gt.at[s], R.sGt.at[i], R.rGt.at[s], dev(p, z, c)).start()
 
     @when(value_owner)
     def _():
         gbank[...] = mm_tn(table[:, half_rows], R.fin[...]).astype(BF)
 
+    last_send(always, 1)
     last_send(top, 0)
 
     @when(no(first_owner))
@@ -1253,6 +1249,10 @@
     rows_out[8:16, 0:512] = R.gaq[0]
     rows_out[8:16, 512:1024] = R.gaq[1]
 
+    for p in peers:
+        arrived(R.gt.at[p], R.rGt.at[p])
+    for p in range(4):
+        gtab[:, p * 256 : (p + 1) * 256] = R.gt[p]
     total = R.hrow[:, own_cols].astype(F32) + R.st1[:, own_cols].astype(F32) + vec[16:17, own_cols]
     for p in peers:
         arrived(R.outR.at[p], R.rOut.at[p])
@@ -1275,7 +1275,7 @@
         for m in range(4):
             gbank[:, m * 256 : (m + 1) * 256] = R.FR[m]
 
-    @when(is_row)
+    @when(used & is_row)
     def _():
         for m in range(4):
             q, h = m // 2, m % 2
@@ -1283,6 +1283,10 @@
                 lo = (2 * h + n) * 256
                 gbank[q * 256 : (q + 1) * 256, lo : lo + 256] = R.FR[m, n * 256 : (n + 1) * 256, :]
 
+    stores = [pltpu.make_async_copy(a, b, R.sRes.at[i]) for i, (a, b) in enumerate(zip(results, targets))]
+    for store in stores:
+        store.start()
+
     for m in range(4):
         tp, tc, own = message(m)
 
@@ -1317,7 +1321,7 @@
     drain_spread(2, 0)
     sent(R.kq.at[c], R.sK.at[15])
     sent(R.gaq.at[c], R.sGa.at[15])
-    for f in range(3):
+    for f in range(2):
         for p in range(4):
             sent(R.msgs.at[0], R.sFc.at[f, p])
     for p in range(4):
@@ -1327,12 +1331,14 @@
     sent(R.fromc, R.sAll.at[10])
     for i in range(3):
         sent(R.mS.at[0:128, :], R.sMp.at[i])
-        sent(mine, R.sMix.at[i])
+        sent(R.mix.at[0:256, 0:256], R.sMix.at[0, i])
+        sent(R.mix.at[0:256, 0:256], R.sMix.at[1, i])
         sent(R.msgs.at[0], R.sOut.at[i])
         sent(R.rsR.at[0], R.sR.at[1, i])
         for phase in range(3):
             sent(R.gmS.at[0], R.sG.at[phase, i])
         sent(R.pixS.at[0], R.sP.at[i])
+        sent(R.gt.at[0], R.sGt.at[i])
         sent(R.fp.at[0], R.sFo.at[1 + i])
         sent(R.fp.at[0], R.sFo.at[4 + i])
         for phase in range(3):
@@ -1349,17 +1355,22 @@
         @when((top if b == 0 else always) & no(own))
         def _():
             sent(R.msgs.at[0], R.sFin.at[b])
+    for store in stores:
+        store.wait()
 
 
 VMEM = pl.BlockSpec(memory_space=pltpu.VMEM)
 SMEM = pl.BlockSpec(memory_space=pltpu.SMEM)
 ARG_SHAPES = (
-    [((2, 192, 256), BF), ((1, 2), F32), ((1, 4), jnp.int32), ((512, 1024), BF), ((512, 1024), BF), ((48, 4, 1024), BF)]
+    [((2, 192, 256), BF), ((512, 1024), BF), ((512, 1024), BF), ((48, 4, 1024), BF)]
     + [((48, 1024), BF)] * 2
     + [((1024,), BF)]
     + [((n, 1024), BF) for n in (3, 2, 2, 2, 3)]
-    + [((4096,), BF), ((1024,), BF)]
+    + [((4096,), BF), ((1024,), BF), ((1, 2), F32), ((1, 4), jnp.int32)]
 )
+
+
+ANY = pl.BlockSpec(memory_space=pl.ANY)
 
 
 def block_call(*args):
@@ -1375,9 +1386,10 @@
     return pl.pallas_call(
         block_kernel,
         out_shape=outs,
-        in_specs=[VMEM, SMEM, SMEM] + [VMEM] * (len(args) - 3),
-        out_specs=[VMEM] * len(outs),
-        scratch_shapes=[pltpu.VMEM(*v) for v in SCRATCH.values()]
+        in_specs=[ANY] * 14 + [SMEM] * 2,
+        out_specs=[ANY] * len(outs),
+        scratch_shapes=[pltpu.VMEM(a.shape, a.dtype) for a in (*args[:14], *outs)]
+        + [pltpu.VMEM(*v) for v in SCRATCH.values()]
         + [pltpu.SemaphoreType.DMA(v) for v in SEMS.values()],
         compiler_params=pltpu.CompilerParams(
             collective_id=1, has_side_effects=True, vmem_limit_bytes=63 * 2**20
@@ -1451,8 +1463,6 @@
 ):
     parts = block_call(
         jnp.transpose(patches, (0, 2, 1)),
-        lead_times.T,
-        short_lengths,
         cotangent.reshape(ROWS, D),
         bank[0],
         patch_w,
@@ -1466,6 +1476,8 @@
         attn_bias,
         fc1_bias,
         fc2_bias,
+        lead_times.T,
+        short_lengths,
     )
     o = finish_call(*parts)
     return (

time: 198 us -> 189 us (0.955)
  Pallas kernels: 197 us -> 188 us
    pallas_call x1, Pallas kernels: 194 us -> 184 us  [block_call(): pl.pallas_call(block_kernel, out_shape=outs, in_specs=[ANY] * 14 + [SMEM]...]
where the time goes in v4:
time: 189 us
  Pallas kernels  188 us (99%)
    pallas_call x1, Pallas kernels, block_call(): pl.pallas_call(block_kernel, out_shape=outs, in_specs=[ANY] * 14 + [SMEM]...  184 us

profile of v4, /device:TPU:25, one launch (start us, length us, event | category | flops | bytes accessed | tf_op | source)
XLA Modules:
  0.0 188.7 jit_solution(9885772576458721249)
XLA Ops:
  0.7 184.4 %shard_map.263 = (bf16[512,256]{1,0:T(8,128)(2,1)}, f32[2,48,256]{2,1,0:T(8,128)}, bf16[512,1024]{1,0:T(8,128)(2,1)}, bf16[256,1024]{1,0:T(8,128)(2,1)}, f32[16,1024]{1,0:T(8,128)}, /*index=5*/f32[16,1024]{1,0:T(8,128)}) custom-call(bf16[2,192,256]{2,1,0:T(8,128)(2,1)} %bitcast.9, bf16[512,1024]{1,0:T(8,128)(2,1)} %bitcast.7, bf16[512,1024]{1,0:T(8,128)(2,1)} %bitcast.8, ...), custom_call_target="tpu_custom_call" | custom-call | tf_op jit(solution)/shard_map/pallas_call | solution.py:1386
  185.0 3.5 %shard_map.264 = (bf16[512,256]{1,0:T(8,128)(2,1)}, f32[2,48,256]{2,1,0:T(8,128)}, f32[512,1024]{1,0:T(8,128)}, f32[48,4,1024]{2,1,0:T(4,128)}, f32[48,1024]{1,0...) custom-call(bf16[512,256]{1,0:T(8,128)(2,1)} %get-tuple-element.34.r, ...), custom_call_target="tpu_custom_call" | custom-call | tf_op jit(solution)/shard_map/pallas_call | solution.py:1436

commit v5 on v4

--- a/solution.py
+++ b/solution.py
@@ -178,12 +178,19 @@
     sIn=(14,),
     sRes=(6,),
     rW=(4, 4, 2),
-    rF=(2, 4, 2),
+    rF=(4, 2),
+    rH=(4, 2, 2),
+    rA=(2,),
+    sA=(4, 2),
+    sAo=(2, 2),
+    sAf=(2,),
+    sAx=(3, 2),
+    sAc=(4, 2),
     sMsg=(4,),
     sOwn=(4, 2),
     sFwd=(4, 4, 2),
-    sFx=(2, 3),
-    sFc=(2, 4),
+    sFx=(3,),
+    sFc=(4,),
     sGt=(3,),
     rGt=(4,),
     rQ=(2,),
@@ -298,7 +305,25 @@
             def _():
                 remote(R.msgs.at[m], R.W.at[z, s, tc], R.sMsg.at[m], R.rW.at[z, s, tc], dev(tp, z, tc)).start()
 
-    scatter(used)
+    out_owner = (s == 0) & (z == 3)
+
+    def half_of(p, h):
+        return R.WF.at[0, p, c, h * 256 : (h + 1) * 256]
+
+    def out_half(h):
+        return R.W.at[3, 0, c, h * 256 : (h + 1) * 256]
+
+    @when(out_owner)
+    def _():
+        for h in range(2):
+            for m in range(4):
+                block = R.msgs.at[m, h * 256 : (h + 1) * 256]
+                if m == 0:
+                    pltpu.make_async_copy(block, out_half(h), R.rA.at[h]).start()
+                else:
+                    remote(block, out_half(h), R.sA.at[m, h], R.rA.at[h], dev(m, z, c)).start()
+
+    scatter(used & no(out_owner))
 
     for i in range(3, 14):
         loads[i].wait()
@@ -385,23 +410,19 @@
         return zz == 3 if b == 0 else zz >= 0
 
     def full_of(zz, b):
-        if b == 0:
-            return zz == 3, 0
-        if b == 1:
-            return zz == 3, 1
-        return None, None
+        return (zz == 3) if b == 1 else None
 
     def spread(zz, b):
         block = R.W.at[zz, b, c]
-        whole, f = full_of(zz, b)
+        whole = full_of(zz, b)
 
         def to_sibling():
             remote(block, block, R.sFwd.at[zz, b, 0], R.rW.at[zz, b, c], sib).start()
 
         def to_layer():
-            pltpu.make_async_copy(block, R.WF.at[f, s, c], R.rF.at[f, s, c]).start()
+            pltpu.make_async_copy(block, R.WF.at[1, s, c], R.rF.at[s, c]).start()
             for i, p in enumerate(peers):
-                remote(block, R.WF.at[f, s, c], R.sFx.at[f, i], R.rF.at[f, s, c], dev(p, z, c)).start()
+                remote(block, R.WF.at[1, s, c], R.sFx.at[i], R.rF.at[s, c], dev(p, z, c)).start()
 
         if whole is None:
             to_sibling()
@@ -411,6 +432,20 @@
             when(no(whole))(to_sibling)
             when(whole)(to_layer)
 
+    def out_layer(h):
+        pltpu.make_async_copy(out_half(h), half_of(s, h), R.rH.at[s, c, h]).start()
+        for i, p in enumerate(peers):
+            remote(out_half(h), half_of(s, h), R.sAx.at[i, h], R.rH.at[s, c, h], dev(p, z, c)).start()
+
+    def out_along(cond):
+        @when(cond)
+        def _():
+            for h in range(2):
+                arrived(out_half(h), R.rA.at[h])
+                remote(out_half(h), out_half(h), R.sAo.at[1, h], R.rA.at[h], dev(s, z ^ 2, c)).start()
+            for h in range(2):
+                remote(out_half(h), out_half(h), R.sAo.at[0, h], R.rA.at[h], dev(s, z ^ 1, c)).start()
+
     def along(cond, b, way):
         block = R.W.at[z, b, c]
         zz = z ^ 1 if way == 0 else here.far
@@ -461,7 +496,7 @@
         for i, p in enumerate(peers):
             remote(piece_of(s, c), piece_of(s, c), R.sMp.at[i], R.rM.at[s, c], dev(p, z, c)).start()
 
-    step(top & (s == 0), 0, False)
+    out_along(top & (s == 0))
     step(no(top) & (s == 1), 1)
     first_feed = z != 2
     for b in (2, 3):
@@ -498,7 +533,7 @@
         R.acc[g * GROUP : (g + 1) * GROUP, 512:1024] = jnp.cos(angle) + base[:, 512:1024]
 
     positions(0)
-    step(top & (s != 0), 0, False)
+    out_along(top & (s != 0))
     step(no(top) & (s != 1), 1)
     step(top, 1, False)
 
@@ -526,7 +561,8 @@
 
     @when(top)
     def _():
-        spread(3, 0)
+        for h in range(2):
+            out_layer(h)
 
     for b in (2, 3):
         mine_first = (s == b) & first_feed
@@ -535,7 +571,6 @@
         aside(no(mine_first), b)
     along(outer, 2, 0)
     along(outer, 3, 0)
-    along(inner & no((s == 2) & first_feed), 2, 0)
     scatter(late)
 
     arrived(R.kq.at[1 - c], R.rK.at[1 - c])
@@ -561,7 +596,16 @@
 
     loop(3, score_part)
 
-    foreign(3, 0)
+    @when(no(top))
+    def _():
+        for h in range(2):
+            arrived(out_half(h), R.rA.at[h])
+
+            @when(z == 1)
+            def _():
+                remote(out_half(h), out_half(h), R.sAf.at[h], R.rA.at[h], dev(s, z ^ 1, c)).start()
+
+            out_layer(h)
 
     for i, p in enumerate([s] + peers):
         if i > 0:
@@ -597,17 +641,28 @@
 
     loop(HEADS, embed_head)
 
-    def pass_on(f):
+    def pass_out():
+        for h in range(2):
+            for p in [s] + peers:
+                arrived(half_of(p, h), R.rH.at[p, c, h])
+                remote(half_of(p, h), half_of(p, h), R.sAc.at[p, h], R.rH.at[p, c, h], sib).start()
+
+    def wait_out():
+        for h in range(2):
+            for p in range(4):
+                arrived(R.WF.at[0, p, 1 - c, h * 256 : (h + 1) * 256], R.rH.at[p, 1 - c, h])
+
+    def pass_on():
         for p in [s] + peers:
-            block = R.WF.at[f, p, c]
-            arrived(block, R.rF.at[f, p, c])
-            remote(block, block, R.sFc.at[f, p], R.rF.at[f, p, c], sib).start()
-
-    def wait_whole(f):
+            block = R.WF.at[1, p, c]
+            arrived(block, R.rF.at[p, c])
+            remote(block, block, R.sFc.at[p], R.rF.at[p, c], sib).start()
+
+    def wait_whole():
         for p in range(4):
-            arrived(R.WF.at[f, p, 1 - c], R.rF.at[f, p, 1 - c])
-
-    pass_on(0)
+            arrived(R.WF.at[1, p, 1 - c], R.rF.at[p, 1 - c])
+
+    pass_out()
 
     def turn_tile(i):
         rows = at(i * 256, 256, 256)
@@ -623,15 +678,16 @@
         spread(3, 1)
 
     foreign(z ^ 3, 2, inner)
+    along(inner & no((s == 2) & first_feed), 2, 0)
     along(inner & no((s == 3) & first_feed), 3, 0)
-    foreign(3, 1, outer)
-    wait_whole(0)
+    wait_out()
 
     def stream0_part(n):
         cols = at(n * 256, 256, 256)
         R.st0[:, cols] = (mm(R.hrow[...], R.WF[0, n].reshape(1024, 256)) + R.acc[:, cols]).astype(BF)
 
     loop(4, stream0_part)
+    foreign(3, 1, outer)
 
     def norm_into(src, dst, which, g):
         def part(i):
@@ -698,9 +754,8 @@
     step(z == 2, 0)
     for b in (2, 3):
         foreign(z ^ 2, b, inner)
-        foreign(z ^ 1, b)
-    pass_on(1)
-    wait_whole(1)
+    pass_on()
+    wait_whole()
     def stream1_part(g, n):
         rows = slice(g * 256, (g + 1) * 256)
         cols = at(n * 256, 256, 256)
@@ -829,6 +884,7 @@
             wait_half(2 + par, b)
 
     for b in (2, 3):
+        foreign(z ^ 1, b, inner)
         foreign(z ^ 2, b, outer)
     wait_feed(early)
     feed(early)
@@ -845,6 +901,7 @@
     transposed(R.nrm2)
     feed_gradients(early)
     for b in (2, 3):
+        foreign(z ^ 1, b, outer)
         foreign(z ^ 3, b, outer)
     later = 1 - early
     gradient_sends(outer, (2, 0))
@@ -882,14 +939,14 @@
                 sent(R.msgs.at[0], R.sOwn.at[b, i])
 
     def drain_spread(zz, b):
-        whole, f = full_of(zz, b)
+        whole = full_of(zz, b)
 
         def side():
             sent(R.msgs.at[0], R.sFwd.at[zz, b, 0])
 
         def layer():
             for i in range(3):
-                sent(R.msgs.at[0], R.sFx.at[f, i])
+                sent(R.msgs.at[0], R.sFx.at[i])
 
         (layer if whole else side)()
 
@@ -978,8 +1035,6 @@
         block = R.hrow.at[:, at(p * 256, 256, 256)]
         remote(block, R.outR.at[s], R.sOut.at[i], R.rOut.at[s], dev(p, z, c)).start()
 
-    send_out(0)
-    send_out(1)
 
     swapped(0, R.gm)
 
@@ -1014,16 +1069,27 @@
         R.rsS[rows, :] = total.astype(BF)
 
     reduce_rows(1, attend_norm)
-    send_out(2)
     for b in (2, 3):
         second_send(3, b)
 
     transposed(R.nrm)
     drain_own(always, 1)
-    drain_own(top, 0)
     for zz in range(4):
         drain_spread(zz, 1)
-    drain_spread(3, 0)
+    piece = R.msgs.at[0, 0:256]
+    for h in range(2):
+        for i in range(3):
+            sent(piece, R.sAx.at[i, h])
+
+        @when(z == 1)
+        def _():
+            sent(piece, R.sAf.at[h])
+
+        @when(top)
+        def _():
+            sent(piece, R.sAo.at[0, h])
+            sent(piece, R.sAo.at[1, h])
+
 
     def attend_gradient(i):
         column_gradient(i, 1, R.tr, R.gq[i])
@@ -1195,6 +1261,9 @@
     for i, p in enumerate(peers):
         block = R.fin.at[part_of(s), :]
         remote(block, block, R.sAll.at[7 + i], R.rAll.at[9 + s], dev(p, z, c)).start()
+    send_out(0)
+    send_out(1)
+    send_out(2)
 
     @when(first_owner)
     def _():
@@ -1290,9 +1359,16 @@
     for m in range(4):
         tp, tc, own = message(m)
 
-        @when((used | late) & no(own))
+        @when((used | late) & no(own) & no(out_owner))
         def _():
             sent(R.msgs.at[m], R.sMsg.at[m])
+
+        if m > 0:
+
+            @when(out_owner)
+            def _():
+                sent(piece, R.sA.at[m, 0])
+                sent(piece, R.sA.at[m, 1])
 
         @when(value_owner & no((2 * c + m // 2 == s) & (c == m % 2)))
         def _():
@@ -1321,9 +1397,10 @@
     drain_spread(2, 0)
     sent(R.kq.at[c], R.sK.at[15])
     sent(R.gaq.at[c], R.sGa.at[15])
-    for f in range(2):
-        for p in range(4):
-            sent(R.msgs.at[0], R.sFc.at[f, p])
+    for p in range(4):
+        sent(R.msgs.at[0], R.sFc.at[p])
+        sent(piece, R.sAc.at[p, 0])
+        sent(piece, R.sAc.at[p, 1])
     for p in range(4):
         sent(R.mS.at[0:128, :], R.sMc.at[p])
     sent(R.fc.at[0], R.sFo.at[0])
@@ -1398,23 +1475,46 @@
 
 
 def finish_kernel(*refs):
-    sources, rest = refs[:6], refs[6:]
-    outs, scratch = rest[:14], rest[14:]
-    out, gpix, gbank, gtab, sums, rows = scratch[:6]
-    sems = scratch[6]
-    copies = [pltpu.make_async_copy(a, b, sems.at[i]) for i, (a, b) in enumerate(zip(sources, scratch[:6]))]
-    for copy in copies:
-        copy.start()
-    for copy in copies:
-        copy.wait()
-    o_out, o_pix, o_bank, o_patch, o_patch_b, o_var, o_query, o_agg, o_lead, o_gain, o_bias, o_attn, o_fc1, o_fc2 = outs
-    o_out[...] = out[...]
-    o_pix[...] = gpix[...]
-    o_bank[...] = gbank[...].astype(F32)
+    sources, targets, rest = refs[:6], refs[6:20], refs[20:]
+    held, made, ins, outs = rest[:6], rest[6:20], rest[20], rest[21]
+    out, gpix, gbank, gtab, sums, rows = held
+    o_out, o_pix, o_bank, o_patch, o_patch_b, o_var, o_query, o_agg, o_lead, o_gain, o_bias, o_attn, o_fc1, o_fc2 = made
+
+    def load(i):
+        return pltpu.make_async_copy(sources[i], held[i], ins.at[i])
+
+    def part(h):
+        rows_h = pl.ds(h * 128, 128)
+        return pltpu.make_async_copy(sources[2].at[rows_h], gbank.at[rows_h], ins.at[6 + h])
+
+    def store(i):
+        return pltpu.make_async_copy(made[i], targets[i], outs.at[i])
+
+    def store_part(h):
+        rows_h = pl.ds(h * 128, 128)
+        return pltpu.make_async_copy(o_bank.at[rows_h], targets[2].at[rows_h], outs.at[14 + h])
+
+    for h in range(4):
+        part(h).start()
+    for i in (3, 4, 5, 0, 1):
+        load(i).start()
+    direct = [pltpu.make_async_copy(held[i], targets[i], outs.at[i]) for i in range(2)]
+    for h in range(4):
+        part(h).wait()
+        o_bank[h * 128 : (h + 1) * 128, :] = gbank[h * 128 : (h + 1) * 128, :].astype(F32)
+        store_part(h).start()
+    load(3).wait()
     for p in range(PIX):
         o_patch[:, p, :] = gtab[p * VARS : (p + 1) * VARS, :].astype(F32)
     o_patch_b[...] = gtab[192:240, :].astype(F32)
     o_var[...] = gtab[192:240, :].astype(F32)
+    for i in (3, 4, 5):
+        store(i).start()
+    for i in range(2):
+        load(i).wait()
+        direct[i].start()
+    load(4).wait()
+    load(5).wait()
     o_query[...] = rows[8, :]
     o_agg[0:1, :] = rows[0:1, :]
     o_agg[1:3, :] = sums[0:2, :]
@@ -1426,6 +1526,14 @@
     for i in range(4):
         o_fc1[i * 1024 : (i + 1) * 1024] = sums[10 + i, :]
     o_fc2[...] = sums[14, :]
+    for i in range(6, 14):
+        store(i).start()
+    for copy in direct:
+        copy.wait()
+    for h in range(4):
+        store_part(h).wait()
+    for i in range(3, 14):
+        store(i).wait()
 
 
 def finish_call(*args):
@@ -1436,9 +1544,10 @@
     return pl.pallas_call(
         finish_kernel,
         out_shape=outs,
-        in_specs=[pl.BlockSpec(memory_space=pl.ANY)] * len(args),
-        out_specs=[VMEM] * len(outs),
-        scratch_shapes=[pltpu.VMEM(a.shape, a.dtype) for a in args] + [pltpu.SemaphoreType.DMA((len(args),))],
+        in_specs=[ANY] * len(args),
+        out_specs=[ANY] * len(outs),
+        scratch_shapes=[pltpu.VMEM(a.shape, a.dtype) for a in (*args, *outs)]
+        + [pltpu.SemaphoreType.DMA((10,)), pltpu.SemaphoreType.DMA((18,))],
         compiler_params=pltpu.CompilerParams(vmem_limit_bytes=63 * 2**20),
     )(*args)
 

time: 189 us -> 186 us (0.984)
  Pallas kernels: 188 us -> 185 us
    pallas_call x1, Pallas kernels: 184 us -> 182 us  [block_call(): pl.pallas_call(block_kernel, out_shape=outs, in_specs=[ANY] * 14 + [SMEM]...]
where the time goes in v5:
time: 186 us
  Pallas kernels  185 us (99%)
    pallas_call x1, Pallas kernels, block_call(): pl.pallas_call(block_kernel, out_shape=outs, in_specs=[ANY] * 14 + [SMEM]...  182 us

profile of v5, /device:TPU:25, one launch (start us, length us, event | category | flops | bytes accessed | tf_op | source)
XLA Modules:
  0.0 186.3 jit_solution(1836505850266948016)
XLA Ops:
  0.7 182.4 %shard_map.263 = (bf16[512,256]{1,0:T(8,128)(2,1)}, f32[2,48,256]{2,1,0:T(8,128)}, bf16[512,1024]{1,0:T(8,128)(2,1)}, bf16[256,1024]{1,0:T(8,128)(2,1)}, f32[16,1024]{1,0:T(8,128)}, /*index=5*/f32[16,1024]{1,0:T(8,128)}) custom-call(bf16[2,192,256]{2,1,0:T(8,128)(2,1)} %bitcast.9, bf16[512,1024]{1,0:T(8,128)(2,1)} %bitcast.7, bf16[512,1024]{1,0:T(8,128)(2,1)} %bitcast.8, ...), custom_call_target="tpu_custom_call" | custom-call | tf_op jit(solution)/shard_map/pallas_call | solution.py:1463
  183.1 3.1 %shard_map.264 = (bf16[512,256]{1,0:T(8,128)(2,1)}, f32[2,48,256]{2,1,0:T(8,128)}, f32[512,1024]{1,0:T(8,128)}, f32[48,4,1024]{2,1,0:T(4,128)}, f32[48,1024]{1,0...) custom-call(bf16[512,256]{1,0:T(8,128)(2,1)} %get-tuple-element.34.r, ...), custom_call_target="tpu_custom_call" | custom-call | tf_op jit(solution)/shard_map/pallas_call | solution.py:1544

commit v6 on v5

--- a/solution.py
+++ b/solution.py
@@ -1246,6 +1246,8 @@
         remote(R.qx.at[0], R.qx.at[1], R.sGq.at[15], R.rGq.at[0], sib).start()
         masked = jnp.where(diag, R.qb[...].astype(F32), 0.0).astype(BF)
         gbank[...] = mm_tn(own, masked).astype(BF)
+
+    def query_grad():
         arrived(R.qx.at[1], R.rGq.at[0])
         row = (R.qx[0] + R.qx[1]).astype(BF)
         R.gqv[...] = jnp.concatenate([row, row], axis=0)
@@ -1265,16 +1267,7 @@
     send_out(1)
     send_out(2)
 
-    @when(first_owner)
-    def _():
-        arrived(R.gqv, R.rGq.at[1])
-        R.gaq[c] = mm_nt(R.gqv[...], bank[...])[0:8]
-        for i, (p, k) in enumerate(others):
-            remote(R.gaq.at[c], R.gaq.at[c], R.sGa.at[i], R.rGa.at[c], dev(p, k, c)).start()
-        aq = jnp.where(c == 0, vec[17:18, 0:512], vec[17:18, 512:1024])
-        aq = jnp.where(iota((16, 512), 0) == 0, aq, 0.0).astype(BF)
-        gbank[...] = mm_tn(aq, R.gqv[...]).astype(BF)
-
+    when(key_owner)(query_grad)
 
     for p in peers:
         arrived(R.fin.at[part_of(p), :], R.rAll.at[9 + p])
@@ -1300,6 +1293,17 @@
     @when(value_owner)
     def _():
         gbank[...] = mm_tn(table[:, half_rows], R.fin[...]).astype(BF)
+
+    @when(first_owner)
+    def _():
+        arrived(R.gqv, R.rGq.at[1])
+        R.gaq[c] = mm_nt(R.gqv[...], bank[...])[0:8]
+        for i, (p, k) in enumerate(others):
+            remote(R.gaq.at[c], R.gaq.at[c], R.sGa.at[i], R.rGa.at[c], dev(p, k, c)).start()
+        aq = jnp.where(c == 0, vec[17:18, 0:512], vec[17:18, 512:1024])
+        aq = jnp.where(iota((16, 512), 0) == 0, aq, 0.0).astype(BF)
+        gbank[...] = mm_tn(aq, R.gqv[...]).astype(BF)
+
 
     last_send(always, 1)
     last_send(top, 0)

time: 186 us -> 186 us (level)
  no operation moved by 1% of the time
where the time goes in v6:
time: 186 us
  Pallas kernels  185 us (99%)
    pallas_call x1, Pallas kernels, block_call(): pl.pallas_call(block_kernel, out_shape=outs, in_specs=[ANY] * 14 + [SMEM]...  182 us

profile of v6, /device:TPU:25, one launch (start us, length us, event | category | flops | bytes accessed | tf_op | source)
XLA Modules:
  0.0 186.0 jit_solution(10735794003344697320)
XLA Ops:
  0.7 182.1 %shard_map.263 = (bf16[512,256]{1,0:T(8,128)(2,1)}, f32[2,48,256]{2,1,0:T(8,128)}, bf16[512,1024]{1,0:T(8,128)(2,1)}, bf16[256,1024]{1,0:T(8,128)(2,1)}, f32[16,1024]{1,0:T(8,128)}, /*index=5*/f32[16,1024]{1,0:T(8,128)}) custom-call(bf16[2,192,256]{2,1,0:T(8,128)(2,1)} %bitcast.9, bf16[512,1024]{1,0:T(8,128)(2,1)} %bitcast.7, bf16[512,1024]{1,0:T(8,128)(2,1)} %bitcast.8, ...), custom_call_target="tpu_custom_call" | custom-call | tf_op jit(solution)/shard_map/pallas_call | solution.py:1467
  182.7 3.1 %shard_map.264 = (bf16[512,256]{1,0:T(8,128)(2,1)}, f32[2,48,256]{2,1,0:T(8,128)}, f32[512,1024]{1,0:T(8,128)}, f32[48,4,1024]{2,1,0:T(4,128)}, f32[48,1024]{1,0...) custom-call(bf16[512,256]{1,0:T(8,128)(2,1)} %get-tuple-element.34.r, ...), custom_call_target="tpu_custom_call" | custom-call | tf_op jit(solution)/shard_map/pallas_call | solution.py:1548
